TPU v7x, 1024 devices: a whole 4x4x32 slice. The times are simulated.
1024 devices in a mesh: rep: 128 (over y_lo, z, core), fsdp: 8 (over x, y_hi).
Axes of the slice: x: 4, y: 4 (y_hi: 2, y_lo: 2; y = y_hi * 2 + y_lo), z: 32, core: 2. Of those that a mesh axis runs over, the one named last changes fastest.
Arguments:
- tokens: bfloat16 [131072, 4608], P('rep', 'fsdp'), may hold values from -3300 to 3300
- norm_gain: bfloat16 [128, 4608], P('rep', 'fsdp'), may hold values from 0.5 to 1.5
- key_weight: bfloat16 [128, 1024, 4608], P('rep', None, 'fsdp'), may hold values from -0.3125 to 0.3125
- key_cotangent: bfloat16 [131072, 1024], P(('rep', 'fsdp')), may hold values from -24 to 24
- global_fragment: float32 [1024, 4608], P('rep', 'fsdp'), may hold values from -6 to 6
- outer_momentum: float32 [1024, 4608], P('rep', 'fsdp'), may hold values from -3 to 3
Outputs:
- keys: bfloat16 [131072, 1024], P(('rep', 'fsdp'))
- gain_grad: float32 [128, 4608], P('rep', 'fsdp')
- new_global: float32 [1024, 4608], P('rep', 'fsdp')
- new_momentum: float32 [1024, 4608], P('rep', 'fsdp')
All inputs are finite; a program needn't handle non-finite values.
Results may differ from a plain program's by a relative error of at most 0.015.
Values may be sent and summed in bfloat16 or wider, within the bound.
No kernel may reach another device: no remote copies, remote signals or barrier semaphores. Data moves between devices by JAX's collectives and lax.ppermute only.
A program may use at most 32 MiB of HBM per device.

v0:
```python
import jax
import jax.numpy as jnp
from jax import lax
from jax.sharding import PartitionSpec as P

D = 4608


rms_eps = 1e-06
inner_rate = 0.3
outer_rate = 0.7
outer_beta = 0.9


def per_device(tokens, norm_gain, key_weight, key_cotangent, global_fragment, outer_momentum):
    tok_float = tokens.astype(jnp.float32)
    square_sum = lax.psum(jnp.sum(tok_float * tok_float, axis=1), "fsdp")
    inv_rms = lax.rsqrt(square_sum / D + rms_eps)
    normed = tok_float * inv_rms[:, None]
    hidden = (normed * norm_gain[0].astype(jnp.float32)).astype(jnp.bfloat16)
    weight = key_weight[0]
    partial_keys = lax.dot_general(
        hidden, weight, (((1,), (1,)), ((), ())), preferred_element_type=jnp.float32
    )
    key_out = lax.psum_scatter(
        partial_keys.astype(jnp.bfloat16), "fsdp", scatter_dimension=0, tiled=True
    )
    cot_all = lax.all_gather(key_cotangent, "fsdp", axis=0, tiled=True)
    hidden_grad = jnp.dot(cot_all, weight, preferred_element_type=jnp.float32)
    gain_grad = jnp.sum(hidden_grad * normed, axis=0)
    weight_grad = lax.dot_general(
        cot_all, hidden, (((0,), (0,)), ((), ())), preferred_element_type=jnp.float32
    )
    inner_new = weight.astype(jnp.float32) - inner_rate * weight_grad
    summed = lax.psum_scatter(inner_new, "rep", scatter_dimension=0, tiled=True)
    avg_grad = global_fragment - summed / lax.axis_size("rep")
    new_momentum = outer_beta * outer_momentum + avg_grad
    new_global = global_fragment - outer_rate * (avg_grad + outer_beta * new_momentum)
    return (key_out, gain_grad[None], new_global, new_momentum)


def solution(mesh):
    return jax.shard_map(
        per_device,
        mesh=mesh,
        in_specs=(
            P("rep", "fsdp"),
            P("rep", "fsdp"),
            P("rep", None, "fsdp"),
            P(("rep", "fsdp"), None),
            P("rep", "fsdp"),
            P("rep", "fsdp"),
        ),
        out_specs=(P(("rep", "fsdp"), None), P("rep", "fsdp"), P("rep", "fsdp"), P("rep", "fsdp")),
        check_vma=False,
    )
```

profile of v0, /device:TPU:1, one launch (start us, length us, event | category | flops | bytes accessed | tf_op | source)
XLA Modules:
  0.0 1039.2 jit_solution(7299902552473549026)
XLA Ops:
  7.2 0.0 all-gather.2.cloned.1.call-start
  7.2 0.7 all-gather.2.cloned.1.call-update
  7.9 0.0 all-reduce.3.cloned.1.call-start
  7.9 1.5 fusion.4
  9.5 21.4 %psum.7 = f32[1024]{0:T(1024)S(1)} all-reduce(f32[1024]{0:T(1024)S(1)} %fusion.4), channel_id=1, replica_groups=mesh['rep'=128,'fsdp'=8] {'fsdp'}, use_global_device_ids=true, to_apply=%region_1.0 | all-reduce | flops 1024 | bytes 8192 | tf_op jit(solution)/shard_map/psum | solution.py:17
  30.9 0.7 convert_reduce_fusion
  31.6 78.7 %all-gather.2.cloned.1.call-done = bf16[1024,1024]{1,0:T(8,128)(2,1)} async-done(((bf16[128,1024]{1,0:T(8,128)(2,1)}), bf16[1024,1024]{1,0:T(8,128)(2,1)}) %all-gather.2.cloned.1.call-update) | async-done | bytes 2097168 | tf_op jit(solution)/shard_map/all_gather | solution.py:28
  110.3 5.1 bitcast_subtract_fusion
  115.4 0.0 copy-start
  115.4 0.0 copy-start.4
  115.4 0.0 all-reduce.3.cloned.1.call-update
  115.5 0.0 reduce-scatter.3.cloned.1.call-start
  115.5 1.2 copy-done
  116.7 0.4 copy-done.4
  117.1 3.3 convolution_convert_fusion
  120.4 0.0 copy-start.3
  120.4 0.0 reduce-scatter.3.cloned.1.call-update
  120.4 1.4 dynamic-slice
  122.5 0.0 copy-done.3
  122.5 0.0 copy-start.1
  122.5 0.0 copy-start.2
  122.5 2.8 fusion.3
  125.4 0.6 broadcast_in_dim.2
  125.9 807.5 %all-reduce.3.cloned.1.call-done = f32[1024,576]{0,1:T(8,128)} async-done(((f32[1024,576]{0,1:T(8,128)}), f32[1024,576]{0,1:T(8,128)}) %all-reduce.3.cloned.1.call-update) | async-done | bytes 2359312
  933.4 1.1 constant_dynamic-slice_fusion
  934.5 0.1 copy.22
  934.6 0.0 copy-done.1
  934.6 0.0 copy-done.2
  934.6 0.6 multiply_subtract_fusion
  935.3 97.4 %reduce-scatter.3.cloned.1.call-done = bf16[128,1024]{1,0:T(8,128)(2,1)} async-done(((bf16[1024,1024]{1,0:T(8,128)(2,1)}), bf16[128,1024]{1,0:T(8,128)(2,1)}) %reduce-scatter.3.cloned.1.call-update) | async-done | bytes 262160 | tf_op jit(solution)/shard_map/reduce_scatter | solution.py:25
  (1 shorter events, 0.0 us)
Async XLA Ops:
  7.2 103.2 %all-gather.2.cloned.1.call-start = ((), (), s32[]{:S(2)}) async-start(), calls=%async_computation.2 | async-start | bytes 2359296 | tf_op jit(solution)/shard_map/all_gather | solution.py:28
  7.9 925.5 %all-reduce.3.cloned.1.call-start = ((), (), s32[]{:S(2)}) async-start(), calls=%async_computation.3 | async-start | bytes 4718592
  115.4 1.3 copy-start
  115.4 1.6 copy-start.4
  115.5 917.2 %reduce-scatter.3.cloned.1.call-start = ((), (), s32[]{:S(2)}) async-start(), calls=%async_computation.1 | async-start | bytes 2359296 | tf_op jit(solution)/shard_map/reduce_scatter | solution.py:25
  120.4 2.1 copy-start.3
  122.5 812.1 %copy-start.1 = (f32[8,576]{1,0:T(8,128)S(1)}, f32[8,576]{1,0:T(8,128)}, u32[]{:S(2)}) copy-start(f32[8,576]{1,0:T(8,128)} %param.10) | copy-start | bytes 55300
  122.5 812.1 %copy-start.2 = (f32[8,576]{1,0:T(8,128)S(1)}, f32[8,576]{1,0:T(8,128)}, u32[]{:S(2)}) copy-start(f32[8,576]{1,0:T(8,128)} %param.11) | copy-start | bytes 55300
Sparse Core Ops, SparseCore 0:
  12.4 97.9 all-gather.1
  115.6 817.7 all-reduce.2
  940.8 91.8 reduce-scatter.2
where the time goes:
time: 1040 us
  waiting for transfers between devices  984 us (95%)
  blocking collectives  21.4 us (2%)
  between operations  14.4 us (1%)
  matrix products  11.3 us (1%)
    unnamed x4, waiting for transfers between devices  808 us
    reduce_scatter x1, waiting for transfers between devices, per_device(): lax.psum_scatter(partial_keys.astype(jnp.bfloat16), 'fsdp', scatter_dimen...  97.4 us
    all_gather x1, waiting for transfers between devices, per_device(): cot_all = lax.all_gather(key_cotangent, 'fsdp', axis=0, tiled=True)  78.7 us
    psum x1, blocking collectives, per_device(): square_sum = lax.psum(jnp.sum(tok_float * tok_float, axis=1), 'fsdp')  21.4 us
  transfers between devices with their start and end apart: 3, of which 3 were waited for; matrix products, arithmetic and copies ran while one was open for 1% of the time, Pallas kernels for 0%

commit v1 on v0

v1 whole, which is shorter than its diff:
```python
import jax
import jax.numpy as jnp
from jax import lax
from jax.sharding import Mesh, PartitionSpec as P

D = 4608
N_REP = 128

rms_eps = 1e-06
inner_rate = 0.3
outer_rate = 0.7
outer_beta = 0.9

FSDP = ("x", "yh")
REP = ("yl", "zh", "zl", "core")
SWAP = [(0, 1), (1, 0)]
f32 = jnp.float32
bf16 = jnp.bfloat16


def spread(block):
    return jnp.broadcast_to(block[None], (8,) + block.shape)


def per_device(tokens, norm_gain, key_weight, key_cotangent, global_fragment, outer_momentum):
    tok_float = tokens.astype(f32)
    square_part = jnp.sum(tok_float * tok_float, axis=1).reshape(8, 128)
    square_all = lax.all_to_all(spread(square_part), FSDP, 0, 0)
    cot_all = lax.all_to_all(spread(key_cotangent), FSDP, 0, 0).reshape(1024, 1024)
    square_sum = jnp.sum(square_all, axis=0).reshape(1024)
    inv_rms = lax.rsqrt(square_sum / D + rms_eps)
    normed = tok_float * inv_rms[:, None]
    hidden = (normed * norm_gain[0].astype(f32)).astype(bf16)
    weight = key_weight[0]
    partial_keys = lax.dot_general(
        hidden, weight, (((1,), (1,)), ((), ())), preferred_element_type=f32
    ).astype(bf16)
    key_parts = lax.all_to_all(partial_keys.reshape(8, 128, 1024), FSDP, 0, 0)
    key_out = jnp.sum(key_parts.astype(f32), axis=0).astype(bf16)
    hidden_grad = jnp.dot(cot_all, weight, preferred_element_type=f32)
    gain_grad = jnp.sum(hidden_grad * normed, axis=0)
    weight_grad = lax.dot_general(
        cot_all, hidden, (((0,), (0,)), ((), ())), preferred_element_type=f32
    )
    inner_new = weight.astype(f32) - inner_rate * weight_grad
    core = lax.axis_index("core")
    yl = lax.axis_index("yl")
    total = inner_new.reshape(2, 8, 4, 2, 8, 576)
    mine = lax.dynamic_index_in_dim(total, core, 3, keepdims=False)
    other = lax.dynamic_index_in_dim(total, 1 - core, 3, keepdims=False)
    total = mine + lax.ppermute(other.astype(bf16), "core", SWAP).astype(f32)
    mine = lax.dynamic_index_in_dim(total, yl, 0, keepdims=False)
    other = lax.dynamic_index_in_dim(total, 1 - yl, 0, keepdims=False)
    total = mine + lax.ppermute(other.astype(bf16), "yl", SWAP).astype(f32)
    total = lax.all_to_all(total.astype(bf16).transpose(1, 0, 2, 3), "zl", 0, 0)
    total = jnp.sum(total.astype(f32), axis=0)
    total = lax.all_to_all(total.astype(bf16), "zh", 0, 0)
    summed = jnp.sum(total.astype(f32), axis=0)
    avg_grad = global_fragment - summed / N_REP
    new_momentum = outer_beta * outer_momentum + avg_grad
    new_global = global_fragment - outer_rate * (avg_grad + outer_beta * new_momentum)
    return (key_out, gain_grad[None], new_global, new_momentum)


def solution(mesh):
    fine = Mesh(mesh.devices.reshape(2, 8, 4, 2, 4, 2), REP + FSDP)
    return jax.shard_map(
        per_device,
        mesh=fine,
        in_specs=(
            P(REP, FSDP),
            P(REP, FSDP),
            P(REP, None, FSDP),
            P(REP + FSDP, None),
            P(REP, FSDP),
            P(REP, FSDP),
        ),
        out_specs=(P(REP + FSDP, None), P(REP, FSDP), P(REP, FSDP), P(REP, FSDP)),
        check_vma=False,
    )
```

time: 1040 us -> 179 us (0.17)
  waiting for transfers between devices: 984 us -> 80.3 us
  starting transfers between devices: 0.12 us -> 54.8 us
  between operations: 14.4 us -> 0.78 us
    unnamed x4 -> x0, waiting for transfers between devices: 808 us -> none
    reduce_scatter x1 -> x0, waiting for transfers between devices: 97.4 us -> none  [per_device(): lax.psum_scatter(partial_keys.astype(jnp.bfloat16), 'fsdp', scatter_dimen...]
    all_gather x1 -> x0, waiting for transfers between devices: 78.7 us -> none  [per_device(): cot_all = lax.all_gather(key_cotangent, 'fsdp', axis=0, tiled=True)]
    all_to_all x0 -> x4, waiting for transfers between devices: none -> 70.7 us  [the longest x1 27.8 us: per_device(): key_parts = lax.all_to_all(partial_keys.reshape(8, 128, 1024), FSDP, 0, 0)]
    all_to_all x0 -> x4, starting transfers between devices: none -> 39.7 us  [the longest x1 26 us: per_device(): total = lax.all_to_all(total.astype(bf16), 'zh', 0, 0)]
    psum x1 -> x0, blocking collectives: 21.4 us -> none  [per_device(): square_sum = lax.psum(jnp.sum(tok_float * tok_float, axis=1), 'fsdp')]
    ppermute x0 -> x2, starting transfers between devices: none -> 15.1 us  [the longest x1 10.9 us: per_device(): total = mine + lax.ppermute(other.astype(bf16), 'core', SWAP).astype(f32)]
    all_to_all x0 -> x1, blocking collectives: none -> 13.8 us  [per_device(): square_all = lax.all_to_all(spread(square_part), FSDP, 0, 0)]
  transfers between devices with their start and end apart: 3 -> 6, of which waited for: 3 -> 6; matrix products, arithmetic and copies ran while one was open for 1% -> 6% of each run, Pallas kernels for 0% -> 0%
where the time goes in v1:
time: 179 us; the launch traced here: 177 us
  waiting for transfers between devices  80.3 us (45%)
  starting transfers between devices  54.8 us (31%)
  blocking collectives  13.8 us (8%)
  matrix products  12.4 us (7%)
  local copies, waits for them, and re-layouts  8.55 us (5%)
  other arithmetic  6.41 us (4%)
    all_to_all x1, waiting for transfers between devices, per_device(): key_parts = lax.all_to_all(partial_keys.reshape(8, 128, 1024), FSDP, 0, 0)  27.8 us
    all_to_all x1, starting transfers between devices, per_device(): total = lax.all_to_all(total.astype(bf16), 'zh', 0, 0)  26 us
    all_to_all x1, waiting for transfers between devices, per_device(): lax.all_to_all(spread(key_cotangent), FSDP, 0, 0).reshape(1024, 1024)  20.4 us
    all_to_all x1, waiting for transfers between devices, per_device(): total = lax.all_to_all(total.astype(bf16), 'zh', 0, 0)  18.4 us
    all_to_all x1, blocking collectives, per_device(): square_all = lax.all_to_all(spread(square_part), FSDP, 0, 0)  13.8 us
    ppermute x1, starting transfers between devices, per_device(): total = mine + lax.ppermute(other.astype(bf16), 'core', SWAP).astype(f32)  10.9 us
    ppermute x1, waiting for transfers between devices, per_device(): total = mine + lax.ppermute(other.astype(bf16), 'yl', SWAP).astype(f32)  7.8 us
    all_to_all x1, starting transfers between devices, per_device(): total = lax.all_to_all(total.astype(bf16).transpose(1, 0, 2, 3), 'zl', 0, 0)  6.35 us
  transfers between devices with their start and end apart: 6, of which 6 were waited for; matrix products, arithmetic and copies ran while one was open for 6% of the time, Pallas kernels for 0%

profile of v1, /device:TPU:1, one launch (start us, length us, event | category | flops | bytes accessed | tf_op | source)
XLA Modules:
  0.0 177.0 jit_solution(7818298774061739564)
XLA Ops:
  0.6 1.5 fusion.4
  2.2 13.8 %all_to_all.25 = f32[8,8,128]{2,1,0:T(8,128)S(1)} all-to-all(f32[8,8,128]{2,1,0:T(8,128)S(1)} %broadcast_in_dim.9), channel_id=1, replica_groups=mesh['yl'=2,'zh'=8,'zl'=4,'core'=2,'x'=4,'yh'=2] {'x','yh'}, dimensions={0} | all-to-all | bytes 65536 | tf_op jit(solution)/shard_map/all_to_all | solution.py:28
  16.0 2.6 %broadcast_in_dim.20 = bf16[8,128,1024]{2,1,0:T(8,128)(2,1)} broadcast(bf16[128,1024]{1,0:T(8,128)(2,1)} %param.9), dimensions={1,2} | broadcast | bytes 2359296 | tf_op jit(solution)/shard_map/broadcast_in_dim | solution.py:22
  18.6 0.0 copy-start.6
  18.6 0.0 copy-start.2
  18.6 3.7 %all-to-all-start.2 = ((bf16[8,128,1024]{2,1,0:T(8,128)(2,1)}), bf16[8,128,1024]{2,1,0:T(8,128)(2,1)S(1)}, u32[]{:S(2)}, u32[]{:S(2)}) async-start(bf16[8,128,1024]{2,1,0:T(8,128)(2,1)} %broadcast_in_dim.20), calls=%async_computation.2 | async-start | bytes 4194304 | tf_op jit(solution)/shard_map/all_to_all | solution.py:29
  22.3 0.0 copy-done.6
  22.4 20.4 %all-to-all-done.2 = bf16[8,128,1024]{2,1,0:T(8,128)(2,1)S(1)} async-done(((bf16[8,128,1024]{2,1,0:T(8,128)(2,1)}), bf16[8,128,1024]{2,1,0:T(8,128)(2,1)S(1)}, u32[]{:S(2)}, u32[]{:S(2)}) %all-to-all-start.2) | async-done | bytes 2097184 | tf_op jit(solution)/shard_map/all_to_all | solution.py:29
  42.8 0.0 copy-start.1
  42.8 1.3 copy-done.1
  44.2 0.0 copy-done.2
  44.2 4.1 %bitcast_subtract_fusion = f32[1024,576]{0,1:T(8,128)} fusion(bf16[1024,1024]{1,0:T(8,128)(2,1)S(1)} %bitcast.32, bf16[1,1024,576]{1,2,0:T(8,128)(2,1)} %param.8, bf16[1024,576]{0,1:T(8,128)(2,1)S(1)} %copy-done.2, f32[576]{0:T(1024)S(1)} %convert_reduce_fusion.1, f32[1024]{0:T(1024)S(1)} %rsqrt_bitcast_fusion), kind=kOutput, calls=%fused_computation.7 | convolution fusion | flops 1212088320 | bytes 6822144 | tf_op jit(solution)/shard_map/dot_general | solution.py:42
  48.3 2.1 %copy.13 = f32[1024,576]{1,0:T(8,128)S(1)} copy(f32[1024,576]{0,1:T(8,128)} %bitcast_subtract_fusion) | data formatting | bytes 4718592 | tf_op jit(solution)/shard_map/sub | solution.py:45
  50.4 0.1 fusion.7
  50.5 10.9 %collective-permute-start = (bf16[2,8,4,8,576]{4,3,2,1,0:T(8,128)(2,1)S(1)}, bf16[2,8,4,8,576]{4,3,2,1,0:T(8,128)(2,1)}, u32[]{:S(2)}, u32[]{:S(2)}) collective-permute-start(bf16[2,8,4,8,576]{4,3,2,1,0:T(8,128)(2,1)S(1)} %fusion.7), channel_id=1, source_target_pairs={{0,8},{8,0},{1,9},{9,1},{2,10},{10,2},{3,11},{11,3},{4,12},{12,4},... | collective-permute-start | bytes 1769480 | tf_op jit(solution)/shard_map/ppermute | solution.py:51
  61.5 1.8 %collective-permute-done = bf16[2,8,4,8,576]{4,3,2,1,0:T(8,128)(2,1)} collective-permute-done((bf16[2,8,4,8,576]{4,3,2,1,0:T(8,128)(2,1)S(1)}, bf16[2,8,4,8,576]{4,3,2,1,0:T(8,128)(2,1)}, u32[]{:S(2)}, u32[]{:S(2)}) %collective-permute-start) | collective-permute-done | bytes 589856 | tf_op jit(solution)/shard_map/ppermute | solution.py:51
  63.3 1.3 bitcast_add_fusion
  64.5 0.0 copy-start
  64.6 1.0 copy-done
  65.6 0.0 copy-start.3
  65.6 4.2 %collective-permute-start.1 = (bf16[8,4,8,576]{3,2,1,0:T(8,128)(2,1)S(1)}, bf16[8,4,8,576]{3,2,1,0:T(8,128)(2,1)S(1)}, u32[]{:S(2)}, u32[]{:S(2)}) collective-permute-start(bf16[8,4,8,576]{3,2,1,0:T(8,128)(2,1)S(1)} %fusion.11), channel_id=1, source_target_pairs={{0,512},{512,0},{1,513},{513,1},{2,514},{514,2},{3,515},{515,3},{4... | collective-permute-start | bytes 884744 | tf_op jit(solution)/shard_map/ppermute | solution.py:54
  69.8 7.8 %collective-permute-done.1 = bf16[8,4,8,576]{3,2,1,0:T(8,128)(2,1)S(1)} collective-permute-done((bf16[8,4,8,576]{3,2,1,0:T(8,128)(2,1)S(1)}, bf16[8,4,8,576]{3,2,1,0:T(8,128)(2,1)S(1)}, u32[]{:S(2)}, u32[]{:S(2)}) %collective-permute-start.1) | collective-permute-done | bytes 294944 | tf_op jit(solution)/shard_map/ppermute | solution.py:54
  77.6 1.1 fusion.12
  78.8 0.8 copy.14
  79.5 6.3 %all-to-all-start.3 = ((bf16[4,8,8,576]{3,2,1,0:T(8,128)(2,1)}), bf16[4,8,8,576]{3,2,1,0:T(8,128)(2,1)S(1)}, u32[]{:S(2)}, u32[]{:S(2)}) async-start(bf16[4,8,8,576]{3,2,1,0:T(8,128)(2,1)} %copy.14), calls=%async_computation.3 | async-start | bytes 655360 | tf_op jit(solution)/shard_map/all_to_all | solution.py:55
  85.9 0.0 copy-done.3
  85.9 4.5 %convolution_convert_fusion = bf16[1024,1024]{1,0:T(8,128)(2,1)} fusion(bf16[1,1024,576]{1,2,0:T(8,128)(2,1)} %param.8, bf16[1024,576]{0,1:T(8,128)(2,1)S(1)} %copy-done.3, f32[576]{0:T(1024)S(1)} %convert_reduce_fusion.1, f32[1024]{0:T(1024)S(1)} %rsqrt_bitcast_fusion), kind=kOutput, calls=%fused_computation.8 | convolution fusion | flops 1211367424 | bytes 4462848 | tf_op jit(solution)/shard_map/dot_general | solution.py:35
  90.4 4.1 %all-to-all-done.3 = bf16[4,8,8,576]{3,2,1,0:T(8,128)(2,1)S(1)} async-done(((bf16[4,8,8,576]{3,2,1,0:T(8,128)(2,1)}), bf16[4,8,8,576]{3,2,1,0:T(8,128)(2,1)S(1)}, u32[]{:S(2)}, u32[]{:S(2)}) %all-to-all-start.3) | async-done | bytes 294944 | tf_op jit(solution)/shard_map/all_to_all | solution.py:55
  94.4 3.6 %all-to-all-start.1 = ((bf16[8,128,1024]{2,1,0:T(8,128)(2,1)}), bf16[8,128,1024]{2,1,0:T(8,128)(2,1)S(1)}, u32[]{:S(2)}, u32[]{:S(2)}) async-start(bf16[8,128,1024]{2,1,0:T(8,128)(2,1)} %bitcast.34), calls=%async_computation.1 | async-start | bytes 4194304 | tf_op jit(solution)/shard_map/all_to_all | solution.py:38
  98.0 0.7 reduce_sum.64
  98.7 27.8 %all-to-all-done.1 = bf16[8,128,1024]{2,1,0:T(8,128)(2,1)S(1)} async-done(((bf16[8,128,1024]{2,1,0:T(8,128)(2,1)}), bf16[8,128,1024]{2,1,0:T(8,128)(2,1)S(1)}, u32[]{:S(2)}, u32[]{:S(2)}) %all-to-all-start.1) | async-done | bytes 2097184 | tf_op jit(solution)/shard_map/all_to_all | solution.py:38
  126.6 26.0 %all-to-all-start.4 = ((bf16[8,8,576]{2,1,0:T(8,128)(2,1)}), bf16[8,8,576]{2,1,0:T(8,128)(2,1)S(1)}, u32[]{:S(2)}, u32[]{:S(2)}) async-start(bf16[8,8,576]{2,1,0:T(8,128)(2,1)} %reduce_sum.64), calls=%async_computation.4 | async-start | bytes 163840 | tf_op jit(solution)/shard_map/all_to_all | solution.py:57
  152.5 3.8 %fusion.3 = f32[576]{0:T(1024)S(1)} fusion(bf16[1024,576]{0,1:T(8,128)(2,1)} %param.6, bf16[1024,1024]{1,0:T(8,128)(2,1)} %bitcast.33, bf16[1,1024,576]{1,2,0:T(8,128)(2,1)} %param.8, f32[1024]{0:T(1024)S(1)} %rsqrt_bitcast_fusion), kind=kOutput, calls=%fused_computation.5 | convolution fusion | flops 1210318336 | bytes 4462848 | tf_op jit(solution)/shard_map/dot_general | solution.py:40
  156.3 0.0 copy-start.4
  156.3 0.0 copy-start.5
  156.3 0.6 broadcast_in_dim.21
  156.9 1.1 reduce_sum.62
  158.0 18.4 %all-to-all-done.4 = bf16[8,8,576]{2,1,0:T(8,128)(2,1)S(1)} async-done(((bf16[8,8,576]{2,1,0:T(8,128)(2,1)}), bf16[8,8,576]{2,1,0:T(8,128)(2,1)S(1)}, u32[]{:S(2)}, u32[]{:S(2)}) %all-to-all-start.4) | async-done | bytes 73760 | tf_op jit(solution)/shard_map/all_to_all | solution.py:57
  176.4 0.0 copy-done.4
  176.4 0.0 copy-done.5
  176.4 0.6 multiply_subtract_fusion
  (6 shorter events, 0.1 us)
Async XLA Ops:
  18.6 3.8 %copy-start.6 = (bf16[1,576]{1,0:T(2,128)(2,1)S(1)}, bf16[1,576]{1,0:T(2,128)(2,1)}, u32[]{:S(2)}) copy-start(bf16[1,576]{1,0:T(2,128)(2,1)} %param.7) | copy-start | bytes 3460
  18.6 25.6 %copy-start.2 = (bf16[1024,576]{0,1:T(8,128)(2,1)S(1)}, bf16[1024,576]{0,1:T(8,128)(2,1)}, u32[]{:S(2)}) copy-start(bf16[1024,576]{0,1:T(8,128)(2,1)} %param.6) | copy-start | bytes 3538948
  18.6 24.2 %all-to-all-start.2 = ((bf16[8,128,1024]{2,1,0:T(8,128)(2,1)}), bf16[8,128,1024]{2,1,0:T(8,128)(2,1)S(1)}, u32[]{:S(2)}, u32[]{:S(2)}) async-start(bf16[8,128,1024]{2,1,0:T(8,128)(2,1)} %broadcast_in_dim.20), calls=%async_computation.2 | async-start | bytes 4194304 | tf_op jit(solution)/shard_map/all_to_all | solution.py:29
  42.8 1.4 copy-start.1
  50.5 12.8 %collective-permute-start = (bf16[2,8,4,8,576]{4,3,2,1,0:T(8,128)(2,1)S(1)}, bf16[2,8,4,8,576]{4,3,2,1,0:T(8,128)(2,1)}, u32[]{:S(2)}, u32[]{:S(2)}) collective-permute-start(bf16[2,8,4,8,576]{4,3,2,1,0:T(8,128)(2,1)S(1)} %fusion.7), channel_id=1, source_target_pairs={{0,8},{8,0},{1,9},{9,1},{2,10},{10,2},{3,11},{11,3},{4,12},{12,4},... | collective-permute-start | bytes 1769480 | tf_op jit(solution)/shard_map/ppermute | solution.py:51
  64.5 1.1 copy-start
  65.6 20.3 %copy-start.3 = (bf16[1024,576]{0,1:T(8,128)(2,1)S(1)}, bf16[1024,576]{0,1:T(8,128)(2,1)}, u32[]{:S(2)}) copy-start(bf16[1024,576]{0,1:T(8,128)(2,1)} %param.6) | copy-start | bytes 3538948
  65.6 12.0 %collective-permute-start.1 = (bf16[8,4,8,576]{3,2,1,0:T(8,128)(2,1)S(1)}, bf16[8,4,8,576]{3,2,1,0:T(8,128)(2,1)S(1)}, u32[]{:S(2)}, u32[]{:S(2)}) collective-permute-start(bf16[8,4,8,576]{3,2,1,0:T(8,128)(2,1)S(1)} %fusion.11), channel_id=1, source_target_pairs={{0,512},{512,0},{1,513},{513,1},{2,514},{514,2},{3,515},{515,3},{4... | collective-permute-start | bytes 884744 | tf_op jit(solution)/shard_map/ppermute | solution.py:54
  79.5 14.9 %all-to-all-start.3 = ((bf16[4,8,8,576]{3,2,1,0:T(8,128)(2,1)}), bf16[4,8,8,576]{3,2,1,0:T(8,128)(2,1)S(1)}, u32[]{:S(2)}, u32[]{:S(2)}) async-start(bf16[4,8,8,576]{3,2,1,0:T(8,128)(2,1)} %copy.14), calls=%async_computation.3 | async-start | bytes 655360 | tf_op jit(solution)/shard_map/all_to_all | solution.py:55
  94.4 32.1 %all-to-all-start.1 = ((bf16[8,128,1024]{2,1,0:T(8,128)(2,1)}), bf16[8,128,1024]{2,1,0:T(8,128)(2,1)S(1)}, u32[]{:S(2)}, u32[]{:S(2)}) async-start(bf16[8,128,1024]{2,1,0:T(8,128)(2,1)} %bitcast.34), calls=%async_computation.1 | async-start | bytes 4194304 | tf_op jit(solution)/shard_map/all_to_all | solution.py:38
  126.6 49.8 %all-to-all-start.4 = ((bf16[8,8,576]{2,1,0:T(8,128)(2,1)}), bf16[8,8,576]{2,1,0:T(8,128)(2,1)S(1)}, u32[]{:S(2)}, u32[]{:S(2)}) async-start(bf16[8,8,576]{2,1,0:T(8,128)(2,1)} %reduce_sum.64), calls=%async_computation.4 | async-start | bytes 163840 | tf_op jit(solution)/shard_map/all_to_all | solution.py:57
  156.3 20.1 %copy-start.4 = (f32[8,576]{1,0:T(8,128)S(1)}, f32[8,576]{1,0:T(8,128)}, u32[]{:S(2)}) copy-start(f32[8,576]{1,0:T(8,128)} %param.10) | copy-start | bytes 55300
  156.3 20.1 %copy-start.5 = (f32[8,576]{1,0:T(8,128)S(1)}, f32[8,576]{1,0:T(8,128)}, u32[]{:S(2)}) copy-start(f32[8,576]{1,0:T(8,128)} %param.11) | copy-start | bytes 55300

commit v2 on v1

v2 whole, which is shorter than its diff:
```python
import functools

import jax
import jax.numpy as jnp
from jax import lax
from jax.experimental import pallas as pl
from jax.experimental.pallas import tpu as pltpu
from jax.sharding import Mesh, PartitionSpec as P

D = 4608
N_REP = 128
FEAT = 576

rms_eps = 1e-06
inner_rate = 0.3
outer_rate = 0.7
outer_beta = 0.9

FSDP = ("x", "yh")
REP = ("yl", "zh", "zl", "core")
ZC = ("zh", "zl", "core")
SWAP = [(0, 1), (1, 0)]
f32 = jnp.float32
bf16 = jnp.bfloat16
S = jax.ShapeDtypeStruct
PARAMS = pltpu.CompilerParams(vmem_limit_bytes=40 * 2**20)


def z_shift(delta):
    pairs = []
    for z in range(32):
        for core, sign in ((0, 1), (1, -1)):
            pairs.append((z * 2 + core, (z + sign * delta) % 32 * 2 + core))
    return pairs


def pack_kernel(cot_ref, tok_ref, first_ref, second_ref, turned):
    yl = lax.axis_index("yl")
    turned[...] = cot_ref[...].astype(f32).T.reshape(2, 32, 2, 8, 128)
    rows = []
    for j in range(8):
        tok = tok_ref[:, j * 128 : (j + 1) * 128].astype(f32)
        rows.append(jnp.sum(tok * tok, axis=0, keepdims=True))
    square = jnp.concatenate(rows, axis=0)
    high = square.astype(bf16).astype(f32)
    middle = (square - high).astype(bf16).astype(f32)
    low = square - high - middle
    tail = jnp.concatenate([high, middle, low, jnp.zeros_like(low)], axis=0).astype(bf16)
    other, mine = turned[1 - yl], turned[yl]
    for core in range(2):
        to_other = other[:, core].reshape(256, 128).astype(bf16)
        to_mine = mine[:, core].reshape(256, 128).astype(bf16)
        for peer in range(8):
            first_ref[core * 8 + peer, 0:256] = to_other
            first_ref[core * 8 + peer, 256:288] = tail
            second_ref[core * 8 + peer] = to_mine


def product(got_ref, core, hidden):
    cot = jnp.concatenate([got_ref[core * 8 + g, 0:256] for g in range(8)], axis=1)
    return lax.dot_general(cot, hidden, (((1,), (1,)), ((), ())), preferred_element_type=f32)


def first_kernel(
    got_ref, tok_ref, tok_sib_ref, gain_ref, gain_sib_ref, w_ref, w_sib_ref,
    send_ref, hid_ref, hid_sib_ref, part_ref, part_sib_ref,
):
    core = lax.axis_index("core")
    yl = lax.axis_index("yl")
    new = jnp.zeros((256, FEAT), f32)
    for which, tok, gain, weight, hid_out, part in (
        (core, tok_ref, gain_ref, w_ref, hid_ref, part_ref),
        (1 - core, tok_sib_ref, gain_sib_ref, w_sib_ref, hid_sib_ref, part_sib_ref),
    ):
        square = jnp.zeros((8, 128), f32)
        for g in range(8):
            tail = got_ref[which * 8 + g, 256:288].astype(f32)
            square += tail[0:8] + (tail[8:16] + tail[16:24])
        inv_rms = lax.rsqrt(square / D + rms_eps)
        for j in range(8):
            normed = tok[:, j * 128 : (j + 1) * 128].astype(f32) * inv_rms[j : j + 1]
            hid_out[:, j * 128 : (j + 1) * 128] = (normed * gain[...]).astype(bf16)
        grad = product(got_ref, which, hid_out[...])
        w = weight[1 - yl].astype(f32)
        part[...] = jnp.sum(w * grad, axis=0, keepdims=True)
        new += w - inner_rate * grad
    send_ref[...] = new.astype(bf16)


def second_kernel(
    got_ref, hid_ref, hid_sib_ref, w_ref, w_sib_ref, arrived_ref, part_ref, part_sib_ref,
    keep_ref, plus_ref, minus_ref, gain_ref, gain_sib_ref, total,
):
    core = lax.axis_index("core")
    yl = lax.axis_index("yl")
    z = lax.axis_index("zh") * 4 + lax.axis_index("zl")
    sign = 1 - 2 * core
    new = arrived_ref[...].astype(f32)
    for which, hid, weight, part, out in (
        (core, hid_ref, w_ref, part_ref, gain_ref),
        (1 - core, hid_sib_ref, w_sib_ref, part_sib_ref, gain_sib_ref),
    ):
        grad = product(got_ref, which, hid[...])
        w = weight[yl].astype(f32)
        out[...] = part[...] + jnp.sum(w * grad, axis=0, keepdims=True)
        new += w - inner_rate * grad
    total[...] = new.reshape(32, 8, FEAT)

    def block(offset):
        return total[(z + sign * offset + 64) % 32]

    for i in range(11):
        at = 3 * i - 12
        keep_ref[i] = block(at)
        minus_ref[i] = block(at - 1).astype(bf16)
        if i < 10:
            plus_ref[i] = block(at + 1).astype(bf16)


def third_kernel(keep_ref, plus_ref, minus_ref, keep_out, plus_out, minus_out):
    total = []
    for i in range(11):
        value = keep_ref[i] + minus_ref[i].astype(f32)
        if i < 10:
            value += plus_ref[i].astype(f32)
        total.append(value)
    for c in range(4):
        keep_out[c] = total[3 * c + 1]
        minus_out[c] = total[3 * c].astype(bf16)
        if c < 3:
            plus_out[c] = total[3 * c + 2].astype(bf16)


def fourth_kernel(keep_ref, plus_ref, minus_ref, keep_out, back_out, on_out, far_out):
    total = []
    for c in range(4):
        value = keep_ref[c] + minus_ref[c].astype(f32)
        if c < 3:
            value += plus_ref[c].astype(f32)
        total.append(value)
    back_out[0] = total[0].astype(bf16)
    keep_out[...] = total[1]
    on_out[0] = total[2].astype(bf16)
    far_out[0] = total[3].astype(bf16)


def per_device(tokens, norm_gain, key_weight, key_cotangent, global_fragment, outer_momentum):
    core = lax.axis_index("core")
    tok = tokens.T
    first, second = pl.pallas_call(
        pack_kernel,
        out_shape=(S((16, 288, 128), bf16), S((16, 256, 128), bf16)),
        scratch_shapes=[pltpu.VMEM((2, 32, 2, 8, 128), f32)],
        compiler_params=PARAMS,
        name="pack",
    )(key_cotangent, tok)
    got_first = lax.all_to_all(first, ("core",) + FSDP, 0, 0)

    weight_t = key_weight[0].T
    blocks = key_weight.reshape(2, 32, 2, 8, FEAT)
    w_mine = lax.dynamic_index_in_dim(blocks, core, 2, keepdims=False).reshape(2, 256, FEAT)
    w_other = lax.dynamic_index_in_dim(blocks, 1 - core, 2, keepdims=False).reshape(2, 256, FEAT)
    gain = norm_gain.astype(f32).reshape(FEAT, 1)
    tok_sib = lax.ppermute(tok, "core", SWAP)
    gain_sib = lax.ppermute(gain, "core", SWAP)
    w_sib = lax.ppermute(w_other, "core", SWAP)

    send, hid, hid_sib, part, part_sib = pl.pallas_call(
        first_kernel,
        out_shape=(
            S((256, FEAT), bf16), S((FEAT, 1024), bf16), S((FEAT, 1024), bf16),
            S((1, FEAT), f32), S((1, FEAT), f32),
        ),
        compiler_params=PARAMS,
        name="first",
    )(got_first, tok, tok_sib, gain, gain_sib, w_mine, w_sib)
    arrived = lax.ppermute(send, "yl", SWAP)
    second, _ = lax.optimization_barrier((second, got_first))
    got_second = lax.all_to_all(second, ("core",) + FSDP, 0, 0)

    partial_keys = lax.dot_general(
        hid, weight_t, (((0,), (0,)), ((), ())), preferred_element_type=f32
    ).astype(bf16)

    keep, plus, minus, part, part_sib = pl.pallas_call(
        second_kernel,
        out_shape=(
            S((11, 8, FEAT), f32), S((10, 8, FEAT), bf16), S((11, 8, FEAT), bf16),
            S((1, FEAT), f32), S((1, FEAT), f32),
        ),
        scratch_shapes=[pltpu.VMEM((32, 8, FEAT), f32)],
        compiler_params=PARAMS,
        name="second",
    )(got_second, hid, hid_sib, w_mine, w_sib, arrived, part, part_sib)

    partial_keys, _ = lax.optimization_barrier((partial_keys, got_second))
    key_parts = lax.all_to_all(partial_keys.reshape(8, 128, 1024), FSDP, 0, 0)
    key_out = jnp.sum(key_parts.astype(f32), axis=0).astype(bf16)

    plus = lax.ppermute(plus, ZC, z_shift(1))
    minus = lax.ppermute(minus, ZC, z_shift(-1))
    keep, plus, minus = pl.pallas_call(
        third_kernel,
        out_shape=(S((4, 8, FEAT), f32), S((3, 8, FEAT), bf16), S((4, 8, FEAT), bf16)),
        compiler_params=PARAMS,
        name="third",
    )(keep, plus, minus)
    plus = lax.ppermute(plus, ZC, z_shift(3))
    minus = lax.ppermute(minus, ZC, z_shift(-3))
    one = S((1, 8, FEAT), bf16)
    keep, back, on, far = pl.pallas_call(
        fourth_kernel,
        out_shape=(S((8, FEAT), f32), one, one, one),
        compiler_params=PARAMS,
        name="fourth",
    )(keep, plus, minus)
    far = lax.ppermute(far, ZC, z_shift(18))
    on = lax.ppermute(on, ZC, z_shift(9))
    back = lax.ppermute(back, ZC, z_shift(-9))
    gain_grad = part + lax.ppermute(part_sib, "core", SWAP)
    gain_grad = gain_grad / norm_gain.astype(f32)
    summed = keep + far[0].astype(f32) + on[0].astype(f32) + back[0].astype(f32)
    avg_grad = global_fragment - summed / N_REP
    new_momentum = outer_beta * outer_momentum + avg_grad
    new_global = global_fragment - outer_rate * (avg_grad + outer_beta * new_momentum)
    return (key_out, gain_grad, new_global, new_momentum)


def solution(mesh):
    fine = Mesh(mesh.devices.reshape(2, 8, 4, 2, 4, 2), REP + FSDP)
    return jax.shard_map(
        per_device,
        mesh=fine,
        in_specs=(
            P(REP, FSDP),
            P(REP, FSDP),
            P(REP, None, FSDP),
            P(REP + FSDP, None),
            P(REP, FSDP),
            P(REP, FSDP),
        ),
        out_specs=(P(REP + FSDP, None), P(REP, FSDP), P(REP, FSDP), P(REP, FSDP)),
        check_vma=False,
    )
```

time: 179 us -> 176 us (0.983)
  the two profiles are of different devices: /device:TPU:1 before, /device:TPU:16 now
where the time goes in v2:
time: 176 us; the launch traced here: 175 us
  starting transfers between devices  89 us (51%)
  waiting for transfers between devices  56.5 us (32%)
  local copies, waits for them, and re-layouts  16.8 us (10%)
  Pallas kernels  5.17 us (3%)
  other arithmetic  3.95 us (2%)
  matrix products  3.21 us (2%)
    ppermute x1, waiting for transfers between devices, per_device(): arrived = lax.ppermute(send, 'yl', SWAP)  28.1 us
    all_to_all x1, starting transfers between devices, per_device(): got_first = lax.all_to_all(first, ('core',) + FSDP, 0, 0)  16.6 us
    all_to_all x1, waiting for transfers between devices, per_device(): got_first = lax.all_to_all(first, ('core',) + FSDP, 0, 0)  13.6 us
    unnamed x33, local copies, waits for them, and re-layouts  12.1 us
    ppermute x1, starting transfers between devices, per_device(): far = lax.ppermute(far, ZC, z_shift(18))  11.1 us
    ppermute x1, starting transfers between devices, per_device(): minus = lax.ppermute(minus, ZC, z_shift(-1))  11.1 us
    ppermute x1, starting transfers between devices, per_device(): on = lax.ppermute(on, ZC, z_shift(9))  8.8 us
    ppermute x1, starting transfers between devices, per_device(): back = lax.ppermute(back, ZC, z_shift(-9))  7.86 us
  transfers between devices with their start and end apart: 15, of which 6 were waited for; matrix products, arithmetic and copies ran while one was open for 7% of the time, Pallas kernels for 3%

profile of v2, /device:TPU:16, one launch (start us, length us, event | category | flops | bytes accessed | tf_op | source)
XLA Modules:
  0.0 175.4 jit_solution(15150186862920921375)
XLA Ops:
  0.6 0.0 copy-start
  0.6 1.3 copy-done
  1.9 0.0 copy-start.10
  1.9 0.9 copy-done.10
  2.9 0.6 pack.1
  3.4 0.0 copy-start.4
  3.5 1.0 copy-done.4
  4.5 0.0 copy-start.9
  4.5 1.0 copy-done.9
  5.4 16.6 %all-to-all-start = ((bf16[16,288,128]{2,1,0:T(8,128)(2,1)}), bf16[16,288,128]{2,1,0:T(8,128)(2,1)S(1)}, u32[]{:S(2)}, u32[]{:S(2)}) async-start(bf16[16,288,128]{2,1,0:T(8,128)(2,1)} %copy-done.4), calls=%async_computation | async-start | bytes 2359296 | tf_op jit(solution)/shard_map/all_to_all | solution.py:157
  22.0 0.0 copy-done.1
  22.1 2.1 %collective-permute-start = (bf16[576,1024]{1,0:T(8,128)(2,1)S(1)}, bf16[576,1024]{1,0:T(8,128)(2,1)}, u32[]{:S(2)}, u32[]{:S(2)}) collective-permute-start(bf16[576,1024]{1,0:T(8,128)(2,1)S(1)} %bitcast.38), channel_id=1, source_target_pairs={{0,8},{8,0},{1,9},{9,1},{2,10},{10,2},{3,11},{11,3},{4,12},{12,4},... | collective-permute-start | bytes 3538952 | tf_op jit(solution)/shard_map/ppermute | solution.py:164
  24.1 2.4 %copy.21 = bf16[1,1024,576]{2,1,0:T(8,128)(2,1)} copy(bf16[1,1024,576]{1,2,0:T(8,128)(2,1)} %param.8) | data formatting | bytes 2359296 | tf_op args[2]
  26.6 13.6 %all-to-all-done.got_ref = bf16[16,288,128]{2,1,0:T(8,128)(2,1)S(1)} async-done(((bf16[16,288,128]{2,1,0:T(8,128)(2,1)}), bf16[16,288,128]{2,1,0:T(8,128)(2,1)S(1)}, u32[]{:S(2)}, u32[]{:S(2)}) %all-to-all-start) | async-done | bytes 1179680 | tf_op jit(solution)/shard_map/all_to_all | solution.py:157
  40.2 6.4 %all-to-all-start.1 = ((bf16[16,256,128]{2,1,0:T(8,128)(2,1)}), bf16[16,256,128]{2,1,0:T(8,128)(2,1)S(1)}, u32[]{:S(2)}, u32[]{:S(2)}) async-start(bf16[16,256,128]{2,1,0:T(8,128)(2,1)} %copy-done.9), calls=%async_computation.1 | async-start | bytes 2097152 | tf_op jit(solution)/shard_map/all_to_all | solution.py:179
  46.6 0.0 copy-done.2
  46.6 1.4 dynamic-slice_bitcast_fusion
  48.0 0.0 copy-start.15
  48.0 1.1 copy.22
  49.1 2.1 %collective-permute-start.2 = (bf16[2,256,576]{1,2,0:T(8,128)(2,1)}, bf16[2,256,576]{1,2,0:T(8,128)(2,1)}, u32[]{:S(2)}, u32[]{:S(2)}) collective-permute-start(bf16[2,256,576]{1,2,0:T(8,128)(2,1)} %copy.22), channel_id=1, source_target_pairs={{0,8},{8,0},{1,9},{9,1},{2,10},{10,2},{3,11},{11,3},{4,12},{12,4},... | collective-permute-start | bytes 1769480 | tf_op jit(solution)/shard_map/ppermute | solution.py:166
  51.2 0.0 copy-done.15
  51.2 0.9 copy.23.gain_ref
  52.1 2.2 %collective-permute-start.1 = (f32[576,1]{1,0:T(8,128)}, f32[576,1]{1,0:T(8,128)}, u32[]{:S(2)}, u32[]{:S(2)}) collective-permute-start(f32[576,1]{1,0:T(8,128)} %copy.23.gain_ref), channel_id=1, source_target_pairs={{0,8},{8,0},{1,9},{9,1},{2,10},{10,2},{3,11},{11,3},{4,12},{12,4},... | collective-permute-start | bytes 6920 | tf_op jit(solution)/shard_map/ppermute | solution.py:165
  54.3 0.0 collective-permute-done.2
  54.3 1.4 copy.24.w_sib_ref
  55.7 0.2 collective-permute-done.1.gain_sib_ref
  55.9 0.0 collective-permute-done.tok_sib_ref
  55.9 1.3 copy-done.3
  57.2 3.4 %first.1 = (bf16[256,576]{1,0:T(8,128)(2,1)S(1)}, bf16[576,1024]{1,0:T(8,128)(2,1)S(1)}, bf16[576,1024]{1,0:T(8,128)(2,1)S(1)}, f32[1,576]{1,0:T(1,128)S(1)}, f32[1,576]{1,0:T(1,128)S(1)}) custom-call(bf16[16,288,128]{2,1,0:T(8,128)(2,1)S(1)} %copy-done.3, bf16[576,1024]{1,0:T(8,128)(2,1)S(1)} %bitcast.39, ...), custom_call_target="tpu_custom_call" | custom-call | tf_op jit(solution)/shard_map/first/pallas_call | solution.py:168
  60.5 0.0 copy-start.7
  60.5 1.1 copy-done.7
  61.6 0.8 copy-done.11
  62.4 0.0 copy-done.12
  62.4 3.2 %convolution_convert_fusion = bf16[1024,1024]{1,0:T(8,128)(2,1)} fusion(bf16[576,1024]{1,0:T(8,128)(2,1)S(1)} %get-tuple-element.26.hid_ref, bf16[1,1024,576]{1,2,0:T(8,128)(2,1)S(1)} %copy-done.12), kind=kOutput, calls=%fused_computation | convolution fusion | flops 1209008128 | bytes 4456448 | tf_op jit(solution)/shard_map/dot_general | solution.py:181
  65.6 1.0 copy-done.5
  66.7 0.0 all-to-all-done.1.got_ref
  66.7 7.4 %all-to-all-start.2 = ((bf16[8,128,1024]{2,1,0:T(8,128)(2,1)}), bf16[8,128,1024]{2,1,0:T(8,128)(2,1)}, u32[]{:S(2)}, u32[]{:S(2)}) async-start(bf16[8,128,1024]{2,1,0:T(8,128)(2,1)} %bitcast.41), calls=%async_computation.2 | async-start | bytes 4194304 | tf_op jit(solution)/shard_map/all_to_all | solution.py:197
  74.0 1.9 %collective-permute-start.3 = (bf16[256,576]{1,0:T(8,128)(2,1)}, bf16[256,576]{1,0:T(8,128)(2,1)S(1)}, u32[]{:S(2)}, u32[]{:S(2)}) collective-permute-start(bf16[256,576]{1,0:T(8,128)(2,1)} %copy-done.11), channel_id=1, source_target_pairs={{0,512},{512,0},{1,513},{513,1},{2,514},{514,2},{3,515},{515,3},{4... | collective-permute-start | bytes 884744 | tf_op jit(solution)/shard_map/ppermute | solution.py:177
  75.9 28.1 %collective-permute-done.3.arrived_ref = bf16[256,576]{1,0:T(8,128)(2,1)S(1)} collective-permute-done((bf16[256,576]{1,0:T(8,128)(2,1)}, bf16[256,576]{1,0:T(8,128)(2,1)S(1)}, u32[]{:S(2)}, u32[]{:S(2)}) %collective-permute-start.3) | collective-permute-done | bytes 294944 | tf_op jit(solution)/shard_map/ppermute | solution.py:177
  104.0 0.0 copy-done.6
  104.0 1.3 copy-done.8
  105.3 1.1 second.1
  106.4 11.1 %collective-permute-start.6 = (bf16[11,8,576]{2,1,0:T(8,128)(2,1)S(1)}, bf16[11,8,576]{2,1,0:T(8,128)(2,1)S(1)}, u32[]{:S(2)}, u32[]{:S(2)}) collective-permute-start(bf16[11,8,576]{2,1,0:T(8,128)(2,1)S(1)} %get-tuple-element.38), channel_id=1, source_target_pairs={{0,496},{8,24},{16,0},{24,40},{32,16},{40,56},{48,32},{56,72},{64,... | collective-permute-start | bytes 304136 | tf_op jit(solution)/shard_map/ppermute | solution.py:201
  117.5 1.9 %collective-permute-start.5 = (bf16[10,8,576]{2,1,0:T(8,128)(2,1)S(1)}, bf16[10,8,576]{2,1,0:T(8,128)(2,1)S(1)}, u32[]{:S(2)}, u32[]{:S(2)}) collective-permute-start(bf16[10,8,576]{2,1,0:T(8,128)(2,1)S(1)} %get-tuple-element.37), channel_id=1, source_target_pairs={{0,16},{8,504},{16,32},{24,8},{32,48},{40,24},{48,64},{56,40},{64,... | collective-permute-start | bytes 276488 | tf_op jit(solution)/shard_map/ppermute | solution.py:200
  119.4 5.8 %collective-permute-done.5.plus_ref = bf16[10,8,576]{2,1,0:T(8,128)(2,1)S(1)} collective-permute-done((bf16[10,8,576]{2,1,0:T(8,128)(2,1)S(1)}, bf16[10,8,576]{2,1,0:T(8,128)(2,1)S(1)}, u32[]{:S(2)}, u32[]{:S(2)}) %collective-permute-start.5) | collective-permute-done | bytes 92192 | tf_op jit(solution)/shard_map/ppermute | solution.py:200
  125.3 0.0 collective-permute-done.6.minus_ref
  125.3 2.8 %collective-permute-start.8 = (bf16[4,8,576]{2,1,0:T(8,128)(2,1)S(1)}, bf16[4,8,576]{2,1,0:T(8,128)(2,1)S(1)}, u32[]{:S(2)}, u32[]{:S(2)}) collective-permute-start(bf16[4,8,576]{2,1,0:T(8,128)(2,1)S(1)} %get-tuple-element.41), channel_id=1, source_target_pairs={{0,464},{8,56},{16,480},{24,72},{32,496},{40,88},{48,0},{56,104},{... | collective-permute-start | bytes 110600 | tf_op jit(solution)/shard_map/ppermute | solution.py:209
  128.1 4.8 %collective-permute-start.7 = (bf16[3,8,576]{2,1,0:T(8,128)(2,1)S(1)}, bf16[3,8,576]{2,1,0:T(8,128)(2,1)S(1)}, u32[]{:S(2)}, u32[]{:S(2)}) collective-permute-start(bf16[3,8,576]{2,1,0:T(8,128)(2,1)S(1)} %get-tuple-element.40), channel_id=1, source_target_pairs={{0,48},{8,472},{16,64},{24,488},{32,80},{40,504},{48,96},{56,8},{6... | collective-permute-start | bytes 82952 | tf_op jit(solution)/shard_map/ppermute | solution.py:208
  133.0 1.9 %collective-permute-start.4 = (f32[1,576]{1,0:T(1,128)S(1)}, f32[1,576]{1,0:T(1,128)S(1)}, u32[]{:S(2)}, u32[]{:S(2)}) collective-permute-start(f32[1,576]{1,0:T(1,128)S(1)} %get-tuple-element.35), channel_id=1, source_target_pairs={{0,8},{8,0},{1,9},{9,1},{2,10},{10,2},{3,11},{11,3},{4,12},{12,4},... | collective-permute-start | bytes 6920 | tf_op jit(solution)/shard_map/ppermute | solution.py:220
  134.9 2.0 %collective-permute-done.7.plus_ref = bf16[3,8,576]{2,1,0:T(8,128)(2,1)S(1)} collective-permute-done((bf16[3,8,576]{2,1,0:T(8,128)(2,1)S(1)}, bf16[3,8,576]{2,1,0:T(8,128)(2,1)S(1)}, u32[]{:S(2)}, u32[]{:S(2)}) %collective-permute-start.7) | collective-permute-done | bytes 27680 | tf_op jit(solution)/shard_map/ppermute | solution.py:208
  136.9 0.0 collective-permute-done.8.minus_ref
  136.9 11.1 %collective-permute-start.9 = (bf16[1,8,576]{2,1,0:T(8,128)(2,1)S(1)}, bf16[1,8,576]{2,1,0:T(8,128)(2,1)S(1)}, u32[]{:S(2)}, u32[]{:S(2)}) collective-permute-start(bf16[1,8,576]{2,1,0:T(8,128)(2,1)S(1)} %get-tuple-element.43), channel_id=1, source_target_pairs={{0,288},{8,232},{16,304},{24,248},{32,320},{40,264},{48,336},{56,2... | collective-permute-start | bytes 27656 | tf_op jit(solution)/shard_map/ppermute | solution.py:217
  148.0 8.8 %collective-permute-start.10 = (bf16[1,8,576]{2,1,0:T(8,128)(2,1)S(1)}, bf16[1,8,576]{2,1,0:T(8,128)(2,1)S(1)}, u32[]{:S(2)}, u32[]{:S(2)}) collective-permute-start(bf16[1,8,576]{2,1,0:T(8,128)(2,1)S(1)} %get-tuple-element.44), channel_id=1, source_target_pairs={{0,144},{8,376},{16,160},{24,392},{32,176},{40,408},{48,192},{56,4... | collective-permute-start | bytes 27656 | tf_op jit(solution)/shard_map/ppermute | solution.py:218
  156.9 7.9 %collective-permute-start.11 = (bf16[1,8,576]{2,1,0:T(8,128)(2,1)S(1)}, bf16[1,8,576]{2,1,0:T(8,128)(2,1)S(1)}, u32[]{:S(2)}, u32[]{:S(2)}) collective-permute-start(bf16[1,8,576]{2,1,0:T(8,128)(2,1)S(1)} %get-tuple-element.45), channel_id=1, source_target_pairs={{0,368},{8,152},{16,384},{24,168},{32,400},{40,184},{48,416},{56,2... | collective-permute-start | bytes 27656 | tf_op jit(solution)/shard_map/ppermute | solution.py:219
  164.7 0.0 collective-permute-done.4
  164.7 0.6 add_divide_fusion
  165.3 0.0 collective-permute-done.9
  165.3 0.0 collective-permute-done.10
  165.3 6.7 %collective-permute-done.11 = bf16[1,8,576]{2,1,0:T(8,128)(2,1)S(1)} collective-permute-done((bf16[1,8,576]{2,1,0:T(8,128)(2,1)S(1)}, bf16[1,8,576]{2,1,0:T(8,128)(2,1)S(1)}, u32[]{:S(2)}, u32[]{:S(2)}) %collective-permute-start.11) | collective-permute-done | bytes 9248 | tf_op jit(solution)/shard_map/ppermute | solution.py:219
  172.0 0.0 copy-done.13
  172.0 0.0 copy-done.14
  172.0 0.6 multiply_subtract_fusion
  172.7 0.0 all-to-all-done.2
  172.7 2.7 %reduce_sum.12 = bf16[128,1024]{1,0:T(8,128)(2,1)} reduce(bf16[8,128,1024]{2,1,0:T(8,128)(2,1)} %all-to-all-done.2, bf16[]{:T(256)} %constant.24.clone.1), dimensions={0}, to_apply=%region_0.1 | reduce | flops 917504 | bytes 2359298 | tf_op jit(solution)/shard_map/reduce_sum | solution.py:198
  (13 shorter events, 0.1 us)
Async XLA Ops:
  0.6 1.3 copy-start
  1.9 0.9 copy-start.10
  3.4 1.0 copy-start.4
  4.5 1.0 copy-start.9
  5.4 16.6 %copy-start.1 = (bf16[1024,576]{0,1:T(8,128)(2,1)S(1)}, bf16[1024,576]{0,1:T(8,128)(2,1)}, u32[]{:S(2)}) copy-start(bf16[1024,576]{0,1:T(8,128)(2,1)} %param.6) | copy-start | bytes 3538948
  5.4 34.8 %all-to-all-start = ((bf16[16,288,128]{2,1,0:T(8,128)(2,1)}), bf16[16,288,128]{2,1,0:T(8,128)(2,1)S(1)}, u32[]{:S(2)}, u32[]{:S(2)}) async-start(bf16[16,288,128]{2,1,0:T(8,128)(2,1)} %copy-done.4), calls=%async_computation | async-start | bytes 2359296 | tf_op jit(solution)/shard_map/all_to_all | solution.py:157
  22.1 33.8 %collective-permute-start = (bf16[576,1024]{1,0:T(8,128)(2,1)S(1)}, bf16[576,1024]{1,0:T(8,128)(2,1)}, u32[]{:S(2)}, u32[]{:S(2)}) collective-permute-start(bf16[576,1024]{1,0:T(8,128)(2,1)S(1)} %bitcast.38), channel_id=1, source_target_pairs={{0,8},{8,0},{1,9},{9,1},{2,10},{10,2},{3,11},{11,3},{4,12},{12,4},... | collective-permute-start | bytes 3538952 | tf_op jit(solution)/shard_map/ppermute | solution.py:164
  40.2 6.4 %copy-start.2 = (bf16[16,288,128]{2,1,0:T(8,128)(2,1)}, bf16[16,288,128]{2,1,0:T(8,128)(2,1)S(1)}, u32[]{:S(2)}) copy-start(bf16[16,288,128]{2,1,0:T(8,128)(2,1)S(1)} %all-to-all-done.got_ref) | copy-start | bytes 3538948
  40.2 26.5 %all-to-all-start.1 = ((bf16[16,256,128]{2,1,0:T(8,128)(2,1)}), bf16[16,256,128]{2,1,0:T(8,128)(2,1)S(1)}, u32[]{:S(2)}, u32[]{:S(2)}) async-start(bf16[16,256,128]{2,1,0:T(8,128)(2,1)} %copy-done.9), calls=%async_computation.1 | async-start | bytes 2097152 | tf_op jit(solution)/shard_map/all_to_all | solution.py:179
  48.0 3.1 %copy-start.15 = (bf16[1,576]{1,0:T(2,128)(2,1)S(1)}, bf16[1,576]{1,0:T(2,128)(2,1)}, u32[]{:S(2)}) copy-start(bf16[1,576]{1,0:T(2,128)(2,1)} %param.7) | copy-start | bytes 3460
  49.1 5.2 %collective-permute-start.2 = (bf16[2,256,576]{1,2,0:T(8,128)(2,1)}, bf16[2,256,576]{1,2,0:T(8,128)(2,1)}, u32[]{:S(2)}, u32[]{:S(2)}) collective-permute-start(bf16[2,256,576]{1,2,0:T(8,128)(2,1)} %copy.22), channel_id=1, source_target_pairs={{0,8},{8,0},{1,9},{9,1},{2,10},{10,2},{3,11},{11,3},{4,12},{12,4},... | collective-permute-start | bytes 1769480 | tf_op jit(solution)/shard_map/ppermute | solution.py:166
  52.1 3.8 %collective-permute-start.1 = (f32[576,1]{1,0:T(8,128)}, f32[576,1]{1,0:T(8,128)}, u32[]{:S(2)}, u32[]{:S(2)}) collective-permute-start(f32[576,1]{1,0:T(8,128)} %copy.23.gain_ref), channel_id=1, source_target_pairs={{0,8},{8,0},{1,9},{9,1},{2,10},{10,2},{3,11},{11,3},{4,12},{12,4},... | collective-permute-start | bytes 6920 | tf_op jit(solution)/shard_map/ppermute | solution.py:165
  55.9 1.3 copy-start.3
  57.2 5.3 %copy-start.12 = (bf16[1,1024,576]{1,2,0:T(8,128)(2,1)S(1)}, bf16[1,1024,576]{1,2,0:T(8,128)(2,1)}, u32[]{:S(2)}) copy-start(bf16[1,1024,576]{1,2,0:T(8,128)(2,1)} %param.8) | copy-start | bytes 3538948
  60.5 1.1 copy-start.7
  61.6 0.8 copy-start.11
  65.6 1.0 copy-start.5
  66.7 37.3 %copy-start.6 = (bf16[576,1024]{1,0:T(8,128)(2,1)S(1)}, bf16[576,1024]{1,0:T(8,128)(2,1)}, u32[]{:S(2)}) copy-start(bf16[576,1024]{1,0:T(8,128)(2,1)} %copy-done.5) | copy-start | bytes 3538948
  66.7 106.0 %all-to-all-start.2 = ((bf16[8,128,1024]{2,1,0:T(8,128)(2,1)}), bf16[8,128,1024]{2,1,0:T(8,128)(2,1)}, u32[]{:S(2)}, u32[]{:S(2)}) async-start(bf16[8,128,1024]{2,1,0:T(8,128)(2,1)} %bitcast.41), calls=%async_computation.2 | async-start | bytes 4194304 | tf_op jit(solution)/shard_map/all_to_all | solution.py:197
  74.0 30.0 %collective-permute-start.3 = (bf16[256,576]{1,0:T(8,128)(2,1)}, bf16[256,576]{1,0:T(8,128)(2,1)S(1)}, u32[]{:S(2)}, u32[]{:S(2)}) collective-permute-start(bf16[256,576]{1,0:T(8,128)(2,1)} %copy-done.11), channel_id=1, source_target_pairs={{0,512},{512,0},{1,513},{513,1},{2,514},{514,2},{3,515},{515,3},{4... | collective-permute-start | bytes 884744 | tf_op jit(solution)/shard_map/ppermute | solution.py:177
  104.0 1.3 copy-start.8
  105.3 66.8 %copy-start.13 = (f32[8,576]{1,0:T(8,128)S(1)}, f32[8,576]{1,0:T(8,128)}, u32[]{:S(2)}) copy-start(f32[8,576]{1,0:T(8,128)} %param.10) | copy-start | bytes 55300
  105.3 66.8 %copy-start.14 = (f32[8,576]{1,0:T(8,128)S(1)}, f32[8,576]{1,0:T(8,128)}, u32[]{:S(2)}) copy-start(f32[8,576]{1,0:T(8,128)} %param.11) | copy-start | bytes 55300
  106.4 18.8 %collective-permute-start.6 = (bf16[11,8,576]{2,1,0:T(8,128)(2,1)S(1)}, bf16[11,8,576]{2,1,0:T(8,128)(2,1)S(1)}, u32[]{:S(2)}, u32[]{:S(2)}) collective-permute-start(bf16[11,8,576]{2,1,0:T(8,128)(2,1)S(1)} %get-tuple-element.38), channel_id=1, source_target_pairs={{0,496},{8,24},{16,0},{24,40},{32,16},{40,56},{48,32},{56,72},{64,... | collective-permute-start | bytes 304136 | tf_op jit(solution)/shard_map/ppermute | solution.py:201
  117.5 7.8 %collective-permute-start.5 = (bf16[10,8,576]{2,1,0:T(8,128)(2,1)S(1)}, bf16[10,8,576]{2,1,0:T(8,128)(2,1)S(1)}, u32[]{:S(2)}, u32[]{:S(2)}) collective-permute-start(bf16[10,8,576]{2,1,0:T(8,128)(2,1)S(1)} %get-tuple-element.37), channel_id=1, source_target_pairs={{0,16},{8,504},{16,32},{24,8},{32,48},{40,24},{48,64},{56,40},{64,... | collective-permute-start | bytes 276488 | tf_op jit(solution)/shard_map/ppermute | solution.py:200
  125.3 11.6 %collective-permute-start.8 = (bf16[4,8,576]{2,1,0:T(8,128)(2,1)S(1)}, bf16[4,8,576]{2,1,0:T(8,128)(2,1)S(1)}, u32[]{:S(2)}, u32[]{:S(2)}) collective-permute-start(bf16[4,8,576]{2,1,0:T(8,128)(2,1)S(1)} %get-tuple-element.41), channel_id=1, source_target_pairs={{0,464},{8,56},{16,480},{24,72},{32,496},{40,88},{48,0},{56,104},{... | collective-permute-start | bytes 110600 | tf_op jit(solution)/shard_map/ppermute | solution.py:209
  128.1 8.8 %collective-permute-start.7 = (bf16[3,8,576]{2,1,0:T(8,128)(2,1)S(1)}, bf16[3,8,576]{2,1,0:T(8,128)(2,1)S(1)}, u32[]{:S(2)}, u32[]{:S(2)}) collective-permute-start(bf16[3,8,576]{2,1,0:T(8,128)(2,1)S(1)} %get-tuple-element.40), channel_id=1, source_target_pairs={{0,48},{8,472},{16,64},{24,488},{32,80},{40,504},{48,96},{56,8},{6... | collective-permute-start | bytes 82952 | tf_op jit(solution)/shard_map/ppermute | solution.py:208
  133.0 31.8 %collective-permute-start.4 = (f32[1,576]{1,0:T(1,128)S(1)}, f32[1,576]{1,0:T(1,128)S(1)}, u32[]{:S(2)}, u32[]{:S(2)}) collective-permute-start(f32[1,576]{1,0:T(1,128)S(1)} %get-tuple-element.35), channel_id=1, source_target_pairs={{0,8},{8,0},{1,9},{9,1},{2,10},{10,2},{3,11},{11,3},{4,12},{12,4},... | collective-permute-start | bytes 6920 | tf_op jit(solution)/shard_map/ppermute | solution.py:220
  136.9 28.4 %collective-permute-start.9 = (bf16[1,8,576]{2,1,0:T(8,128)(2,1)S(1)}, bf16[1,8,576]{2,1,0:T(8,128)(2,1)S(1)}, u32[]{:S(2)}, u32[]{:S(2)}) collective-permute-start(bf16[1,8,576]{2,1,0:T(8,128)(2,1)S(1)} %get-tuple-element.43), channel_id=1, source_target_pairs={{0,288},{8,232},{16,304},{24,248},{32,320},{40,264},{48,336},{56,2... | collective-permute-start | bytes 27656 | tf_op jit(solution)/shard_map/ppermute | solution.py:217
  148.0 17.3 %collective-permute-start.10 = (bf16[1,8,576]{2,1,0:T(8,128)(2,1)S(1)}, bf16[1,8,576]{2,1,0:T(8,128)(2,1)S(1)}, u32[]{:S(2)}, u32[]{:S(2)}) collective-permute-start(bf16[1,8,576]{2,1,0:T(8,128)(2,1)S(1)} %get-tuple-element.44), channel_id=1, source_target_pairs={{0,144},{8,376},{16,160},{24,392},{32,176},{40,408},{48,192},{56,4... | collective-permute-start | bytes 27656 | tf_op jit(solution)/shard_map/ppermute | solution.py:218
  156.9 15.2 %collective-permute-start.11 = (bf16[1,8,576]{2,1,0:T(8,128)(2,1)S(1)}, bf16[1,8,576]{2,1,0:T(8,128)(2,1)S(1)}, u32[]{:S(2)}, u32[]{:S(2)}) collective-permute-start(bf16[1,8,576]{2,1,0:T(8,128)(2,1)S(1)} %get-tuple-element.45), channel_id=1, source_target_pairs={{0,368},{8,152},{16,384},{24,168},{32,400},{40,184},{48,416},{56,2... | collective-permute-start | bytes 27656 | tf_op jit(solution)/shard_map/ppermute | solution.py:219

commit v3 on v1

v3 whole, which is shorter than its diff:
```python
import jax
import jax.numpy as jnp
from jax import lax
from jax.experimental import pallas as pl
from jax.experimental.pallas import tpu as pltpu
from jax.sharding import Mesh, PartitionSpec as P

D = 4608
N_REP = 128
FEAT = 576

rms_eps = 1e-06
inner_rate = 0.3
outer_rate = 0.7
outer_beta = 0.9

FSDP = ("x", "yh")
REP = ("yl", "zh", "zl", "core")
SWAP = [(0, 1), (1, 0)]
f32 = jnp.float32
bf16 = jnp.bfloat16
S = jax.ShapeDtypeStruct
PARAMS = pltpu.CompilerParams(vmem_limit_bytes=24 * 2**20)


HBM = pl.BlockSpec(memory_space=pltpu.HBM)
CHEAP = pl.CostEstimate(flops=1000, bytes_accessed=1000, transcendentals=0)
ANY = pl.BlockSpec(memory_space=pl.ANY)
VMEM = pl.BlockSpec(memory_space=pltpu.VMEM)


def far(array):
    return pltpu.with_memory_space_constraint(array, pltpu.HBM)


def partner(bits):
    return [(i, i ^ bits) for i in range(8)]


def turned_columns(cot, turned):
    turned[...] = cot[...].astype(f32).T.reshape(2, 32, 2, 8, 128)


def send_out(buffer, out_ref, sems):
    copies = []
    for core in range(2):
        for peer in range(8):
            at = core * 8 + peer
            copies.append(pltpu.make_async_copy(buffer.at[core], out_ref.at[at], sems.at[at]))
            copies[-1].start()
    for copy in copies:
        copy.wait()


def pack_first_kernel(cot_hbm, tok_hbm, out_ref, cot, tok, turned, buffer, sems, in_sems):
    yl = lax.axis_index("yl")
    cot_copy = pltpu.make_async_copy(cot_hbm, cot, in_sems.at[0])
    tok_copy = pltpu.make_async_copy(tok_hbm, tok, in_sems.at[1])
    cot_copy.start()
    tok_copy.start()
    cot_copy.wait()
    turned_columns(cot, turned)
    block = turned[1 - yl]
    for core in range(2):
        buffer[core, 0:256] = block[:, core].reshape(256, 128).astype(bf16)
    tok_copy.wait()
    rows = []
    for j in range(8):
        part = tok[:, j * 128 : (j + 1) * 128].astype(f32)
        rows.append(jnp.sum(part * part, axis=0, keepdims=True))
    square = jnp.concatenate(rows, axis=0)
    high = square.astype(bf16).astype(f32)
    middle = (square - high).astype(bf16).astype(f32)
    low = square - high - middle
    tail = jnp.concatenate([high, middle, low, jnp.zeros_like(low)], axis=0).astype(bf16)
    for core in range(2):
        buffer[core, 256:288] = tail
    send_out(buffer, out_ref, sems)


def pack_second_kernel(cot, w_sib, out_ref, turned, buffer, sems):
    turned_columns(cot, turned)
    block = turned[lax.axis_index("yl")]
    for core in range(2):
        buffer[core] = block[:, core].reshape(256, 128).astype(bf16)
    send_out(buffer, out_ref, sems)


def weight_kernel(wt_ref, gain_ref, mine_ref, other_ref, turned):
    core = lax.axis_index("core")
    turned[...] = wt_ref[...].astype(f32).T.reshape(64, 2, 8, FEAT)
    gain = jnp.broadcast_to(gain_ref[...].astype(f32), (16, FEAT)).astype(bf16)
    for which, out in ((core, mine_ref), (1 - core, other_ref)):
        out[0:512] = turned[:, which].reshape(512, FEAT).astype(bf16)
        out[512:528] = gain


def product(got, hidden):
    cot = jnp.concatenate([got[g, 0:256] for g in range(8)], axis=1)
    return lax.dot_general(cot, hidden, (((1,), (1,)), ((), ())), preferred_element_type=f32)


def half_rows(which):
    return pl.ds(pl.multiple_of(which * 256, 256), 256)


def eight(which):
    return pl.ds(which * 8, 8)


def start_all(pairs, sems):
    copies = [pltpu.make_async_copy(src, dst, sems.at[i]) for i, (src, dst) in enumerate(pairs)]
    for copy in copies:
        copy.start()
    return copies


def first_kernel(
    got_hbm, tok_hbm, tok_sib_hbm, w_hbm, w_sib_hbm,
    send_ref, hid_hbm, hid_sib_hbm, part_ref, part_sib_ref,
    got, tok, weight, gains, hid, sems,
):
    core = lax.axis_index("core")
    yl = lax.axis_index("yl")
    copies = start_all(
        [
            (got_hbm.at[eight(core)], got.at[0]),
            (tok_hbm, tok.at[0]),
            (w_hbm.at[pl.ds(512, 16)], gains.at[0]),
            (w_hbm.at[half_rows(1 - yl)], weight.at[0]),
            (got_hbm.at[eight(1 - core)], got.at[1]),
            (tok_sib_hbm, tok.at[1]),
            (w_sib_hbm.at[pl.ds(512, 16)], gains.at[1]),
            (w_sib_hbm.at[half_rows(1 - yl)], weight.at[1]),
        ],
        sems,
    )
    new = jnp.zeros((256, FEAT), f32)
    out_copies = []
    for slot, (hid_out, part) in enumerate(((hid_hbm, part_ref), (hid_sib_hbm, part_sib_ref))):
        copies[slot * 4].wait()
        square = jnp.zeros((8, 128), f32)
        for g in range(8):
            tail = got[slot, g, 256:288].astype(f32)
            square += tail[0:8] + (tail[8:16] + tail[16:24])
        inv_rms = lax.rsqrt(square / D + rms_eps)
        copies[slot * 4 + 2].wait()
        gain = gains[slot].astype(f32)[0:8].T[:, 0:1]
        copies[slot * 4 + 1].wait()
        for j in range(8):
            at = slice(j * 128, (j + 1) * 128)
            normed = tok[slot, :, at].astype(f32) * inv_rms[j : j + 1]
            hid[slot, :, at] = (normed * gain).astype(bf16)
        out_copies.append(pltpu.make_async_copy(hid.at[slot], hid_out, sems.at[8 + slot]))
        out_copies[-1].start()
        grad = product(got.at[slot], hid[slot])
        copies[slot * 4 + 3].wait()
        w = weight[slot].astype(f32)
        part[...] = jnp.sum(w * grad, axis=0, keepdims=True)
        new += w - inner_rate * grad
    send_ref[...] = new.astype(bf16)
    for copy in out_copies:
        copy.wait()


def second_kernel(
    got_hbm, hid_hbm, hid_sib_hbm, w_hbm, w_sib_hbm, arrived_hbm, part_ref, part_sib_ref,
    out_ref, gain_ref, gain_sib_ref,
    got, hid, weight, arrived, sems,
):
    core = lax.axis_index("core")
    yl = lax.axis_index("yl")
    copies = start_all(
        [
            (hid_hbm, hid.at[0]),
            (got_hbm.at[eight(core)], got.at[0]),
            (w_hbm.at[half_rows(yl)], weight.at[0]),
            (hid_sib_hbm, hid.at[1]),
            (got_hbm.at[eight(1 - core)], got.at[1]),
            (w_sib_hbm.at[half_rows(yl)], weight.at[1]),
            (arrived_hbm, arrived),
        ],
        sems,
    )
    new = jnp.zeros((256, FEAT), f32)
    for slot, (part, out) in enumerate(((part_ref, gain_ref), (part_sib_ref, gain_sib_ref))):
        copies[slot * 3].wait()
        copies[slot * 3 + 1].wait()
        grad = product(got.at[slot], hid[slot])
        copies[slot * 3 + 2].wait()
        w = weight[slot].astype(f32)
        out[...] = part[...] + jnp.sum(w * grad, axis=0, keepdims=True)
        new += w - inner_rate * grad
    copies[6].wait()
    total = (new + arrived[...].astype(f32)).reshape(8, 4, 8, FEAT)
    for zl in range(4):
        out_ref[zl] = total[:, zl].reshape(64, FEAT).astype(bf16)


def keys_kernel(hid_ref, wt_ref, after_ref, *outs):
    me = lax.axis_index("x") * 2 + lax.axis_index("yh")
    for bit, out in enumerate(outs):
        group = me ^ bit
        hid = hid_ref[:, pl.ds(pl.multiple_of(group * 128, 128), 128)]
        out[...] = lax.dot_general(
            hid, wt_ref[...], (((0,), (0,)), ((), ())), preferred_element_type=f32
        ).astype(bf16)


def per_device(tokens, norm_gain, key_weight, key_cotangent, global_fragment, outer_momentum):
    tok = tokens.T
    weight_t = key_weight[0].T
    first = pl.pallas_call(
        pack_first_kernel,
        out_shape=pltpu.HBM((16, 288, 128), bf16),
        in_specs=[HBM, HBM],
        out_specs=HBM,
        scratch_shapes=[
            pltpu.VMEM((128, 1024), bf16),
            pltpu.VMEM((FEAT, 1024), bf16),
            pltpu.VMEM((2, 32, 2, 8, 128), f32),
            pltpu.VMEM((2, 288, 128), bf16),
            pltpu.SemaphoreType.DMA((16,)),
            pltpu.SemaphoreType.DMA((2,)),
        ],
        compiler_params=PARAMS,
        name="pack_first",
    )(far(key_cotangent), far(tok))
    got_first = lax.all_to_all(first, ("core",) + FSDP, 0, 0)

    tok_sib = lax.ppermute(tok, "core", SWAP)
    w_mine, w_other = pl.pallas_call(
        weight_kernel,
        out_shape=(S((528, FEAT), bf16), S((528, FEAT), bf16)),
        scratch_shapes=[pltpu.VMEM((64, 2, 8, FEAT), f32)],
        compiler_params=PARAMS,
        cost_estimate=CHEAP,
        name="weights",
    )(weight_t, norm_gain)
    w_sib = lax.ppermute(w_other, "core", SWAP)
    second = pl.pallas_call(
        pack_second_kernel,
        out_shape=pltpu.HBM((16, 256, 128), bf16),
        in_specs=[VMEM, ANY],
        out_specs=HBM,
        scratch_shapes=[
            pltpu.VMEM((2, 32, 2, 8, 128), f32),
            pltpu.VMEM((2, 256, 128), bf16),
            pltpu.SemaphoreType.DMA((16,)),
        ],
        compiler_params=PARAMS,
        cost_estimate=CHEAP,
        name="pack_second",
    )(key_cotangent, w_sib)

    send, hid, hid_sib, part, part_sib = pl.pallas_call(
        first_kernel,
        out_shape=(
            S((256, FEAT), bf16), pltpu.HBM((FEAT, 1024), bf16), pltpu.HBM((FEAT, 1024), bf16),
            S((1, FEAT), f32), S((1, FEAT), f32),
        ),
        in_specs=[HBM] * 5,
        out_specs=(VMEM, HBM, HBM, VMEM, VMEM),
        scratch_shapes=[
            pltpu.VMEM((2, 8, 288, 128), bf16),
            pltpu.VMEM((2, FEAT, 1024), bf16),
            pltpu.VMEM((2, 256, FEAT), bf16),
            pltpu.VMEM((2, 16, FEAT), bf16),
            pltpu.VMEM((2, FEAT, 1024), bf16),
            pltpu.SemaphoreType.DMA((10,)),
        ],
        compiler_params=PARAMS,
        name="first",
    )(far(got_first), far(tok), far(tok_sib), far(w_mine), far(w_sib))
    arrived = lax.ppermute(send, "yl", SWAP)
    got_second = lax.all_to_all(second, ("core",) + FSDP, 0, 0)

    payload, part, part_sib = pl.pallas_call(
        second_kernel,
        out_shape=(S((4, 64, FEAT), bf16), S((1, FEAT), f32), S((1, FEAT), f32)),
        in_specs=[HBM] * 6 + [VMEM] * 2,
        scratch_shapes=[
            pltpu.VMEM((2, 8, 256, 128), bf16),
            pltpu.VMEM((2, FEAT, 1024), bf16),
            pltpu.VMEM((2, 256, FEAT), bf16),
            pltpu.VMEM((256, FEAT), bf16),
            pltpu.SemaphoreType.DMA((7,)),
        ],
        compiler_params=PARAMS,
        name="second",
    )(
        far(got_second), far(hid), far(hid_sib), far(w_mine), far(w_sib), far(arrived), part, part_sib
    )

    keys = pl.pallas_call(
        keys_kernel,
        out_shape=tuple(S((128, 1024), bf16) for _ in range(8)),
        in_specs=[VMEM, VMEM, ANY],
        compiler_params=PARAMS,
        name="keys",
    )(hid, weight_t, payload)
    pieces = [lax.ppermute(keys[bit], FSDP, partner(bit)) for bit in range(1, 8)]
    z_parts = lax.all_to_all(payload, "zl", 0, 0)
    z_sum = jnp.sum(z_parts.astype(f32), axis=0).astype(bf16).reshape(8, 8, FEAT)
    z_parts = lax.all_to_all(z_sum, "zh", 0, 0)
    summed = jnp.sum(z_parts.astype(f32), axis=0)

    gain_grad = part + lax.ppermute(part_sib, "core", SWAP)
    gain_grad = gain_grad / norm_gain.astype(f32)
    avg_grad = global_fragment - summed / N_REP
    new_momentum = outer_beta * outer_momentum + avg_grad
    new_global = global_fragment - outer_rate * (avg_grad + outer_beta * new_momentum)
    key_out = keys[0].astype(f32)
    for piece in pieces:
        key_out += piece.astype(f32)
    return (key_out.astype(bf16), gain_grad, new_global, new_momentum)


def solution(mesh):
    fine = Mesh(mesh.devices.reshape(2, 8, 4, 2, 4, 2), REP + FSDP)
    return jax.shard_map(
        per_device,
        mesh=fine,
        in_specs=(
            P(REP, FSDP),
            P(REP, FSDP),
            P(REP, None, FSDP),
            P(REP + FSDP, None),
            P(REP, FSDP),
            P(REP, FSDP),
        ),
        out_specs=(P(REP + FSDP, None), P(REP, FSDP), P(REP, FSDP), P(REP, FSDP)),
        check_vma=False,
    )
```

time: 179 us -> 158 us (0.88)
  the two profiles are of different devices: /device:TPU:1 before, /device:TPU:16 now
where the time goes in v3:
time: 158 us; the launch traced here: 157 us
  starting transfers between devices  83.9 us (53%)
  waiting for transfers between devices  52.1 us (33%)
  Pallas kernels  15.8 us (10%)
  other arithmetic  2.97 us (2%)
  local copies, waits for them, and re-layouts  1.6 us (1%)
    ppermute x7, starting transfers between devices, per_device(): lax.ppermute(keys[bit], FSDP, partner(bit))  27.5 us
    all_to_all x1, waiting for transfers between devices, per_device(): z_parts = lax.all_to_all(z_sum, 'zh', 0, 0)  25.4 us
    all_to_all x1, starting transfers between devices, per_device(): z_parts = lax.all_to_all(z_sum, 'zh', 0, 0)  20.5 us
    all_to_all x1, starting transfers between devices, per_device(): got_first = lax.all_to_all(first, ('core',) + FSDP, 0, 0)  17.2 us
    ppermute x1, waiting for transfers between devices, per_device(): arrived = lax.ppermute(send, 'yl', SWAP)  15.7 us
    all_to_all x1, waiting for transfers between devices, per_device(): got_first = lax.all_to_all(first, ('core',) + FSDP, 0, 0)  11 us
    all_to_all x1, starting transfers between devices, per_device(): got_second = lax.all_to_all(second, ('core',) + FSDP, 0, 0)  7.04 us
    pallas_call x1, Pallas kernels, per_device(): pl.pallas_call(second_kernel, out_shape=(S((4, 64, FEAT), bf16), S((1, FE...  4.3 us
  transfers between devices with their start and end apart: 15, of which 3 were waited for; matrix products, arithmetic and copies ran while one was open for 1% of the time, Pallas kernels for 6%

profile of v3, /device:TPU:16, one launch (start us, length us, event | category | flops | bytes accessed | tf_op | source)
XLA Modules:
  0.0 157.4 jit_solution(10515323291608894068)
XLA Ops:
  0.6 2.9 %pack_first.1 = bf16[16,288,128]{2,1,0:T(8,128)(2,1)} custom-call(bf16[128,1024]{1,0:T(8,128)(2,1)} %cot.1, bf16[576,1024]{1,0:T(8,128)(2,1)} %bitcast.7), custom_call_target="tpu_custom_call" | custom-call | tf_op jit(solution)/shard_map/pack_first/pallas_call | solution.py:213
  3.5 0.0 copy-start.1
  3.5 0.0 copy-start.5
  3.5 0.0 copy-start.6
  3.5 17.2 %all-to-all-start = ((bf16[16,288,128]{2,1,0:T(8,128)(2,1)}), bf16[16,288,128]{2,1,0:T(8,128)(2,1)}, u32[]{:S(2)}, u32[]{:S(2)}) async-start(bf16[16,288,128]{2,1,0:T(8,128)(2,1)} %pack_first.1), calls=%async_computation | async-start | bytes 2359296 | tf_op jit(solution)/shard_map/all_to_all | solution.py:229
  20.8 0.0 copy-start.4
  20.8 0.0 copy-done.1
  20.8 0.0 copy-done.5
  20.8 0.7 weights.1
  21.5 0.0 copy-start.3
  21.5 0.8 copy-done.3
  22.3 2.1 %collective-permute-start.1 = (bf16[528,576]{1,0:T(8,128)(2,1)S(1)}, bf16[528,576]{1,0:T(8,128)(2,1)S(1)}, u32[]{:S(2)}, u32[]{:S(2)}) collective-permute-start(bf16[528,576]{1,0:T(8,128)(2,1)S(1)} %get-tuple-element.23), channel_id=1, source_target_pairs={{0,8},{8,0},{1,9},{9,1},{2,10},{10,2},{3,11},{11,3},{4,12},{12,4},... | collective-permute-start | bytes 1824776 | tf_op jit(solution)/shard_map/ppermute | solution.py:240
  24.4 0.0 copy-done.6
  24.4 2.3 %collective-permute-start = (bf16[576,1024]{1,0:T(8,128)(2,1)S(1)}, bf16[576,1024]{1,0:T(8,128)(2,1)}, u32[]{:S(2)}, u32[]{:S(2)}) collective-permute-start(bf16[576,1024]{1,0:T(8,128)(2,1)S(1)} %bitcast.9), channel_id=1, source_target_pairs={{0,8},{8,0},{1,9},{9,1},{2,10},{10,2},{3,11},{11,3},{4,12},{12,4},... | collective-permute-start | bytes 3538952 | tf_op jit(solution)/shard_map/ppermute | solution.py:231
  26.7 0.0 collective-permute-done.1.w_sib_hbm.w_sib
  26.7 0.0 copy-done.4
  26.7 0.0 copy-start
  26.7 1.3 pack_second.1
  28.1 11.0 %all-to-all-done.got_hbm = bf16[16,288,128]{2,1,0:T(8,128)(2,1)} async-done(((bf16[16,288,128]{2,1,0:T(8,128)(2,1)}), bf16[16,288,128]{2,1,0:T(8,128)(2,1)}, u32[]{:S(2)}, u32[]{:S(2)}) %all-to-all-start) | async-done | bytes 1179680 | tf_op jit(solution)/shard_map/all_to_all | solution.py:229
  39.0 0.0 copy-done
  39.0 7.0 %all-to-all-start.1 = ((bf16[16,256,128]{2,1,0:T(8,128)(2,1)}), bf16[16,256,128]{2,1,0:T(8,128)(2,1)}, u32[]{:S(2)}, u32[]{:S(2)}) async-start(bf16[16,256,128]{2,1,0:T(8,128)(2,1)} %pack_second.1), calls=%async_computation.1 | async-start | bytes 2097152 | tf_op jit(solution)/shard_map/all_to_all | solution.py:276
  46.1 0.0 collective-permute-done.tok_sib_hbm
  46.1 4.3 %first.1 = (bf16[256,576]{1,0:T(8,128)(2,1)S(1)}, bf16[576,1024]{1,0:T(8,128)(2,1)}, bf16[576,1024]{1,0:T(8,128)(2,1)}, f32[1,576]{1,0:T(1,128)S(1)}, f32[1,576]{1,0:T(1,128)S(1)}) custom-call(bf16[16,288,128]{2,1,0:T(8,128)(2,1)} %all-to-all-done.got_hbm, bf16[576,1024]{1,0:T(8,128)(2,1)} %bitcast.8, bf16[576,1024]{1,0:T(8,128)(2,1)} %collective-permute-done.tok_sib_hbm, ...), custom_call_target="tpu_custom_call" | custom-call | tf_op jit(solution)/shard_map/first/pallas_call | solution.py:256
  50.4 1.9 %collective-permute-start.2 = (bf16[256,576]{1,0:T(8,128)(2,1)S(1)}, bf16[256,576]{1,0:T(8,128)(2,1)S(1)}, u32[]{:S(2)}, u32[]{:S(2)}) collective-permute-start(bf16[256,576]{1,0:T(8,128)(2,1)S(1)} %get-tuple-element.26), channel_id=1, source_target_pairs={{0,512},{512,0},{1,513},{513,1},{2,514},{514,2},{3,515},{515,3},{4... | collective-permute-start | bytes 884744 | tf_op jit(solution)/shard_map/ppermute | solution.py:275
  52.3 15.7 %collective-permute-done.2.arrived_hbm = bf16[256,576]{1,0:T(8,128)(2,1)S(1)} collective-permute-done((bf16[256,576]{1,0:T(8,128)(2,1)S(1)}, bf16[256,576]{1,0:T(8,128)(2,1)S(1)}, u32[]{:S(2)}, u32[]{:S(2)}) %collective-permute-start.2) | collective-permute-done | bytes 294944 | tf_op jit(solution)/shard_map/ppermute | solution.py:275
  68.0 0.0 copy-start.7
  68.0 0.0 all-to-all-done.1.got_hbm
  68.0 0.7 copy-done.7
  68.7 0.0 copy-start.2
  68.7 4.3 %second.1 = (bf16[4,64,576]{2,1,0:T(8,128)(2,1)}, f32[1,576]{1,0:T(1,128)S(1)}, f32[1,576]{1,0:T(1,128)S(1)}) custom-call(bf16[16,256,128]{2,1,0:T(8,128)(2,1)} %all-to-all-done.1.got_hbm, bf16[576,1024]{1,0:T(8,128)(2,1)} %get-tuple-element.24.hid_hbm.hid_ref, bf16[576,1024]{1,0:T(8,128)(2,1)} %get-tuple-element.25.hid_sib_hbm, bf16[528,576]{1,0:T(8,128)(2,1)} %copy-done.3, ...), custom_call_target="tpu_custom_call" | custom-call | tf_op jit(solution)/shard_map/second/pallas_call | solution.py:278
  73.0 3.5 %all-to-all-start.2 = ((bf16[4,64,576]{2,1,0:T(8,128)(2,1)}), bf16[4,64,576]{2,1,0:T(8,128)(2,1)S(1)}, u32[]{:S(2)}, u32[]{:S(2)}) async-start(bf16[4,64,576]{2,1,0:T(8,128)(2,1)} %get-tuple-element.29.after_ref), calls=%async_computation.2 | async-start | bytes 655360 | tf_op jit(solution)/shard_map/all_to_all | solution.py:303
  76.5 0.0 copy-done.2
  76.5 2.3 %keys.1 = (bf16[128,1024]{1,0:T(8,128)(2,1)S(1)}, bf16[128,1024]{1,0:T(8,128)(2,1)S(1)}, bf16[128,1024]{1,0:T(8,128)(2,1)S(1)}, bf16[128,1024]{1,0:T(8,128)(2,1)...) custom-call(bf16[576,1024]{1,0:T(8,128)(2,1)S(1)} %copy-done.2, ...), custom_call_target="tpu_custom_call" | custom-call | tf_op jit(solution)/shard_map/keys/pallas_call | solution.py:295
  78.9 2.3 %collective-permute-start.3 = (bf16[128,1024]{1,0:T(8,128)(2,1)S(1)}, bf16[128,1024]{1,0:T(8,128)(2,1)S(1)}, u32[]{:S(2)}, u32[]{:S(2)}) collective-permute-start(bf16[128,1024]{1,0:T(8,128)(2,1)S(1)} %get-tuple-element.31), channel_id=1, source_target_pairs={{0,1},{1,0},{2,3},{3,2},{4,5},{5,4},{6,7},{7,6},{8,9},{9,8},{10,11... | collective-permute-start | bytes 786440 | tf_op jit(solution)/shard_map/ppermute | solution.py:302
  81.1 2.4 %collective-permute-start.4 = (bf16[128,1024]{1,0:T(8,128)(2,1)S(1)}, bf16[128,1024]{1,0:T(8,128)(2,1)S(1)}, u32[]{:S(2)}, u32[]{:S(2)}) collective-permute-start(bf16[128,1024]{1,0:T(8,128)(2,1)S(1)} %get-tuple-element.32), channel_id=1, source_target_pairs={{0,2},{1,3},{2,0},{3,1},{4,6},{5,7},{6,4},{7,5},{8,10},{9,11},{10,... | collective-permute-start | bytes 786440 | tf_op jit(solution)/shard_map/ppermute | solution.py:302
  83.6 1.9 %collective-permute-start.10 = (f32[1,576]{1,0:T(1,128)S(1)}, f32[1,576]{1,0:T(1,128)S(1)}, u32[]{:S(2)}, u32[]{:S(2)}) collective-permute-start(f32[1,576]{1,0:T(1,128)S(1)} %get-tuple-element.39), channel_id=1, source_target_pairs={{0,8},{8,0},{1,9},{9,1},{2,10},{10,2},{3,11},{11,3},{4,12},{12,4},... | collective-permute-start | bytes 6920 | tf_op jit(solution)/shard_map/ppermute | solution.py:308
  85.5 6.0 %collective-permute-start.5 = (bf16[128,1024]{1,0:T(8,128)(2,1)}, bf16[128,1024]{1,0:T(8,128)(2,1)S(1)}, u32[]{:S(2)}, u32[]{:S(2)}) collective-permute-start(bf16[128,1024]{1,0:T(8,128)(2,1)} %get-tuple-element.33), channel_id=1, source_target_pairs={{0,3},{1,2},{2,1},{3,0},{4,7},{5,6},{6,5},{7,4},{8,11},{9,10},{10,... | collective-permute-start | bytes 786440 | tf_op jit(solution)/shard_map/ppermute | solution.py:302
  91.5 3.4 %collective-permute-start.6 = (bf16[128,1024]{1,0:T(8,128)(2,1)}, bf16[128,1024]{1,0:T(8,128)(2,1)S(1)}, u32[]{:S(2)}, u32[]{:S(2)}) collective-permute-start(bf16[128,1024]{1,0:T(8,128)(2,1)} %get-tuple-element.34), channel_id=1, source_target_pairs={{0,4},{1,5},{2,6},{3,7},{4,0},{5,1},{6,2},{7,3},{8,12},{9,13},{10,... | collective-permute-start | bytes 786440 | tf_op jit(solution)/shard_map/ppermute | solution.py:302
  94.9 0.0 collective-permute-done.10
  94.9 3.8 %collective-permute-start.7 = (bf16[128,1024]{1,0:T(8,128)(2,1)}, bf16[128,1024]{1,0:T(8,128)(2,1)S(1)}, u32[]{:S(2)}, u32[]{:S(2)}) collective-permute-start(bf16[128,1024]{1,0:T(8,128)(2,1)} %get-tuple-element.35), channel_id=1, source_target_pairs={{0,5},{1,4},{2,7},{3,6},{4,1},{5,0},{6,3},{7,2},{8,13},{9,12},{10,... | collective-permute-start | bytes 786440 | tf_op jit(solution)/shard_map/ppermute | solution.py:302
  98.7 0.0 collective-permute-done.3
  98.7 3.6 %collective-permute-start.8 = (bf16[128,1024]{1,0:T(8,128)(2,1)S(1)}, bf16[128,1024]{1,0:T(8,128)(2,1)S(1)}, u32[]{:S(2)}, u32[]{:S(2)}) collective-permute-start(bf16[128,1024]{1,0:T(8,128)(2,1)S(1)} %get-tuple-element.36), channel_id=1, source_target_pairs={{0,6},{1,7},{2,4},{3,5},{4,2},{5,3},{6,0},{7,1},{8,14},{9,15},{10,... | collective-permute-start | bytes 786440 | tf_op jit(solution)/shard_map/ppermute | solution.py:302
  102.3 0.0 collective-permute-done.4
  102.3 6.1 %collective-permute-start.9 = (bf16[128,1024]{1,0:T(8,128)(2,1)S(1)}, bf16[128,1024]{1,0:T(8,128)(2,1)S(1)}, u32[]{:S(2)}, u32[]{:S(2)}) collective-permute-start(bf16[128,1024]{1,0:T(8,128)(2,1)S(1)} %get-tuple-element.37), channel_id=1, source_target_pairs={{0,7},{1,6},{2,5},{3,4},{4,3},{5,2},{6,1},{7,0},{8,15},{9,14},{10,... | collective-permute-start | bytes 786440 | tf_op jit(solution)/shard_map/ppermute | solution.py:302
  108.4 0.0 all-to-all-done.2
  108.4 0.7 reduce_sum.21
  109.1 20.5 %all-to-all-start.3 = ((bf16[8,8,576]{2,1,0:T(8,128)(2,1)}), bf16[8,8,576]{2,1,0:T(8,128)(2,1)S(1)}, u32[]{:S(2)}, u32[]{:S(2)}) async-start(bf16[8,8,576]{2,1,0:T(8,128)(2,1)} %bitcast.3), calls=%async_computation.3 | async-start | bytes 163840 | tf_op jit(solution)/shard_map/all_to_all | solution.py:305
  129.6 0.6 convert_divide_fusion
  130.2 0.0 collective-permute-done.5
  130.2 0.0 collective-permute-done.6
  130.2 0.0 collective-permute-done.7
  130.2 0.0 collective-permute-done.8
  130.2 0.0 collective-permute-done.9
  130.2 0.0 copy-start.8
  130.2 0.0 copy-start.9
  130.3 1.1 add_convert_fusion
  131.3 25.4 %all-to-all-done.3 = bf16[8,8,576]{2,1,0:T(8,128)(2,1)S(1)} async-done(((bf16[8,8,576]{2,1,0:T(8,128)(2,1)}), bf16[8,8,576]{2,1,0:T(8,128)(2,1)S(1)}, u32[]{:S(2)}, u32[]{:S(2)}) %all-to-all-start.3) | async-done | bytes 73760 | tf_op jit(solution)/shard_map/all_to_all | solution.py:305
  156.8 0.0 copy-done.8
  156.8 0.0 copy-done.9
  156.8 0.6 multiply_subtract_fusion
  (1 shorter events, 0.0 us)
Async XLA Ops:
  3.5 17.3 %copy-start.1 = (bf16[1,1024,576]{1,2,0:T(8,128)(2,1)S(1)}, bf16[1,1024,576]{1,2,0:T(8,128)(2,1)}, u32[]{:S(2)}) copy-start(bf16[1,1024,576]{1,2,0:T(8,128)(2,1)} %param.8) | copy-start | bytes 3538948
  3.5 17.3 %copy-start.5 = (bf16[1,576]{1,0:T(2,128)(2,1)S(1)}, bf16[1,576]{1,0:T(2,128)(2,1)}, u32[]{:S(2)}) copy-start(bf16[1,576]{1,0:T(2,128)(2,1)} %gain_ref.1) | copy-start | bytes 3460
  3.5 20.9 %copy-start.6 = (bf16[1024,576]{0,1:T(8,128)(2,1)S(1)}, bf16[1024,576]{0,1:T(8,128)(2,1)}, u32[]{:S(2)}) copy-start(bf16[1024,576]{0,1:T(8,128)(2,1)} %param.6) | copy-start | bytes 3538948
  3.5 35.5 %all-to-all-start = ((bf16[16,288,128]{2,1,0:T(8,128)(2,1)}), bf16[16,288,128]{2,1,0:T(8,128)(2,1)}, u32[]{:S(2)}, u32[]{:S(2)}) async-start(bf16[16,288,128]{2,1,0:T(8,128)(2,1)} %pack_first.1), calls=%async_computation | async-start | bytes 2359296 | tf_op jit(solution)/shard_map/all_to_all | solution.py:229
  20.8 5.9 %copy-start.4 = (bf16[128,1024]{1,0:T(8,128)(2,1)S(1)}, bf16[128,1024]{1,0:T(8,128)(2,1)}, u32[]{:S(2)}) copy-start(bf16[128,1024]{1,0:T(8,128)(2,1)} %cot.1) | copy-start | bytes 786436
  21.5 0.8 copy-start.3
  22.3 4.3 %collective-permute-start.1 = (bf16[528,576]{1,0:T(8,128)(2,1)S(1)}, bf16[528,576]{1,0:T(8,128)(2,1)S(1)}, u32[]{:S(2)}, u32[]{:S(2)}) collective-permute-start(bf16[528,576]{1,0:T(8,128)(2,1)S(1)} %get-tuple-element.23), channel_id=1, source_target_pairs={{0,8},{8,0},{1,9},{9,1},{2,10},{10,2},{3,11},{11,3},{4,12},{12,4},... | collective-permute-start | bytes 1824776 | tf_op jit(solution)/shard_map/ppermute | solution.py:240
  24.4 21.6 %collective-permute-start = (bf16[576,1024]{1,0:T(8,128)(2,1)S(1)}, bf16[576,1024]{1,0:T(8,128)(2,1)}, u32[]{:S(2)}, u32[]{:S(2)}) collective-permute-start(bf16[576,1024]{1,0:T(8,128)(2,1)S(1)} %bitcast.9), channel_id=1, source_target_pairs={{0,8},{8,0},{1,9},{9,1},{2,10},{10,2},{3,11},{11,3},{4,12},{12,4},... | collective-permute-start | bytes 3538952 | tf_op jit(solution)/shard_map/ppermute | solution.py:231
  26.7 12.3 %copy-start = (bf16[528,576]{1,0:T(8,128)(2,1)}, bf16[528,576]{1,0:T(8,128)(2,1)S(1)}, u32[]{:S(2)}) copy-start(bf16[528,576]{1,0:T(8,128)(2,1)S(1)} %collective-permute-done.1.w_sib_hbm.w_sib) | copy-start | bytes 1824772
  39.0 29.0 %all-to-all-start.1 = ((bf16[16,256,128]{2,1,0:T(8,128)(2,1)}), bf16[16,256,128]{2,1,0:T(8,128)(2,1)}, u32[]{:S(2)}, u32[]{:S(2)}) async-start(bf16[16,256,128]{2,1,0:T(8,128)(2,1)} %pack_second.1), calls=%async_computation.1 | async-start | bytes 2097152 | tf_op jit(solution)/shard_map/all_to_all | solution.py:276
  50.4 17.6 %collective-permute-start.2 = (bf16[256,576]{1,0:T(8,128)(2,1)S(1)}, bf16[256,576]{1,0:T(8,128)(2,1)S(1)}, u32[]{:S(2)}, u32[]{:S(2)}) collective-permute-start(bf16[256,576]{1,0:T(8,128)(2,1)S(1)} %get-tuple-element.26), channel_id=1, source_target_pairs={{0,512},{512,0},{1,513},{513,1},{2,514},{514,2},{3,515},{515,3},{4... | collective-permute-start | bytes 884744 | tf_op jit(solution)/shard_map/ppermute | solution.py:275
  68.0 0.7 copy-start.7
  68.7 7.8 %copy-start.2 = (bf16[576,1024]{1,0:T(8,128)(2,1)S(1)}, bf16[576,1024]{1,0:T(8,128)(2,1)}, u32[]{:S(2)}) copy-start(bf16[576,1024]{1,0:T(8,128)(2,1)} %get-tuple-element.24.hid_hbm.hid_ref) | copy-start | bytes 3538948
  73.0 35.3 %all-to-all-start.2 = ((bf16[4,64,576]{2,1,0:T(8,128)(2,1)}), bf16[4,64,576]{2,1,0:T(8,128)(2,1)S(1)}, u32[]{:S(2)}, u32[]{:S(2)}) async-start(bf16[4,64,576]{2,1,0:T(8,128)(2,1)} %get-tuple-element.29.after_ref), calls=%async_computation.2 | async-start | bytes 655360 | tf_op jit(solution)/shard_map/all_to_all | solution.py:303
  78.9 19.9 %collective-permute-start.3 = (bf16[128,1024]{1,0:T(8,128)(2,1)S(1)}, bf16[128,1024]{1,0:T(8,128)(2,1)S(1)}, u32[]{:S(2)}, u32[]{:S(2)}) collective-permute-start(bf16[128,1024]{1,0:T(8,128)(2,1)S(1)} %get-tuple-element.31), channel_id=1, source_target_pairs={{0,1},{1,0},{2,3},{3,2},{4,5},{5,4},{6,7},{7,6},{8,9},{9,8},{10,11... | collective-permute-start | bytes 786440 | tf_op jit(solution)/shard_map/ppermute | solution.py:302
  81.1 21.2 %collective-permute-start.4 = (bf16[128,1024]{1,0:T(8,128)(2,1)S(1)}, bf16[128,1024]{1,0:T(8,128)(2,1)S(1)}, u32[]{:S(2)}, u32[]{:S(2)}) collective-permute-start(bf16[128,1024]{1,0:T(8,128)(2,1)S(1)} %get-tuple-element.32), channel_id=1, source_target_pairs={{0,2},{1,3},{2,0},{3,1},{4,6},{5,7},{6,4},{7,5},{8,10},{9,11},{10,... | collective-permute-start | bytes 786440 | tf_op jit(solution)/shard_map/ppermute | solution.py:302
  83.6 11.3 %collective-permute-start.10 = (f32[1,576]{1,0:T(1,128)S(1)}, f32[1,576]{1,0:T(1,128)S(1)}, u32[]{:S(2)}, u32[]{:S(2)}) collective-permute-start(f32[1,576]{1,0:T(1,128)S(1)} %get-tuple-element.39), channel_id=1, source_target_pairs={{0,8},{8,0},{1,9},{9,1},{2,10},{10,2},{3,11},{11,3},{4,12},{12,4},... | collective-permute-start | bytes 6920 | tf_op jit(solution)/shard_map/ppermute | solution.py:308
  85.5 44.7 %collective-permute-start.5 = (bf16[128,1024]{1,0:T(8,128)(2,1)}, bf16[128,1024]{1,0:T(8,128)(2,1)S(1)}, u32[]{:S(2)}, u32[]{:S(2)}) collective-permute-start(bf16[128,1024]{1,0:T(8,128)(2,1)} %get-tuple-element.33), channel_id=1, source_target_pairs={{0,3},{1,2},{2,1},{3,0},{4,7},{5,6},{6,5},{7,4},{8,11},{9,10},{10,... | collective-permute-start | bytes 786440 | tf_op jit(solution)/shard_map/ppermute | solution.py:302
  91.5 38.7 %collective-permute-start.6 = (bf16[128,1024]{1,0:T(8,128)(2,1)}, bf16[128,1024]{1,0:T(8,128)(2,1)S(1)}, u32[]{:S(2)}, u32[]{:S(2)}) collective-permute-start(bf16[128,1024]{1,0:T(8,128)(2,1)} %get-tuple-element.34), channel_id=1, source_target_pairs={{0,4},{1,5},{2,6},{3,7},{4,0},{5,1},{6,2},{7,3},{8,12},{9,13},{10,... | collective-permute-start | bytes 786440 | tf_op jit(solution)/shard_map/ppermute | solution.py:302
  94.9 35.3 %collective-permute-start.7 = (bf16[128,1024]{1,0:T(8,128)(2,1)}, bf16[128,1024]{1,0:T(8,128)(2,1)S(1)}, u32[]{:S(2)}, u32[]{:S(2)}) collective-permute-start(bf16[128,1024]{1,0:T(8,128)(2,1)} %get-tuple-element.35), channel_id=1, source_target_pairs={{0,5},{1,4},{2,7},{3,6},{4,1},{5,0},{6,3},{7,2},{8,13},{9,12},{10,... | collective-permute-start | bytes 786440 | tf_op jit(solution)/shard_map/ppermute | solution.py:302
  98.7 31.5 %collective-permute-start.8 = (bf16[128,1024]{1,0:T(8,128)(2,1)S(1)}, bf16[128,1024]{1,0:T(8,128)(2,1)S(1)}, u32[]{:S(2)}, u32[]{:S(2)}) collective-permute-start(bf16[128,1024]{1,0:T(8,128)(2,1)S(1)} %get-tuple-element.36), channel_id=1, source_target_pairs={{0,6},{1,7},{2,4},{3,5},{4,2},{5,3},{6,0},{7,1},{8,14},{9,15},{10,... | collective-permute-start | bytes 786440 | tf_op jit(solution)/shard_map/ppermute | solution.py:302
  102.3 27.9 %collective-permute-start.9 = (bf16[128,1024]{1,0:T(8,128)(2,1)S(1)}, bf16[128,1024]{1,0:T(8,128)(2,1)S(1)}, u32[]{:S(2)}, u32[]{:S(2)}) collective-permute-start(bf16[128,1024]{1,0:T(8,128)(2,1)S(1)} %get-tuple-element.37), channel_id=1, source_target_pairs={{0,7},{1,6},{2,5},{3,4},{4,3},{5,2},{6,1},{7,0},{8,15},{9,14},{10,... | collective-permute-start | bytes 786440 | tf_op jit(solution)/shard_map/ppermute | solution.py:302
  109.1 47.7 %all-to-all-start.3 = ((bf16[8,8,576]{2,1,0:T(8,128)(2,1)}), bf16[8,8,576]{2,1,0:T(8,128)(2,1)S(1)}, u32[]{:S(2)}, u32[]{:S(2)}) async-start(bf16[8,8,576]{2,1,0:T(8,128)(2,1)} %bitcast.3), calls=%async_computation.3 | async-start | bytes 163840 | tf_op jit(solution)/shard_map/all_to_all | solution.py:305
  130.2 26.5 %copy-start.8 = (f32[8,576]{1,0:T(8,128)S(1)}, f32[8,576]{1,0:T(8,128)}, u32[]{:S(2)}) copy-start(f32[8,576]{1,0:T(8,128)} %param.10) | copy-start | bytes 55300
  130.2 26.5 %copy-start.9 = (f32[8,576]{1,0:T(8,128)S(1)}, f32[8,576]{1,0:T(8,128)}, u32[]{:S(2)}) copy-start(f32[8,576]{1,0:T(8,128)} %param.11) | copy-start | bytes 55300

commit v4 on v3

v4 whole, which is shorter than its diff:
```python
import jax
import jax.numpy as jnp
from jax import lax
from jax.experimental import pallas as pl
from jax.experimental.pallas import tpu as pltpu
from jax.sharding import Mesh, PartitionSpec as P

D = 4608
N_REP = 128
FEAT = 576

rms_eps = 1e-06
inner_rate = 0.3
outer_rate = 0.7
outer_beta = 0.9

FSDP = ("x", "yh")
REP = ("yl", "zh", "zl", "core")
ZC = ("zh", "zl", "core")
SWAP = [(0, 1), (1, 0)]
f32 = jnp.float32
bf16 = jnp.bfloat16
S = jax.ShapeDtypeStruct
PARAMS = pltpu.CompilerParams(vmem_limit_bytes=24 * 2**20)


HBM = pl.BlockSpec(memory_space=pltpu.HBM)
CHEAP = pl.CostEstimate(flops=1000, bytes_accessed=1000, transcendentals=0)
ANY = pl.BlockSpec(memory_space=pl.ANY)
VMEM = pl.BlockSpec(memory_space=pltpu.VMEM)


def far(array):
    return pltpu.with_memory_space_constraint(array, pltpu.HBM)


def z_shift(delta):
    pairs = []
    for z in range(32):
        for core, sign in ((0, 1), (1, -1)):
            pairs.append((z * 2 + core, (z + sign * delta) % 32 * 2 + core))
    return pairs


def send_out(buffer, out_ref, sems):
    copies = []
    for core in range(2):
        for peer in range(8):
            at = core * 8 + peer
            copies.append(pltpu.make_async_copy(buffer.at[core], out_ref.at[at], sems.at[at]))
            copies[-1].start()
    for copy in copies:
        copy.wait()


def pack_kernel(cot_hbm, tok_hbm, out_ref, cot, tok, buffer, sems, in_sems):
    cot_copy = pltpu.make_async_copy(cot_hbm, cot, in_sems.at[0])
    tok_copy = pltpu.make_async_copy(tok_hbm, tok, in_sems.at[1])
    cot_copy.start()
    tok_copy.start()
    cot_copy.wait()
    turned = cot[...].astype(f32).T.reshape(64, 2, 8, 128)
    for core in range(2):
        buffer[core, 0:512] = turned[:, core].reshape(512, 128).astype(bf16)
    tok_copy.wait()
    rows = []
    for j in range(8):
        part = tok[:, j * 128 : (j + 1) * 128].astype(f32)
        rows.append(jnp.sum(part * part, axis=0, keepdims=True))
    square = jnp.concatenate(rows, axis=0)
    high = square.astype(bf16).astype(f32)
    middle = (square - high).astype(bf16).astype(f32)
    low = square - high - middle
    tail = jnp.concatenate([high, middle, low, jnp.zeros_like(low)], axis=0).astype(bf16)
    for core in range(2):
        buffer[core, 512:544] = tail
    send_out(buffer, out_ref, sems)


def weight_kernel(wt_ref, gain_ref, mine_ref, other_ref, turned):
    core = lax.axis_index("core")
    turned[...] = wt_ref[...].astype(f32).T.reshape(64, 2, 8, FEAT)
    gain = jnp.broadcast_to(gain_ref[...].astype(f32), (16, FEAT)).astype(bf16)
    for which, out in ((core, mine_ref), (1 - core, other_ref)):
        out[0:512] = turned[:, which].reshape(512, FEAT).astype(bf16)
        out[512:528] = gain


def product(got, hidden):
    cot = jnp.concatenate([got[g, 0:512] for g in range(8)], axis=1)
    return lax.dot_general(cot, hidden, (((1,), (1,)), ((), ())), preferred_element_type=f32)


def eight(which):
    return pl.ds(which * 8, 8)


def start_all(pairs, sems):
    copies = [pltpu.make_async_copy(src, dst, sems.at[i]) for i, (src, dst) in enumerate(pairs)]
    for copy in copies:
        copy.start()
    return copies


def grad_kernel(
    got_hbm, tok_hbm, tok_sib_hbm, w_hbm, w_sib_hbm,
    send_ref, keep_ref, hid_hbm, part_ref, part_sib_ref,
    got, tok, weight, hid, sems,
):
    core = lax.axis_index("core")
    yl = lax.axis_index("yl")
    copies = start_all(
        [
            (got_hbm.at[eight(core)], got.at[0]),
            (tok_hbm, tok.at[0]),
            (w_hbm, weight.at[0]),
            (got_hbm.at[eight(1 - core)], got.at[1]),
            (tok_sib_hbm, tok.at[1]),
            (w_sib_hbm, weight.at[1]),
        ],
        sems,
    )
    new = jnp.zeros((512, FEAT), f32)
    hid_copy = pltpu.make_async_copy(hid.at[0], hid_hbm, sems.at[6])
    for slot, part in enumerate((part_ref, part_sib_ref)):
        copies[slot * 3].wait()
        square = jnp.zeros((8, 128), f32)
        for g in range(8):
            tail = got[slot, g, 512:544].astype(f32)
            square += tail[0:8] + (tail[8:16] + tail[16:24])
        inv_rms = lax.rsqrt(square / D + rms_eps)
        copies[slot * 3 + 1].wait()
        copies[slot * 3 + 2].wait()
        gain = weight[slot, 512:528].astype(f32)[0:8].T[:, 0:1]
        for j in range(8):
            at = slice(j * 128, (j + 1) * 128)
            normed = tok[slot, :, at].astype(f32) * inv_rms[j : j + 1]
            hid[slot, :, at] = (normed * gain).astype(bf16)
        if slot == 0:
            hid_copy.start()
        grad = product(got.at[slot], hid[slot])
        w = weight[slot, 0:512].astype(f32)
        part[...] = jnp.sum(w * grad, axis=0, keepdims=True)
        new += w - inner_rate * grad

    @pl.when(yl == 0)
    def _():
        keep_ref[...] = new[0:256]
        send_ref[...] = new[256:512].astype(bf16)

    @pl.when(yl == 1)
    def _():
        keep_ref[...] = new[256:512]
        send_ref[...] = new[0:256].astype(bf16)

    hid_copy.wait()


def split_kernel(keep_in, arrived, keep, plus, minus, twice, total):
    core = lax.axis_index("core")
    z = lax.axis_index("zh") * 4 + lax.axis_index("zl")
    sign = 1 - 2 * core
    total[...] = (keep_in[...] + arrived[...].astype(f32)).reshape(32, 8, FEAT)

    def block(offset):
        return total[(z + sign * offset + 64) % 32]

    for i in range(8):
        keep[i] = block(4 * (i - 3))
        minus[i] = block(4 * (i - 3) - 1).astype(bf16)
        plus[i] = block(4 * (i - 4) + 1).astype(bf16)
        twice[i] = block(4 * (i - 4) + 2).astype(bf16)


def middle_kernel(keep, plus, minus, twice, keep_out, plus_out, minus_out):
    total = []
    for i in range(9):
        value = jnp.zeros((8, FEAT), f32)
        if i > 0:
            value += keep[i - 1] + minus[i - 1].astype(f32)
        if i < 8:
            value += plus[i].astype(f32) + twice[i].astype(f32)
        total.append(value)
    for c in range(3):
        minus_out[c] = total[3 * c].astype(bf16)
        keep_out[c] = total[3 * c + 1]
        plus_out[c] = total[3 * c + 2].astype(bf16)


def last_kernel(keep, plus, minus, keep_out, back_out, on_out):
    total = [keep[c] + plus[c].astype(f32) + minus[c].astype(f32) for c in range(3)]
    back_out[0] = total[0].astype(bf16)
    keep_out[...] = total[1]
    on_out[0] = total[2].astype(bf16)


def keys_kernel(hid_ref, wt_ref, out_ref):
    for group in range(8):
        hid = hid_ref[:, group * 128 : (group + 1) * 128]
        out_ref[group] = lax.dot_general(
            hid, wt_ref[...], (((0,), (0,)), ((), ())), preferred_element_type=f32
        ).astype(bf16)


def pass_kernel(array, after, also, out):
    pass


def per_device(tokens, norm_gain, key_weight, key_cotangent, global_fragment, outer_momentum):
    tok = tokens.T
    weight_t = key_weight[0].T
    packed = pl.pallas_call(
        pack_kernel,
        out_shape=pltpu.HBM((16, 544, 128), bf16),
        in_specs=[HBM, HBM],
        out_specs=HBM,
        scratch_shapes=[
            pltpu.VMEM((128, 1024), bf16),
            pltpu.VMEM((FEAT, 1024), bf16),
            pltpu.VMEM((2, 544, 128), bf16),
            pltpu.SemaphoreType.DMA((16,)),
            pltpu.SemaphoreType.DMA((2,)),
        ],
        compiler_params=PARAMS,
        name="pack",
    )(far(key_cotangent), far(tok))
    got = lax.all_to_all(packed, ("core",) + FSDP, 0, 0)

    tok_sib = lax.ppermute(tok, "core", SWAP)
    w_mine, w_other = pl.pallas_call(
        weight_kernel,
        out_shape=(S((528, FEAT), bf16), S((528, FEAT), bf16)),
        scratch_shapes=[pltpu.VMEM((64, 2, 8, FEAT), f32)],
        compiler_params=PARAMS,
        cost_estimate=CHEAP,
        name="weights",
    )(weight_t, norm_gain)
    w_sib = lax.ppermute(w_other, "core", SWAP)

    send, keep, hid, part, part_sib = pl.pallas_call(
        grad_kernel,
        out_shape=(
            S((256, FEAT), bf16), S((256, FEAT), f32), pltpu.HBM((FEAT, 1024), bf16),
            S((1, FEAT), f32), S((1, FEAT), f32),
        ),
        in_specs=[ANY] + [HBM] * 4,
        out_specs=(VMEM, VMEM, HBM, VMEM, VMEM),
        scratch_shapes=[
            pltpu.VMEM((2, 8, 544, 128), bf16),
            pltpu.VMEM((2, FEAT, 1024), bf16),
            pltpu.VMEM((2, 528, FEAT), bf16),
            pltpu.VMEM((2, FEAT, 1024), bf16),
            pltpu.SemaphoreType.DMA((7,)),
        ],
        compiler_params=PARAMS,
        name="grad",
    )(got, far(tok), far(tok_sib), far(w_mine), far(w_sib))
    arrived = lax.ppermute(send, "yl", SWAP)
    part_sib = lax.ppermute(part_sib, "core", SWAP)

    keys = pl.pallas_call(
        keys_kernel,
        out_shape=pltpu.HBM((8, 128, 1024), bf16),
        out_specs=VMEM,
        compiler_params=PARAMS,
        name="keys",
    )(hid, weight_t)

    eight_blocks = S((8, 8, FEAT), bf16)
    three = S((3, 8, FEAT), bf16)
    one = S((1, 8, FEAT), bf16)
    keep, plus, minus, twice = pl.pallas_call(
        split_kernel,
        out_shape=(S((8, 8, FEAT), f32), eight_blocks, eight_blocks, eight_blocks),
        scratch_shapes=[pltpu.VMEM((32, 8, FEAT), f32)],
        compiler_params=PARAMS,
        name="split",
    )(keep, arrived)
    keys = pl.pallas_call(
        pass_kernel,
        out_shape=pltpu.HBM((8, 128, 1024), bf16),
        in_specs=[HBM, ANY, ANY],
        out_specs=HBM,
        input_output_aliases={0: 0},
        compiler_params=PARAMS,
        name="pass_on",
    )(keys, plus, part_sib)
    key_parts = lax.all_to_all(keys, FSDP, 0, 0)

    plus = lax.ppermute(plus, ZC, z_shift(1))
    minus = lax.ppermute(minus, ZC, z_shift(-1))
    twice = lax.ppermute(twice, ZC, z_shift(2))
    keep, plus, minus = pl.pallas_call(
        middle_kernel,
        out_shape=(S((3, 8, FEAT), f32), three, three),
        compiler_params=PARAMS,
        name="middle",
    )(keep, plus, minus, twice)
    plus = lax.ppermute(plus, ZC, z_shift(4))
    minus = lax.ppermute(minus, ZC, z_shift(-4))
    keep, back, on = pl.pallas_call(
        last_kernel,
        out_shape=(S((8, FEAT), f32), one, one),
        compiler_params=PARAMS,
        name="last",
    )(keep, plus, minus)
    on = lax.ppermute(on, ZC, z_shift(12))
    back = lax.ppermute(back, ZC, z_shift(-12))
    summed = keep + on[0].astype(f32) + back[0].astype(f32)

    gain_grad = (part + part_sib) / norm_gain.astype(f32)
    avg_grad = global_fragment - summed / N_REP
    new_momentum = outer_beta * outer_momentum + avg_grad
    new_global = global_fragment - outer_rate * (avg_grad + outer_beta * new_momentum)
    key_out = jnp.sum(key_parts.astype(f32), axis=0).astype(bf16)
    return (key_out, gain_grad, new_global, new_momentum)


def solution(mesh):
    fine = Mesh(mesh.devices.reshape(2, 8, 4, 2, 4, 2), REP + FSDP)
    return jax.shard_map(
        per_device,
        mesh=fine,
        in_specs=(
            P(REP, FSDP),
            P(REP, FSDP),
            P(REP, None, FSDP),
            P(REP + FSDP, None),
            P(REP, FSDP),
            P(REP, FSDP),
        ),
        out_specs=(P(REP + FSDP, None), P(REP, FSDP), P(REP, FSDP), P(REP, FSDP)),
        check_vma=False,
    )
```

time: 158 us -> 142 us (0.90)
  the two profiles are of different devices: /device:TPU:16 before, /device:TPU:2 now
where the time goes in v4:
time: 142 us
  starting transfers between devices  72.9 us (51%)
  waiting for transfers between devices  50.3 us (35%)
  Pallas kernels  12.2 us (9%)
  local copies, waits for them, and re-layouts  2.98 us (2%)
  other arithmetic  2.33 us (2%)
    all_to_all x1, waiting for transfers between devices, per_device(): got = lax.all_to_all(packed, ('core',) + FSDP, 0, 0)  23.4 us
    all_to_all x1, starting transfers between devices, per_device(): got = lax.all_to_all(packed, ('core',) + FSDP, 0, 0)  16.8 us
    ppermute x1, starting transfers between devices, per_device(): back = lax.ppermute(back, ZC, z_shift(-12))  14.6 us
    ppermute x1, waiting for transfers between devices, per_device(): on = lax.ppermute(on, ZC, z_shift(12))  13.7 us
    ppermute x1, starting transfers between devices, per_device(): minus = lax.ppermute(minus, ZC, z_shift(-1))  9.38 us
    ppermute x1, starting transfers between devices, per_device(): minus = lax.ppermute(minus, ZC, z_shift(-4))  7.83 us
    ppermute x1, waiting for transfers between devices, per_device(): twice = lax.ppermute(twice, ZC, z_shift(2))  6.95 us
    all_to_all x1, starting transfers between devices, per_device(): key_parts = lax.all_to_all(keys, FSDP, 0, 0)  5.55 us
  transfers between devices with their start and end apart: 13, of which 7 were waited for; matrix products, arithmetic and copies ran while one was open for 1% of the time, Pallas kernels for 3%

profile of v4, /device:TPU:2, one launch (start us, length us, event | category | flops | bytes accessed | tf_op | source)
XLA Modules:
  0.0 141.6 jit_solution(1001178173000571222)
XLA Ops:
  0.6 3.2 %pack.1 = bf16[16,544,128]{2,1,0:T(8,128)(2,1)} custom-call(bf16[128,1024]{1,0:T(8,128)(2,1)} %cot_hbm.1, bf16[576,1024]{1,0:T(8,128)(2,1)} %bitcast.22), custom_call_target="tpu_custom_call" | custom-call | tf_op jit(solution)/shard_map/pack/pallas_call | solution.py:212
  3.8 0.0 copy-start
  3.8 0.0 copy-start.3
  3.9 16.8 %all-to-all-start = ((bf16[16,544,128]{2,1,0:T(8,128)(2,1)}), bf16[16,544,128]{2,1,0:T(8,128)(2,1)S(1)}, u32[]{:S(2)}, u32[]{:S(2)}) async-start(bf16[16,544,128]{2,1,0:T(8,128)(2,1)} %pack.1), calls=%async_computation | async-start | bytes 4456448 | tf_op jit(solution)/shard_map/all_to_all | solution.py:227
  20.7 2.1 %collective-permute-start = (bf16[576,1024]{1,0:T(8,128)(2,1)}, bf16[576,1024]{1,0:T(8,128)(2,1)}, u32[]{:S(2)}, u32[]{:S(2)}) collective-permute-start(bf16[576,1024]{1,0:T(8,128)(2,1)} %bitcast.23), channel_id=1, source_target_pairs={{0,8},{8,0},{1,9},{9,1},{2,10},{10,2},{3,11},{11,3},{4,12},{12,4},... | collective-permute-start | bytes 3538952 | tf_op jit(solution)/shard_map/ppermute | solution.py:229
  22.8 0.0 copy-done
  22.8 0.0 copy-done.3
  22.8 0.7 weights.1
  23.5 0.0 copy-start.2
  23.5 0.8 copy-done.2
  24.4 2.2 %collective-permute-start.1 = (bf16[528,576]{1,0:T(8,128)(2,1)S(1)}, bf16[528,576]{1,0:T(8,128)(2,1)S(1)}, u32[]{:S(2)}, u32[]{:S(2)}) collective-permute-start(bf16[528,576]{1,0:T(8,128)(2,1)S(1)} %get-tuple-element.22), channel_id=1, source_target_pairs={{0,8},{8,0},{1,9},{9,1},{2,10},{10,2},{3,11},{11,3},{4,12},{12,4},... | collective-permute-start | bytes 1824776 | tf_op jit(solution)/shard_map/ppermute | solution.py:238
  26.6 1.8 %collective-permute-done.1.w_sib_hbm = bf16[528,576]{1,0:T(8,128)(2,1)S(1)} collective-permute-done((bf16[528,576]{1,0:T(8,128)(2,1)S(1)}, bf16[528,576]{1,0:T(8,128)(2,1)S(1)}, u32[]{:S(2)}, u32[]{:S(2)}) %collective-permute-start.1) | collective-permute-done | bytes 608288 | tf_op jit(solution)/shard_map/ppermute | solution.py:238
  28.4 0.0 copy-start.4
  28.4 0.9 copy-done.4
  29.2 0.0 collective-permute-done.tok_sib_hbm
  29.2 23.4 %all-to-all-done.got_hbm = bf16[16,544,128]{2,1,0:T(8,128)(2,1)S(1)} async-done(((bf16[16,544,128]{2,1,0:T(8,128)(2,1)}), bf16[16,544,128]{2,1,0:T(8,128)(2,1)S(1)}, u32[]{:S(2)}, u32[]{:S(2)}) %all-to-all-start) | async-done | bytes 2228256 | tf_op jit(solution)/shard_map/all_to_all | solution.py:227
  52.7 4.9 %grad.1 = (bf16[256,576]{1,0:T(8,128)(2,1)S(1)}, f32[256,576]{1,0:T(8,128)S(1)}, bf16[576,1024]{1,0:T(8,128)(2,1)}, f32[1,576]{1,0:T(1,128)S(1)}, f32[1,576]{1,0:T(1,128)S(1)}) custom-call(bf16[16,544,128]{2,1,0:T(8,128)(2,1)S(1)} %all-to-all-done.got_hbm, bf16[576,1024]{1,0:T(8,128)(2,1)} %bitcast.24, bf16[576,1024]{1,0:T(8,128)(2,1)} %collective-permute-done.tok_sib_hbm, ...), custom_call_target="tpu_custom_call" | custom-call | tf_op jit(solution)/shard_map/grad/pallas_call | solution.py:240
  57.5 1.9 %collective-permute-start.2 = (bf16[256,576]{1,0:T(8,128)(2,1)S(1)}, bf16[256,576]{1,0:T(8,128)(2,1)S(1)}, u32[]{:S(2)}, u32[]{:S(2)}) collective-permute-start(bf16[256,576]{1,0:T(8,128)(2,1)S(1)} %get-tuple-element.25), channel_id=1, source_target_pairs={{0,512},{512,0},{1,513},{513,1},{2,514},{514,2},{3,515},{515,3},{4... | collective-permute-start | bytes 884744 | tf_op jit(solution)/shard_map/ppermute | solution.py:258
  59.5 1.9 %collective-permute-start.3 = (f32[1,576]{1,0:T(1,128)S(1)}, f32[1,576]{1,0:T(1,128)S(1)}, u32[]{:S(2)}, u32[]{:S(2)}) collective-permute-start(f32[1,576]{1,0:T(1,128)S(1)} %get-tuple-element.27), channel_id=1, source_target_pairs={{0,8},{8,0},{1,9},{9,1},{2,10},{10,2},{3,11},{11,3},{4,12},{12,4},... | collective-permute-start | bytes 6920 | tf_op jit(solution)/shard_map/ppermute | solution.py:259
  61.4 0.0 copy-start.1
  61.4 1.3 copy-done.1
  62.7 3.3 %keys.1.array = bf16[8,128,1024]{2,1,0:T(8,128)(2,1)} custom-call(bf16[576,1024]{1,0:T(8,128)(2,1)S(1)} %copy-done.1, bf16[576,1024]{1,0:T(8,128)(2,1)S(1)} %bitcast.21), custom_call_target="tpu_custom_call" | custom-call | tf_op jit(solution)/shard_map/keys/pallas_call | solution.py:261
  65.9 2.5 %collective-permute-done.2.arrived = bf16[256,576]{1,0:T(8,128)(2,1)S(1)} collective-permute-done((bf16[256,576]{1,0:T(8,128)(2,1)S(1)}, bf16[256,576]{1,0:T(8,128)(2,1)S(1)}, u32[]{:S(2)}, u32[]{:S(2)}) %collective-permute-start.2) | collective-permute-done | bytes 294944 | tf_op jit(solution)/shard_map/ppermute | solution.py:258
  68.4 0.1 split.1
  68.6 0.0 collective-permute-done.3.also
  68.6 0.0 copy-start.5
  68.6 0.0 copy-start.6
  68.6 5.5 %all-to-all-start.1 = ((bf16[8,128,1024]{2,1,0:T(8,128)(2,1)}), bf16[8,128,1024]{2,1,0:T(8,128)(2,1)S(1)}, u32[]{:S(2)}, u32[]{:S(2)}) async-start(bf16[8,128,1024]{2,1,0:T(8,128)(2,1)} %pass_on.1), calls=%async_computation.1 | async-start | bytes 4194304 | tf_op jit(solution)/shard_map/all_to_all | solution.py:288
  74.2 1.9 %collective-permute-start.4 = (bf16[8,8,576]{2,1,0:T(8,128)(2,1)S(1)}, bf16[8,8,576]{2,1,0:T(8,128)(2,1)S(1)}, u32[]{:S(2)}, u32[]{:S(2)}) collective-permute-start(bf16[8,8,576]{2,1,0:T(8,128)(2,1)S(1)} %get-tuple-element.26.after), channel_id=1, source_target_pairs={{0,16},{8,504},{16,32},{24,8},{32,48},{40,24},{48,64},{56,40},{64,... | collective-permute-start | bytes 221192 | tf_op jit(solution)/shard_map/ppermute | solution.py:290
  76.1 9.4 %collective-permute-start.5 = (bf16[8,8,576]{2,1,0:T(8,128)(2,1)S(1)}, bf16[8,8,576]{2,1,0:T(8,128)(2,1)S(1)}, u32[]{:S(2)}, u32[]{:S(2)}) collective-permute-start(bf16[8,8,576]{2,1,0:T(8,128)(2,1)S(1)} %get-tuple-element.30), channel_id=1, source_target_pairs={{0,496},{8,24},{16,0},{24,40},{32,16},{40,56},{48,32},{56,72},{64,... | collective-permute-start | bytes 221192 | tf_op jit(solution)/shard_map/ppermute | solution.py:291
  85.5 1.9 %collective-permute-start.6 = (bf16[8,8,576]{2,1,0:T(8,128)(2,1)S(1)}, bf16[8,8,576]{2,1,0:T(8,128)(2,1)S(1)}, u32[]{:S(2)}, u32[]{:S(2)}) collective-permute-start(bf16[8,8,576]{2,1,0:T(8,128)(2,1)S(1)} %get-tuple-element.31), channel_id=1, source_target_pairs={{0,32},{8,488},{16,48},{24,504},{32,64},{40,8},{48,80},{56,24},{64... | collective-permute-start | bytes 221192 | tf_op jit(solution)/shard_map/ppermute | solution.py:292
  87.4 0.0 collective-permute-done.4.plus
  87.4 0.1 collective-permute-done.5.minus
  87.5 6.9 %collective-permute-done.6.twice = bf16[8,8,576]{2,1,0:T(8,128)(2,1)S(1)} collective-permute-done((bf16[8,8,576]{2,1,0:T(8,128)(2,1)S(1)}, bf16[8,8,576]{2,1,0:T(8,128)(2,1)S(1)}, u32[]{:S(2)}, u32[]{:S(2)}) %collective-permute-start.6) | collective-permute-done | bytes 73760 | tf_op jit(solution)/shard_map/ppermute | solution.py:292
  94.5 1.9 %collective-permute-start.7 = (bf16[3,8,576]{2,1,0:T(8,128)(2,1)S(1)}, bf16[3,8,576]{2,1,0:T(8,128)(2,1)S(1)}, u32[]{:S(2)}, u32[]{:S(2)}) collective-permute-start(bf16[3,8,576]{2,1,0:T(8,128)(2,1)S(1)} %get-tuple-element.33), channel_id=1, source_target_pairs={{0,64},{8,456},{16,80},{24,472},{32,96},{40,488},{48,112},{56,504}... | collective-permute-start | bytes 82952 | tf_op jit(solution)/shard_map/ppermute | solution.py:299
  96.4 7.8 %collective-permute-start.8 = (bf16[3,8,576]{2,1,0:T(8,128)(2,1)S(1)}, bf16[3,8,576]{2,1,0:T(8,128)(2,1)S(1)}, u32[]{:S(2)}, u32[]{:S(2)}) collective-permute-start(bf16[3,8,576]{2,1,0:T(8,128)(2,1)S(1)} %get-tuple-element.34), channel_id=1, source_target_pairs={{0,448},{8,72},{16,464},{24,88},{32,480},{40,104},{48,496},{56,120... | collective-permute-start | bytes 82952 | tf_op jit(solution)/shard_map/ppermute | solution.py:300
  104.3 0.0 collective-permute-done.7.plus
  104.3 1.8 %collective-permute-done.8.minus = bf16[3,8,576]{2,1,0:T(8,128)(2,1)S(1)} collective-permute-done((bf16[3,8,576]{2,1,0:T(8,128)(2,1)S(1)}, bf16[3,8,576]{2,1,0:T(8,128)(2,1)S(1)}, u32[]{:S(2)}, u32[]{:S(2)}) %collective-permute-start.8) | collective-permute-done | bytes 27680 | tf_op jit(solution)/shard_map/ppermute | solution.py:300
  106.1 14.6 %collective-permute-start.10 = (bf16[1,8,576]{2,1,0:T(8,128)(2,1)S(1)}, bf16[1,8,576]{2,1,0:T(8,128)(2,1)S(1)}, u32[]{:S(2)}, u32[]{:S(2)}) collective-permute-start(bf16[1,8,576]{2,1,0:T(8,128)(2,1)S(1)} %get-tuple-element.37), channel_id=1, source_target_pairs={{0,320},{8,200},{16,336},{24,216},{32,352},{40,232},{48,368},{56,2... | collective-permute-start | bytes 27656 | tf_op jit(solution)/shard_map/ppermute | solution.py:308
  120.7 4.8 %collective-permute-start.9 = (bf16[1,8,576]{2,1,0:T(8,128)(2,1)S(1)}, bf16[1,8,576]{2,1,0:T(8,128)(2,1)S(1)}, u32[]{:S(2)}, u32[]{:S(2)}) collective-permute-start(bf16[1,8,576]{2,1,0:T(8,128)(2,1)S(1)} %get-tuple-element.36), channel_id=1, source_target_pairs={{0,192},{8,328},{16,208},{24,344},{32,224},{40,360},{48,240},{56,3... | collective-permute-start | bytes 27656 | tf_op jit(solution)/shard_map/ppermute | solution.py:307
  125.5 0.6 convert_divide_fusion
  126.1 0.0 collective-permute-done.10
  126.1 13.7 %collective-permute-done.9 = bf16[1,8,576]{2,1,0:T(8,128)(2,1)S(1)} collective-permute-done((bf16[1,8,576]{2,1,0:T(8,128)(2,1)S(1)}, bf16[1,8,576]{2,1,0:T(8,128)(2,1)S(1)}, u32[]{:S(2)}, u32[]{:S(2)}) %collective-permute-start.9) | collective-permute-done | bytes 9248 | tf_op jit(solution)/shard_map/ppermute | solution.py:307
  139.8 0.0 copy-done.5
  139.8 0.0 copy-done.6
  139.8 0.6 multiply_subtract_fusion
  140.5 0.0 all-to-all-done.1
  140.5 1.1 reduce_sum.12
  (3 shorter events, 0.1 us)
Async XLA Ops:
  3.8 18.9 %copy-start = (bf16[1,1024,576]{1,2,0:T(8,128)(2,1)S(1)}, bf16[1,1024,576]{1,2,0:T(8,128)(2,1)}, u32[]{:S(2)}) copy-start(bf16[1,1024,576]{1,2,0:T(8,128)(2,1)} %param.8) | copy-start | bytes 3538948
  3.8 18.9 %copy-start.3 = (bf16[1,576]{1,0:T(2,128)(2,1)S(1)}, bf16[1,576]{1,0:T(2,128)(2,1)}, u32[]{:S(2)}) copy-start(bf16[1,576]{1,0:T(2,128)(2,1)} %gain_ref.1) | copy-start | bytes 3460
  3.9 48.8 %all-to-all-start = ((bf16[16,544,128]{2,1,0:T(8,128)(2,1)}), bf16[16,544,128]{2,1,0:T(8,128)(2,1)S(1)}, u32[]{:S(2)}, u32[]{:S(2)}) async-start(bf16[16,544,128]{2,1,0:T(8,128)(2,1)} %pack.1), calls=%async_computation | async-start | bytes 4456448 | tf_op jit(solution)/shard_map/all_to_all | solution.py:227
  20.7 8.5 %collective-permute-start = (bf16[576,1024]{1,0:T(8,128)(2,1)}, bf16[576,1024]{1,0:T(8,128)(2,1)}, u32[]{:S(2)}, u32[]{:S(2)}) collective-permute-start(bf16[576,1024]{1,0:T(8,128)(2,1)} %bitcast.23), channel_id=1, source_target_pairs={{0,8},{8,0},{1,9},{9,1},{2,10},{10,2},{3,11},{11,3},{4,12},{12,4},... | collective-permute-start | bytes 3538952 | tf_op jit(solution)/shard_map/ppermute | solution.py:229
  23.5 0.8 copy-start.2
  24.4 4.0 %collective-permute-start.1 = (bf16[528,576]{1,0:T(8,128)(2,1)S(1)}, bf16[528,576]{1,0:T(8,128)(2,1)S(1)}, u32[]{:S(2)}, u32[]{:S(2)}) collective-permute-start(bf16[528,576]{1,0:T(8,128)(2,1)S(1)} %get-tuple-element.22), channel_id=1, source_target_pairs={{0,8},{8,0},{1,9},{9,1},{2,10},{10,2},{3,11},{11,3},{4,12},{12,4},... | collective-permute-start | bytes 1824776 | tf_op jit(solution)/shard_map/ppermute | solution.py:238
  28.4 0.9 copy-start.4
  57.5 10.9 %collective-permute-start.2 = (bf16[256,576]{1,0:T(8,128)(2,1)S(1)}, bf16[256,576]{1,0:T(8,128)(2,1)S(1)}, u32[]{:S(2)}, u32[]{:S(2)}) collective-permute-start(bf16[256,576]{1,0:T(8,128)(2,1)S(1)} %get-tuple-element.25), channel_id=1, source_target_pairs={{0,512},{512,0},{1,513},{513,1},{2,514},{514,2},{3,515},{515,3},{4... | collective-permute-start | bytes 884744 | tf_op jit(solution)/shard_map/ppermute | solution.py:258
  59.5 9.1 %collective-permute-start.3 = (f32[1,576]{1,0:T(1,128)S(1)}, f32[1,576]{1,0:T(1,128)S(1)}, u32[]{:S(2)}, u32[]{:S(2)}) collective-permute-start(f32[1,576]{1,0:T(1,128)S(1)} %get-tuple-element.27), channel_id=1, source_target_pairs={{0,8},{8,0},{1,9},{9,1},{2,10},{10,2},{3,11},{11,3},{4,12},{12,4},... | collective-permute-start | bytes 6920 | tf_op jit(solution)/shard_map/ppermute | solution.py:259
  61.4 1.3 copy-start.1
  68.6 71.2 %copy-start.5 = (f32[8,576]{1,0:T(8,128)S(1)}, f32[8,576]{1,0:T(8,128)}, u32[]{:S(2)}) copy-start(f32[8,576]{1,0:T(8,128)} %param.10) | copy-start | bytes 55300
  68.6 71.2 %copy-start.6 = (f32[8,576]{1,0:T(8,128)S(1)}, f32[8,576]{1,0:T(8,128)}, u32[]{:S(2)}) copy-start(f32[8,576]{1,0:T(8,128)} %param.11) | copy-start | bytes 55300
  68.6 71.9 %all-to-all-start.1 = ((bf16[8,128,1024]{2,1,0:T(8,128)(2,1)}), bf16[8,128,1024]{2,1,0:T(8,128)(2,1)S(1)}, u32[]{:S(2)}, u32[]{:S(2)}) async-start(bf16[8,128,1024]{2,1,0:T(8,128)(2,1)} %pass_on.1), calls=%async_computation.1 | async-start | bytes 4194304 | tf_op jit(solution)/shard_map/all_to_all | solution.py:288
  74.2 13.2 %collective-permute-start.4 = (bf16[8,8,576]{2,1,0:T(8,128)(2,1)S(1)}, bf16[8,8,576]{2,1,0:T(8,128)(2,1)S(1)}, u32[]{:S(2)}, u32[]{:S(2)}) collective-permute-start(bf16[8,8,576]{2,1,0:T(8,128)(2,1)S(1)} %get-tuple-element.26.after), channel_id=1, source_target_pairs={{0,16},{8,504},{16,32},{24,8},{32,48},{40,24},{48,64},{56,40},{64,... | collective-permute-start | bytes 221192 | tf_op jit(solution)/shard_map/ppermute | solution.py:290
  76.1 11.4 %collective-permute-start.5 = (bf16[8,8,576]{2,1,0:T(8,128)(2,1)S(1)}, bf16[8,8,576]{2,1,0:T(8,128)(2,1)S(1)}, u32[]{:S(2)}, u32[]{:S(2)}) collective-permute-start(bf16[8,8,576]{2,1,0:T(8,128)(2,1)S(1)} %get-tuple-element.30), channel_id=1, source_target_pairs={{0,496},{8,24},{16,0},{24,40},{32,16},{40,56},{48,32},{56,72},{64,... | collective-permute-start | bytes 221192 | tf_op jit(solution)/shard_map/ppermute | solution.py:291
  85.5 9.0 %collective-permute-start.6 = (bf16[8,8,576]{2,1,0:T(8,128)(2,1)S(1)}, bf16[8,8,576]{2,1,0:T(8,128)(2,1)S(1)}, u32[]{:S(2)}, u32[]{:S(2)}) collective-permute-start(bf16[8,8,576]{2,1,0:T(8,128)(2,1)S(1)} %get-tuple-element.31), channel_id=1, source_target_pairs={{0,32},{8,488},{16,48},{24,504},{32,64},{40,8},{48,80},{56,24},{64... | collective-permute-start | bytes 221192 | tf_op jit(solution)/shard_map/ppermute | solution.py:292
  94.5 9.8 %collective-permute-start.7 = (bf16[3,8,576]{2,1,0:T(8,128)(2,1)S(1)}, bf16[3,8,576]{2,1,0:T(8,128)(2,1)S(1)}, u32[]{:S(2)}, u32[]{:S(2)}) collective-permute-start(bf16[3,8,576]{2,1,0:T(8,128)(2,1)S(1)} %get-tuple-element.33), channel_id=1, source_target_pairs={{0,64},{8,456},{16,80},{24,472},{32,96},{40,488},{48,112},{56,504}... | collective-permute-start | bytes 82952 | tf_op jit(solution)/shard_map/ppermute | solution.py:299
  96.4 9.7 %collective-permute-start.8 = (bf16[3,8,576]{2,1,0:T(8,128)(2,1)S(1)}, bf16[3,8,576]{2,1,0:T(8,128)(2,1)S(1)}, u32[]{:S(2)}, u32[]{:S(2)}) collective-permute-start(bf16[3,8,576]{2,1,0:T(8,128)(2,1)S(1)} %get-tuple-element.34), channel_id=1, source_target_pairs={{0,448},{8,72},{16,464},{24,88},{32,480},{40,104},{48,496},{56,120... | collective-permute-start | bytes 82952 | tf_op jit(solution)/shard_map/ppermute | solution.py:300
  106.1 20.0 %collective-permute-start.10 = (bf16[1,8,576]{2,1,0:T(8,128)(2,1)S(1)}, bf16[1,8,576]{2,1,0:T(8,128)(2,1)S(1)}, u32[]{:S(2)}, u32[]{:S(2)}) collective-permute-start(bf16[1,8,576]{2,1,0:T(8,128)(2,1)S(1)} %get-tuple-element.37), channel_id=1, source_target_pairs={{0,320},{8,200},{16,336},{24,216},{32,352},{40,232},{48,368},{56,2... | collective-permute-start | bytes 27656 | tf_op jit(solution)/shard_map/ppermute | solution.py:308
  120.7 19.1 %collective-permute-start.9 = (bf16[1,8,576]{2,1,0:T(8,128)(2,1)S(1)}, bf16[1,8,576]{2,1,0:T(8,128)(2,1)S(1)}, u32[]{:S(2)}, u32[]{:S(2)}) collective-permute-start(bf16[1,8,576]{2,1,0:T(8,128)(2,1)S(1)} %get-tuple-element.36), channel_id=1, source_target_pairs={{0,192},{8,328},{16,208},{24,344},{32,224},{40,360},{48,240},{56,3... | collective-permute-start | bytes 27656 | tf_op jit(solution)/shard_map/ppermute | solution.py:307

commit v5 on v1

v5 whole, which is shorter than its diff:
```python
import functools

import jax
import jax.numpy as jnp
from jax import lax
from jax.experimental import pallas as pl
from jax.experimental.pallas import tpu as pltpu
from jax.sharding import Mesh, PartitionSpec as P

D = 4608
N_REP = 128
FEAT = 576

rms_eps = 1e-06
inner_rate = 0.3
outer_rate = 0.7
outer_beta = 0.9

FSDP = ("x", "yh")
REP = ("yl", "z", "core")
SWAP = [(0, 1), (1, 0)]
f32 = jnp.float32
bf16 = jnp.bfloat16
S = jax.ShapeDtypeStruct
PARAMS = pltpu.CompilerParams(vmem_limit_bytes=24 * 2**20)


HBM = pl.BlockSpec(memory_space=pltpu.HBM)
CHEAP = pl.CostEstimate(flops=1000, bytes_accessed=1000, transcendentals=0)
ANY = pl.BlockSpec(memory_space=pl.ANY)
VMEM = pl.BlockSpec(memory_space=pltpu.VMEM)


def far(array):
    return pltpu.with_memory_space_constraint(array, pltpu.HBM)


ALONG_X = (2, 4, 6)
ACROSS = (1, 3, 5, 7)


def partner(bits):
    return [(i, i ^ bits) for i in range(8)]


def pack_kernel(cot_hbm, tok_hbm, out_ref, cot, tok, buffer, sems, in_sems):
    cot_copy = pltpu.make_async_copy(cot_hbm, cot, in_sems.at[0])
    tok_copy = pltpu.make_async_copy(tok_hbm, tok, in_sems.at[1])
    cot_copy.start()
    tok_copy.start()
    cot_copy.wait()
    buffer[0:1024] = cot[...].astype(f32).T.astype(bf16)
    tok_copy.wait()
    rows = []
    for j in range(8):
        part = tok[:, j * 128 : (j + 1) * 128].astype(f32)
        rows.append(jnp.sum(part * part, axis=0, keepdims=True))
    square = jnp.concatenate(rows, axis=0)
    high = square.astype(bf16).astype(f32)
    middle = (square - high).astype(bf16).astype(f32)
    low = square - high - middle
    tail = jnp.concatenate([high, middle, low, jnp.zeros_like(low)], axis=0).astype(bf16)
    buffer[1024:1056] = tail
    copies = []
    for peer in range(8):
        copies.append(pltpu.make_async_copy(buffer, out_ref.at[peer], sems.at[peer]))
        copies[-1].start()
    for copy in copies:
        copy.wait()


def weight_kernel(wt_ref, out_ref):
    out_ref[...] = wt_ref[...].astype(f32).T.astype(bf16)


def start_all(pairs, sems):
    copies = [pltpu.make_async_copy(src, dst, sems.at[i]) for i, (src, dst) in enumerate(pairs)]
    for copy in copies:
        copy.start()
    return copies


def grad_kernel(
    got_ref, tok_ref, w_ref, gain_ref,
    core_a_ref, core_b_ref, own_a_ref, own_b_ref, hid_hbm, gain_grad_ref,
    got, tok, weight, hid, total, sems,
):
    core = lax.axis_index("core")
    yl = lax.axis_index("yl")
    copies = start_all([(got_ref, got), (tok_ref, tok), (w_ref, weight)], sems)
    hid_copy = pltpu.make_async_copy(hid, hid_hbm, sems.at[3])
    gain_row = gain_ref[...].astype(f32)
    gain = jnp.broadcast_to(gain_row, (8, FEAT)).T[:, 0:1]
    copies[0].wait()
    square = jnp.zeros((8, 128), f32)
    for g in range(8):
        tail = got[g, 1024:1056].astype(f32)
        square += tail[0:8] + (tail[8:16] + tail[16:24])
    inv_rms = lax.rsqrt(square / D + rms_eps)
    copies[1].wait()
    for j in range(8):
        at = slice(j * 128, (j + 1) * 128)
        normed = tok[:, at].astype(f32) * inv_rms[j : j + 1]
        hid[:, at] = (normed * gain).astype(bf16)
    hid_copy.start()
    cot = jnp.concatenate([got[g, 0:1024] for g in range(8)], axis=1)
    grad = lax.dot_general(cot, hid[...], (((1,), (1,)), ((), ())), preferred_element_type=f32)
    copies[2].wait()
    w = weight[...].astype(f32)
    gain_grad_ref[...] = jnp.sum(w * grad, axis=0, keepdims=True) / gain_row
    total[...] = (w - inner_rate * grad).reshape(2, 32, 2, 8, FEAT)
    core_a_ref[...] = total[1 - yl, :, 1 - core].reshape(256, FEAT).astype(bf16)
    core_b_ref[...] = total[yl, :, 1 - core].reshape(256, FEAT).astype(bf16)
    own_a_ref[...] = total[1 - yl, :, core].reshape(256, FEAT)
    own_b_ref[...] = total[yl, :, core].reshape(256, FEAT)
    hid_copy.wait()


def pair_kernel(own, sibling, out):
    out[...] = (own[...] + sibling[...].astype(f32)).astype(bf16)


def three_kernel(own, sibling, arrived, after, out):
    out[...] = (own[...] + sibling[...].astype(f32) + arrived[...].astype(f32)).astype(bf16)


def keys_kernel(bits, hid_ref, wt_ref, after_ref, *outs):
    me = lax.axis_index("x") * 2 + lax.axis_index("yh")
    for bit, out in zip(bits, outs):
        group = me ^ bit
        hid = hid_ref[:, pl.ds(pl.multiple_of(group * 128, 128), 128)]
        out[...] = lax.dot_general(
            hid, wt_ref[...], (((0,), (0,)), ((), ())), preferred_element_type=f32
        ).astype(bf16)


def partial_keys(bits, hid, weight_t, after, name):
    return pl.pallas_call(
        functools.partial(keys_kernel, bits),
        out_shape=tuple(S((128, 1024), bf16) for _ in bits),
        in_specs=[VMEM, VMEM, ANY],
        compiler_params=PARAMS,
        name=name,
    )(hid, weight_t, after)


def per_device(tokens, norm_gain, key_weight, key_cotangent, global_fragment, outer_momentum):
    tok = tokens.T
    weight_t = key_weight[0].T
    packed = pl.pallas_call(
        pack_kernel,
        out_shape=pltpu.HBM((8, 1056, 128), bf16),
        in_specs=[HBM, HBM],
        out_specs=HBM,
        scratch_shapes=[
            pltpu.VMEM((128, 1024), bf16),
            pltpu.VMEM((FEAT, 1024), bf16),
            pltpu.VMEM((1056, 128), bf16),
            pltpu.SemaphoreType.DMA((8,)),
            pltpu.SemaphoreType.DMA((2,)),
        ],
        compiler_params=PARAMS,
        name="pack",
    )(far(key_cotangent), far(tok))
    got = lax.all_to_all(packed, FSDP, 0, 0)
    weight = pl.pallas_call(
        weight_kernel,
        out_shape=pltpu.HBM((1024, FEAT), bf16),
        out_specs=VMEM,
        compiler_params=PARAMS,
        cost_estimate=CHEAP,
        name="turn",
    )(weight_t)

    quarter = S((256, FEAT), bf16)
    core_a, core_b, own_a, own_b, hid, gain_grad = pl.pallas_call(
        grad_kernel,
        out_shape=(
            quarter, quarter, S((256, FEAT), f32), S((256, FEAT), f32),
            pltpu.HBM((FEAT, 1024), bf16), S((1, FEAT), f32),
        ),
        in_specs=[ANY, HBM, HBM, VMEM],
        out_specs=(VMEM, VMEM, VMEM, VMEM, HBM, VMEM),
        scratch_shapes=[
            pltpu.VMEM((8, 1056, 128), bf16),
            pltpu.VMEM((FEAT, 1024), bf16),
            pltpu.VMEM((1024, FEAT), bf16),
            pltpu.VMEM((FEAT, 1024), bf16),
            pltpu.VMEM((2, 32, 2, 8, FEAT), f32),
            pltpu.SemaphoreType.DMA((4,)),
        ],
        compiler_params=PARAMS,
        name="grad",
    )(got, far(tok), far(weight), norm_gain)

    sibling_a = lax.ppermute(core_a, "core", SWAP)
    sibling_b = lax.ppermute(core_b, "core", SWAP)
    pair = pl.pallas_call(pair_kernel, out_shape=quarter, compiler_params=PARAMS, name="pair")(own_a, sibling_a)
    arrived = lax.ppermute(pair, "yl", SWAP)
    along = partial_keys((0,) + ALONG_X, hid, weight_t, pair, "keys_along")
    pieces = [lax.ppermute(piece, FSDP, partner(bit)) for bit, piece in zip(ALONG_X, along[1:])]
    share = pl.pallas_call(
        three_kernel,
        out_shape=quarter,
        in_specs=[VMEM, VMEM, VMEM, ANY],
        compiler_params=PARAMS,
        name="share",
    )(own_b, sibling_b, arrived, pieces[0])
    z_parts = lax.all_to_all(share.reshape(32, 8, FEAT), "z", 0, 0)
    across = partial_keys(ACROSS, hid, weight_t, share, "keys_across")
    pieces += [lax.ppermute(piece, FSDP, partner(bit)) for bit, piece in zip(ACROSS, across)]
    summed = jnp.sum(z_parts.astype(f32), axis=0)

    avg_grad = global_fragment - summed / N_REP
    new_momentum = outer_beta * outer_momentum + avg_grad
    new_global = global_fragment - outer_rate * (avg_grad + outer_beta * new_momentum)
    key_out = along[0].astype(f32)
    for piece in pieces:
        key_out += piece.astype(f32)
    return (key_out.astype(bf16), gain_grad, new_global, new_momentum)


def solution(mesh):
    fine = Mesh(mesh.devices.reshape(2, 32, 2, 4, 2), REP + FSDP)
    return jax.shard_map(
        per_device,
        mesh=fine,
        in_specs=(
            P(REP, FSDP),
            P(REP, FSDP),
            P(REP, None, FSDP),
            P(REP + FSDP, None),
            P(REP, FSDP),
            P(REP, FSDP),
        ),
        out_specs=(P(REP + FSDP, None), P(REP, FSDP), P(REP, FSDP), P(REP, FSDP)),
        check_vma=False,
    )
```

time: 179 us -> 145 us (0.81)
  the two profiles are of different devices: /device:TPU:1 before, /device:TPU:8 now
where the time goes in v5:
time: 145 us
  starting transfers between devices  68.9 us (48%)
  waiting for transfers between devices  59.4 us (41%)
  Pallas kernels  12.8 us (9%)
  other arithmetic  2.7 us (2%)
    all_to_all x1, waiting for transfers between devices, per_device(): got = lax.all_to_all(packed, FSDP, 0, 0)  30.6 us
    all_to_all x1, starting transfers between devices, per_device(): z_parts = lax.all_to_all(share.reshape(32, 8, FEAT), 'z', 0, 0)  29.9 us
    ppermute x7, starting transfers between devices, per_device(): lax.ppermute(piece, FSDP, partner(bit))  26.4 us
    ppermute x7, waiting for transfers between devices, per_device(): lax.ppermute(piece, FSDP, partner(bit))  17.2 us
    all_to_all x1, waiting for transfers between devices, per_device(): z_parts = lax.all_to_all(share.reshape(32, 8, FEAT), 'z', 0, 0)  11.5 us
    all_to_all x1, starting transfers between devices, per_device(): got = lax.all_to_all(packed, FSDP, 0, 0)  6.18 us
    pallas_call x1, Pallas kernels, per_device(): pl.pallas_call(grad_kernel, out_shape=(quarter, quarter, S((256, FEAT), f...  5.21 us
    pallas_call x1, Pallas kernels, per_device(): pl.pallas_call(pack_kernel, out_shape=pltpu.HBM((8, 1056, 128), bf16), in...  3.09 us
  transfers between devices with their start and end apart: 12, of which 4 were waited for; matrix products, arithmetic and copies ran while one was open for 1% of the time, Pallas kernels for 3%

profile of v5, /device:TPU:8, one launch (start us, length us, event | category | flops | bytes accessed | tf_op | source)
XLA Modules:
  0.0 144.6 jit_solution(15483436573803468398)
XLA Ops:
  0.6 3.1 %pack.1 = bf16[8,1056,128]{2,1,0:T(8,128)(2,1)} custom-call(bf16[128,1024]{1,0:T(8,128)(2,1)} %cot_hbm.1, bf16[576,1024]{1,0:T(8,128)(2,1)} %bitcast.8), custom_call_target="tpu_custom_call" | custom-call | tf_op jit(solution)/shard_map/pack/pallas_call | solution.py:150
  3.7 0.0 copy-start
  3.7 6.2 %all-to-all-start = ((bf16[8,1056,128]{2,1,0:T(8,128)(2,1)}), bf16[8,1056,128]{2,1,0:T(8,128)(2,1)S(1)}, u32[]{:S(2)}, u32[]{:S(2)}) async-start(bf16[8,1056,128]{2,1,0:T(8,128)(2,1)} %pack.1), calls=%async_computation | async-start | bytes 4325376 | tf_op jit(solution)/shard_map/all_to_all | solution.py:165
  9.9 0.0 copy-start.2
  9.9 0.0 copy-done
  9.9 1.5 %turn.1.w_ref = bf16[1024,576]{1,0:T(8,128)(2,1)} custom-call(bf16[576,1024]{1,0:T(8,128)(2,1)S(1)} %bitcast.5), custom_call_target="tpu_custom_call" | custom-call | flops 1000 | bytes 1000 | tf_op jit(solution)/shard_map/turn/pallas_call | solution.py:166
  11.4 30.6 %all-to-all-done.got_ref = bf16[8,1056,128]{2,1,0:T(8,128)(2,1)S(1)} async-done(((bf16[8,1056,128]{2,1,0:T(8,128)(2,1)}), bf16[8,1056,128]{2,1,0:T(8,128)(2,1)S(1)}, u32[]{:S(2)}, u32[]{:S(2)}) %all-to-all-start) | async-done | bytes 2162720 | tf_op jit(solution)/shard_map/all_to_all | solution.py:165
  42.0 0.0 copy-done.2
  42.0 5.2 %grad.1 = (bf16[256,576]{1,0:T(8,128)(2,1)S(1)}, bf16[256,576]{1,0:T(8,128)(2,1)S(1)}, f32[256,576]{1,0:T(8,128)S(1)}, f32[256,576]{1,0:T(8,128)S(1)}, bf16[576,1024]{1,0:T(8,128)(2,1)}, /*index=5*/f32[1,576]{1,0:T(1,128)}) custom-call(bf16[8,1056,128]{2,1,0:T(8,128)(2,1)S(1)} %all-to-all-done.got_ref, bf16[576,1024]{1,0:T(8,128)(2,1)} %bitcast.9, ...), custom_call_target="tpu_custom_call" | custom-call | tf_op jit(solution)/shard_map/grad/pallas_call | solution.py:176
  47.2 0.0 copy-start.1
  47.2 2.1 %collective-permute-start = (bf16[256,576]{1,0:T(8,128)(2,1)S(1)}, bf16[256,576]{1,0:T(8,128)(2,1)S(1)}, u32[]{:S(2)}, u32[]{:S(2)}) collective-permute-start(bf16[256,576]{1,0:T(8,128)(2,1)S(1)} %get-tuple-element.20), channel_id=1, source_target_pairs={{0,8},{8,0},{1,9},{9,1},{2,10},{10,2},{3,11},{11,3},{4,12},{12,4},... | collective-permute-start | bytes 884744 | tf_op jit(solution)/shard_map/ppermute | solution.py:196
  49.3 2.4 %collective-permute-start.4 = (bf16[256,576]{1,0:T(8,128)(2,1)S(1)}, bf16[256,576]{1,0:T(8,128)(2,1)S(1)}, u32[]{:S(2)}, u32[]{:S(2)}) collective-permute-start(bf16[256,576]{1,0:T(8,128)(2,1)S(1)} %get-tuple-element.26), channel_id=1, source_target_pairs={{0,8},{8,0},{1,9},{9,1},{2,10},{10,2},{3,11},{11,3},{4,12},{12,4},... | collective-permute-start | bytes 884744 | tf_op jit(solution)/shard_map/ppermute | solution.py:197
  51.7 0.0 collective-permute-done.sibling
  51.7 0.1 pair.1.after_ref
  51.8 1.9 %collective-permute-start.5 = (bf16[256,576]{1,0:T(8,128)(2,1)S(1)}, bf16[256,576]{1,0:T(8,128)(2,1)S(1)}, u32[]{:S(2)}, u32[]{:S(2)}) collective-permute-start(bf16[256,576]{1,0:T(8,128)(2,1)S(1)} %pair.1.after_ref), channel_id=1, source_target_pairs={{0,512},{512,0},{1,513},{513,1},{2,514},{514,2},{3,515},{515,3},{4... | collective-permute-start | bytes 884744 | tf_op jit(solution)/shard_map/ppermute | solution.py:199
  53.7 0.0 copy-done.1
  53.7 1.1 keys_along.1
  54.8 1.9 %collective-permute-start.1 = (bf16[128,1024]{1,0:T(8,128)(2,1)S(1)}, bf16[128,1024]{1,0:T(8,128)(2,1)S(1)}, u32[]{:S(2)}, u32[]{:S(2)}) collective-permute-start(bf16[128,1024]{1,0:T(8,128)(2,1)S(1)} %get-tuple-element.22), channel_id=1, source_target_pairs={{0,2},{1,3},{2,0},{3,1},{4,6},{5,7},{6,4},{7,5},{8,10},{9,11},{10,... | collective-permute-start | bytes 786440 | tf_op jit(solution)/shard_map/ppermute | solution.py:201
  56.7 0.0 collective-permute-done.4.sibling
  56.7 8.2 %collective-permute-done.1.after = bf16[128,1024]{1,0:T(8,128)(2,1)S(1)} collective-permute-done((bf16[128,1024]{1,0:T(8,128)(2,1)S(1)}, bf16[128,1024]{1,0:T(8,128)(2,1)S(1)}, u32[]{:S(2)}, u32[]{:S(2)}) %collective-permute-start.1) | collective-permute-done | bytes 262176 | tf_op jit(solution)/shard_map/ppermute | solution.py:201
  64.9 0.0 collective-permute-done.5.arrived
  64.9 0.8 share.1.after_ref
  65.8 29.9 %all-to-all-start.1 = ((bf16[32,8,576]{2,1,0:T(8,128)(2,1)}), bf16[32,8,576]{2,1,0:T(8,128)(2,1)}, u32[]{:S(2)}, u32[]{:S(2)}) async-start(bf16[32,8,576]{2,1,0:T(8,128)(2,1)} %bitcast.4), calls=%async_computation.1 | async-start | bytes 655360 | tf_op jit(solution)/shard_map/all_to_all | solution.py:209
  95.7 2.2 %collective-permute-start.2 = (bf16[128,1024]{1,0:T(8,128)(2,1)S(1)}, bf16[128,1024]{1,0:T(8,128)(2,1)S(1)}, u32[]{:S(2)}, u32[]{:S(2)}) collective-permute-start(bf16[128,1024]{1,0:T(8,128)(2,1)S(1)} %get-tuple-element.23), channel_id=1, source_target_pairs={{0,4},{1,5},{2,6},{3,7},{4,0},{5,1},{6,2},{7,3},{8,12},{9,13},{10,... | collective-permute-start | bytes 786440 | tf_op jit(solution)/shard_map/ppermute | solution.py:201
  97.9 4.6 %collective-permute-start.3 = (bf16[128,1024]{1,0:T(8,128)(2,1)S(1)}, bf16[128,1024]{1,0:T(8,128)(2,1)S(1)}, u32[]{:S(2)}, u32[]{:S(2)}) collective-permute-start(bf16[128,1024]{1,0:T(8,128)(2,1)S(1)} %get-tuple-element.24), channel_id=1, source_target_pairs={{0,6},{1,7},{2,4},{3,5},{4,2},{5,3},{6,0},{7,1},{8,14},{9,15},{10,... | collective-permute-start | bytes 786440 | tf_op jit(solution)/shard_map/ppermute | solution.py:201
  102.5 1.1 keys_across.1
  103.5 2.9 %collective-permute-start.6 = (bf16[128,1024]{1,0:T(8,128)(2,1)S(1)}, bf16[128,1024]{1,0:T(8,128)(2,1)S(1)}, u32[]{:S(2)}, u32[]{:S(2)}) collective-permute-start(bf16[128,1024]{1,0:T(8,128)(2,1)S(1)} %get-tuple-element.27), channel_id=1, source_target_pairs={{0,1},{1,0},{2,3},{3,2},{4,5},{5,4},{6,7},{7,6},{8,9},{9,8},{10,11... | collective-permute-start | bytes 786440 | tf_op jit(solution)/shard_map/ppermute | solution.py:211
  106.4 4.4 %collective-permute-start.7 = (bf16[128,1024]{1,0:T(8,128)(2,1)S(1)}, bf16[128,1024]{1,0:T(8,128)(2,1)S(1)}, u32[]{:S(2)}, u32[]{:S(2)}) collective-permute-start(bf16[128,1024]{1,0:T(8,128)(2,1)S(1)} %get-tuple-element.28), channel_id=1, source_target_pairs={{0,3},{1,2},{2,1},{3,0},{4,7},{5,6},{6,5},{7,4},{8,11},{9,10},{10,... | collective-permute-start | bytes 786440 | tf_op jit(solution)/shard_map/ppermute | solution.py:211
  110.9 3.9 %collective-permute-start.8 = (bf16[128,1024]{1,0:T(8,128)(2,1)S(1)}, bf16[128,1024]{1,0:T(8,128)(2,1)S(1)}, u32[]{:S(2)}, u32[]{:S(2)}) collective-permute-start(bf16[128,1024]{1,0:T(8,128)(2,1)S(1)} %get-tuple-element.29), channel_id=1, source_target_pairs={{0,5},{1,4},{2,7},{3,6},{4,1},{5,0},{6,3},{7,2},{8,13},{9,12},{10,... | collective-permute-start | bytes 786440 | tf_op jit(solution)/shard_map/ppermute | solution.py:211
  114.7 0.0 collective-permute-done.2
  114.8 6.5 %collective-permute-start.9 = (bf16[128,1024]{1,0:T(8,128)(2,1)S(1)}, bf16[128,1024]{1,0:T(8,128)(2,1)S(1)}, u32[]{:S(2)}, u32[]{:S(2)}) collective-permute-start(bf16[128,1024]{1,0:T(8,128)(2,1)S(1)} %get-tuple-element.30), channel_id=1, source_target_pairs={{0,7},{1,6},{2,5},{3,4},{4,3},{5,2},{6,1},{7,0},{8,15},{9,14},{10,... | collective-permute-start | bytes 786440 | tf_op jit(solution)/shard_map/ppermute | solution.py:211
  121.3 0.0 collective-permute-done.3
  121.3 9.0 %collective-permute-done.6 = bf16[128,1024]{1,0:T(8,128)(2,1)S(1)} collective-permute-done((bf16[128,1024]{1,0:T(8,128)(2,1)S(1)}, bf16[128,1024]{1,0:T(8,128)(2,1)S(1)}, u32[]{:S(2)}, u32[]{:S(2)}) %collective-permute-start.6) | collective-permute-done | bytes 262176 | tf_op jit(solution)/shard_map/ppermute | solution.py:211
  130.3 0.0 collective-permute-done.7
  130.3 0.0 collective-permute-done.8
  130.3 0.0 collective-permute-done.9
  130.3 0.0 copy-start.3
  130.3 0.0 copy-start.4
  130.3 1.0 add_convert_fusion
  131.4 11.5 %all-to-all-done.1 = bf16[32,8,576]{2,1,0:T(8,128)(2,1)} async-done(((bf16[32,8,576]{2,1,0:T(8,128)(2,1)}), bf16[32,8,576]{2,1,0:T(8,128)(2,1)}, u32[]{:S(2)}, u32[]{:S(2)}) %all-to-all-start.1) | async-done | bytes 294944 | tf_op jit(solution)/shard_map/all_to_all | solution.py:209
  142.9 1.0 convert_reduce_fusion
  144.0 0.0 copy-done.3
  144.0 0.0 copy-done.4
  144.0 0.6 multiply_subtract_fusion
Async XLA Ops:
  3.7 6.2 %copy-start = (bf16[1,1024,576]{1,2,0:T(8,128)(2,1)S(1)}, bf16[1,1024,576]{1,2,0:T(8,128)(2,1)}, u32[]{:S(2)}) copy-start(bf16[1,1024,576]{1,2,0:T(8,128)(2,1)} %param.8) | copy-start | bytes 3538948
  3.7 38.3 %all-to-all-start = ((bf16[8,1056,128]{2,1,0:T(8,128)(2,1)}), bf16[8,1056,128]{2,1,0:T(8,128)(2,1)S(1)}, u32[]{:S(2)}, u32[]{:S(2)}) async-start(bf16[8,1056,128]{2,1,0:T(8,128)(2,1)} %pack.1), calls=%async_computation | async-start | bytes 4325376 | tf_op jit(solution)/shard_map/all_to_all | solution.py:165
  9.9 32.1 %copy-start.2 = (bf16[1,576]{1,0:T(2,128)(2,1)S(1)}, bf16[1,576]{1,0:T(2,128)(2,1)}, u32[]{:S(2)}) copy-start(bf16[1,576]{1,0:T(2,128)(2,1)} %gain_ref.1) | copy-start | bytes 3460
  47.2 6.5 %copy-start.1 = (bf16[576,1024]{1,0:T(8,128)(2,1)S(1)}, bf16[576,1024]{1,0:T(8,128)(2,1)}, u32[]{:S(2)}) copy-start(bf16[576,1024]{1,0:T(8,128)(2,1)} %get-tuple-element.18.hid_ref) | copy-start | bytes 3538948
  47.2 4.5 %collective-permute-start = (bf16[256,576]{1,0:T(8,128)(2,1)S(1)}, bf16[256,576]{1,0:T(8,128)(2,1)S(1)}, u32[]{:S(2)}, u32[]{:S(2)}) collective-permute-start(bf16[256,576]{1,0:T(8,128)(2,1)S(1)} %get-tuple-element.20), channel_id=1, source_target_pairs={{0,8},{8,0},{1,9},{9,1},{2,10},{10,2},{3,11},{11,3},{4,12},{12,4},... | collective-permute-start | bytes 884744 | tf_op jit(solution)/shard_map/ppermute | solution.py:196
  49.3 7.4 %collective-permute-start.4 = (bf16[256,576]{1,0:T(8,128)(2,1)S(1)}, bf16[256,576]{1,0:T(8,128)(2,1)S(1)}, u32[]{:S(2)}, u32[]{:S(2)}) collective-permute-start(bf16[256,576]{1,0:T(8,128)(2,1)S(1)} %get-tuple-element.26), channel_id=1, source_target_pairs={{0,8},{8,0},{1,9},{9,1},{2,10},{10,2},{3,11},{11,3},{4,12},{12,4},... | collective-permute-start | bytes 884744 | tf_op jit(solution)/shard_map/ppermute | solution.py:197
  51.8 13.1 %collective-permute-start.5 = (bf16[256,576]{1,0:T(8,128)(2,1)S(1)}, bf16[256,576]{1,0:T(8,128)(2,1)S(1)}, u32[]{:S(2)}, u32[]{:S(2)}) collective-permute-start(bf16[256,576]{1,0:T(8,128)(2,1)S(1)} %pair.1.after_ref), channel_id=1, source_target_pairs={{0,512},{512,0},{1,513},{513,1},{2,514},{514,2},{3,515},{515,3},{4... | collective-permute-start | bytes 884744 | tf_op jit(solution)/shard_map/ppermute | solution.py:199
  54.8 10.1 %collective-permute-start.1 = (bf16[128,1024]{1,0:T(8,128)(2,1)S(1)}, bf16[128,1024]{1,0:T(8,128)(2,1)S(1)}, u32[]{:S(2)}, u32[]{:S(2)}) collective-permute-start(bf16[128,1024]{1,0:T(8,128)(2,1)S(1)} %get-tuple-element.22), channel_id=1, source_target_pairs={{0,2},{1,3},{2,0},{3,1},{4,6},{5,7},{6,4},{7,5},{8,10},{9,11},{10,... | collective-permute-start | bytes 786440 | tf_op jit(solution)/shard_map/ppermute | solution.py:201
  65.8 77.2 %all-to-all-start.1 = ((bf16[32,8,576]{2,1,0:T(8,128)(2,1)}), bf16[32,8,576]{2,1,0:T(8,128)(2,1)}, u32[]{:S(2)}, u32[]{:S(2)}) async-start(bf16[32,8,576]{2,1,0:T(8,128)(2,1)} %bitcast.4), calls=%async_computation.1 | async-start | bytes 655360 | tf_op jit(solution)/shard_map/all_to_all | solution.py:209
  95.7 19.1 %collective-permute-start.2 = (bf16[128,1024]{1,0:T(8,128)(2,1)S(1)}, bf16[128,1024]{1,0:T(8,128)(2,1)S(1)}, u32[]{:S(2)}, u32[]{:S(2)}) collective-permute-start(bf16[128,1024]{1,0:T(8,128)(2,1)S(1)} %get-tuple-element.23), channel_id=1, source_target_pairs={{0,4},{1,5},{2,6},{3,7},{4,0},{5,1},{6,2},{7,3},{8,12},{9,13},{10,... | collective-permute-start | bytes 786440 | tf_op jit(solution)/shard_map/ppermute | solution.py:201
  97.9 23.4 %collective-permute-start.3 = (bf16[128,1024]{1,0:T(8,128)(2,1)S(1)}, bf16[128,1024]{1,0:T(8,128)(2,1)S(1)}, u32[]{:S(2)}, u32[]{:S(2)}) collective-permute-start(bf16[128,1024]{1,0:T(8,128)(2,1)S(1)} %get-tuple-element.24), channel_id=1, source_target_pairs={{0,6},{1,7},{2,4},{3,5},{4,2},{5,3},{6,0},{7,1},{8,14},{9,15},{10,... | collective-permute-start | bytes 786440 | tf_op jit(solution)/shard_map/ppermute | solution.py:201
  103.5 26.8 %collective-permute-start.6 = (bf16[128,1024]{1,0:T(8,128)(2,1)S(1)}, bf16[128,1024]{1,0:T(8,128)(2,1)S(1)}, u32[]{:S(2)}, u32[]{:S(2)}) collective-permute-start(bf16[128,1024]{1,0:T(8,128)(2,1)S(1)} %get-tuple-element.27), channel_id=1, source_target_pairs={{0,1},{1,0},{2,3},{3,2},{4,5},{5,4},{6,7},{7,6},{8,9},{9,8},{10,11... | collective-permute-start | bytes 786440 | tf_op jit(solution)/shard_map/ppermute | solution.py:211
  106.4 23.9 %collective-permute-start.7 = (bf16[128,1024]{1,0:T(8,128)(2,1)S(1)}, bf16[128,1024]{1,0:T(8,128)(2,1)S(1)}, u32[]{:S(2)}, u32[]{:S(2)}) collective-permute-start(bf16[128,1024]{1,0:T(8,128)(2,1)S(1)} %get-tuple-element.28), channel_id=1, source_target_pairs={{0,3},{1,2},{2,1},{3,0},{4,7},{5,6},{6,5},{7,4},{8,11},{9,10},{10,... | collective-permute-start | bytes 786440 | tf_op jit(solution)/shard_map/ppermute | solution.py:211
  110.9 19.5 %collective-permute-start.8 = (bf16[128,1024]{1,0:T(8,128)(2,1)S(1)}, bf16[128,1024]{1,0:T(8,128)(2,1)S(1)}, u32[]{:S(2)}, u32[]{:S(2)}) collective-permute-start(bf16[128,1024]{1,0:T(8,128)(2,1)S(1)} %get-tuple-element.29), channel_id=1, source_target_pairs={{0,5},{1,4},{2,7},{3,6},{4,1},{5,0},{6,3},{7,2},{8,13},{9,12},{10,... | collective-permute-start | bytes 786440 | tf_op jit(solution)/shard_map/ppermute | solution.py:211
  114.8 15.6 %collective-permute-start.9 = (bf16[128,1024]{1,0:T(8,128)(2,1)S(1)}, bf16[128,1024]{1,0:T(8,128)(2,1)S(1)}, u32[]{:S(2)}, u32[]{:S(2)}) collective-permute-start(bf16[128,1024]{1,0:T(8,128)(2,1)S(1)} %get-tuple-element.30), channel_id=1, source_target_pairs={{0,7},{1,6},{2,5},{3,4},{4,3},{5,2},{6,1},{7,0},{8,15},{9,14},{10,... | collective-permute-start | bytes 786440 | tf_op jit(solution)/shard_map/ppermute | solution.py:211
  130.3 13.6 %copy-start.3 = (f32[8,576]{1,0:T(8,128)S(1)}, f32[8,576]{1,0:T(8,128)}, u32[]{:S(2)}) copy-start(f32[8,576]{1,0:T(8,128)} %param.10) | copy-start | bytes 55300
  130.3 13.6 %copy-start.4 = (f32[8,576]{1,0:T(8,128)S(1)}, f32[8,576]{1,0:T(8,128)}, u32[]{:S(2)}) copy-start(f32[8,576]{1,0:T(8,128)} %param.11) | copy-start | bytes 55300

commit v6 on v5

--- a/solution.py
+++ b/solution.py
@@ -1,5 +1,3 @@
-import functools
-
 import jax
 import jax.numpy as jnp
 from jax import lax
@@ -16,6 +14,7 @@
 outer_rate = 0.7
 outer_beta = 0.9
 
+ZC = ("z", "core")
 FSDP = ("x", "yh")
 REP = ("yl", "z", "core")
 SWAP = [(0, 1), (1, 0)]
@@ -35,12 +34,13 @@
     return pltpu.with_memory_space_constraint(array, pltpu.HBM)
 
 
-ALONG_X = (2, 4, 6)
-ACROSS = (1, 3, 5, 7)
-
-
-def partner(bits):
-    return [(i, i ^ bits) for i in range(8)]
+def ahead(first, second):
+    pairs = []
+    for z in range(32):
+        for core, step in ((0, first), (1, second)):
+            if step is not None:
+                pairs.append((z * 2 + core, (z + (1 - 2 * core) * step) % 32 * 2 + core))
+    return pairs
 
 
 def pack_kernel(cot_hbm, tok_hbm, out_ref, cot, tok, buffer, sems, in_sems):
@@ -108,11 +108,15 @@
     copies[2].wait()
     w = weight[...].astype(f32)
     gain_grad_ref[...] = jnp.sum(w * grad, axis=0, keepdims=True) / gain_row
-    total[...] = (w - inner_rate * grad).reshape(2, 32, 2, 8, FEAT)
-    core_a_ref[...] = total[1 - yl, :, 1 - core].reshape(256, FEAT).astype(bf16)
-    core_b_ref[...] = total[yl, :, 1 - core].reshape(256, FEAT).astype(bf16)
-    own_a_ref[...] = total[1 - yl, :, core].reshape(256, FEAT)
-    own_b_ref[...] = total[yl, :, core].reshape(256, FEAT)
+    total[...] = (w - inner_rate * grad).reshape(2, 32, 16, FEAT)
+    z = lax.axis_index("z")
+    for t in range(16):
+        own = (z + (1 - 2 * core) * t - core + 64) % 32
+        sibling = (z + (2 * core - 1) * t - (1 - core) + 64) % 32
+        core_a_ref[t] = total[1 - yl, sibling].astype(bf16)
+        core_b_ref[t] = total[yl, sibling].astype(bf16)
+        own_a_ref[t] = total[1 - yl, own]
+        own_b_ref[t] = total[yl, own]
     hid_copy.wait()
 
 
@@ -120,28 +124,49 @@
     out[...] = (own[...] + sibling[...].astype(f32)).astype(bf16)
 
 
-def three_kernel(own, sibling, arrived, after, out):
-    out[...] = (own[...] + sibling[...].astype(f32) + arrived[...].astype(f32)).astype(bf16)
-
-
-def keys_kernel(bits, hid_ref, wt_ref, after_ref, *outs):
-    me = lax.axis_index("x") * 2 + lax.axis_index("yh")
-    for bit, out in zip(bits, outs):
-        group = me ^ bit
-        hid = hid_ref[:, pl.ds(pl.multiple_of(group * 128, 128), 128)]
-        out[...] = lax.dot_general(
+def halve(total, keep, send):
+    for i in range(total.shape[0] // 2):
+        keep[i] = total[2 * i]
+        send[i] = total[2 * i + 1].astype(bf16)
+
+
+def share_kernel(own, sibling, arrived, keep, send):
+    halve(own[...] + sibling[...].astype(f32) + arrived[...].astype(f32), keep, send)
+
+
+def fold_kernel(kept, arrived, keep, send):
+    halve(kept[...] + arrived[...].astype(f32), keep, send)
+
+
+def end_kernel(kept, arrived, near_by, mine, other, total):
+    core = lax.axis_index("core")
+    held = kept[0] * (1 - core).astype(f32)
+    both = held + arrived[0].astype(f32) + near_by[0].astype(f32)
+    total[...] = both.reshape(2, 8, FEAT)
+    mine[...] = total[core]
+    other[...] = total[1 - core]
+
+
+def fold(kept, arrived):
+    n = kept.shape[0] // 2
+    return pl.pallas_call(
+        fold_kernel,
+        out_shape=(S((n, 16, FEAT), f32), S((n, 16, FEAT), bf16)),
+        compiler_params=PARAMS,
+        name="fold",
+    )(kept, arrived)
+
+
+def keys_kernel(hid_ref, wt_ref, after_ref, out_ref):
+    for group in range(8):
+        hid = hid_ref[:, group * 128 : (group + 1) * 128]
+        out_ref[group] = lax.dot_general(
             hid, wt_ref[...], (((0,), (0,)), ((), ())), preferred_element_type=f32
         ).astype(bf16)
 
 
-def partial_keys(bits, hid, weight_t, after, name):
-    return pl.pallas_call(
-        functools.partial(keys_kernel, bits),
-        out_shape=tuple(S((128, 1024), bf16) for _ in bits),
-        in_specs=[VMEM, VMEM, ANY],
-        compiler_params=PARAMS,
-        name=name,
-    )(hid, weight_t, after)
+def pass_kernel(array, after, out):
+    pass
 
 
 def per_device(tokens, norm_gain, key_weight, key_cotangent, global_fragment, outer_momentum):
@@ -172,11 +197,12 @@
         name="turn",
     )(weight_t)
 
-    quarter = S((256, FEAT), bf16)
+    quarter = S((16, 16, FEAT), bf16)
+    quarter_wide = S((16, 16, FEAT), f32)
     core_a, core_b, own_a, own_b, hid, gain_grad = pl.pallas_call(
         grad_kernel,
         out_shape=(
-            quarter, quarter, S((256, FEAT), f32), S((256, FEAT), f32),
+            quarter, quarter, quarter_wide, quarter_wide,
             pltpu.HBM((FEAT, 1024), bf16), S((1, FEAT), f32),
         ),
         in_specs=[ANY, HBM, HBM, VMEM],
@@ -186,7 +212,7 @@
             pltpu.VMEM((FEAT, 1024), bf16),
             pltpu.VMEM((1024, FEAT), bf16),
             pltpu.VMEM((FEAT, 1024), bf16),
-            pltpu.VMEM((2, 32, 2, 8, FEAT), f32),
+            pltpu.VMEM((2, 32, 16, FEAT), f32),
             pltpu.SemaphoreType.DMA((4,)),
         ],
         compiler_params=PARAMS,
@@ -197,26 +223,48 @@
     sibling_b = lax.ppermute(core_b, "core", SWAP)
     pair = pl.pallas_call(pair_kernel, out_shape=quarter, compiler_params=PARAMS, name="pair")(own_a, sibling_a)
     arrived = lax.ppermute(pair, "yl", SWAP)
-    along = partial_keys((0,) + ALONG_X, hid, weight_t, pair, "keys_along")
-    pieces = [lax.ppermute(piece, FSDP, partner(bit)) for bit, piece in zip(ALONG_X, along[1:])]
-    share = pl.pallas_call(
-        three_kernel,
-        out_shape=quarter,
-        in_specs=[VMEM, VMEM, VMEM, ANY],
+    keys = pl.pallas_call(
+        keys_kernel,
+        out_shape=pltpu.HBM((8, 128, 1024), bf16),
+        in_specs=[VMEM, VMEM, ANY],
+        out_specs=VMEM,
+        compiler_params=PARAMS,
+        name="keys",
+    )(hid, weight_t, pair)
+
+    keep, send = pl.pallas_call(
+        share_kernel,
+        out_shape=(S((8, 16, FEAT), f32), S((8, 16, FEAT), bf16)),
         compiler_params=PARAMS,
         name="share",
-    )(own_b, sibling_b, arrived, pieces[0])
-    z_parts = lax.all_to_all(share.reshape(32, 8, FEAT), "z", 0, 0)
-    across = partial_keys(ACROSS, hid, weight_t, share, "keys_across")
-    pieces += [lax.ppermute(piece, FSDP, partner(bit)) for bit, piece in zip(ACROSS, across)]
-    summed = jnp.sum(z_parts.astype(f32), axis=0)
+    )(own_b, sibling_b, arrived)
+    keys = pl.pallas_call(
+        pass_kernel,
+        out_shape=pltpu.HBM((8, 128, 1024), bf16),
+        in_specs=[HBM, ANY],
+        out_specs=HBM,
+        input_output_aliases={0: 0},
+        compiler_params=PARAMS,
+        name="pass_on",
+    )(keys, send)
+    key_parts = lax.all_to_all(keys, FSDP, 0, 0)
+    for step in (1, 2, 4):
+        keep, send = fold(keep, lax.ppermute(send, ZC, ahead(step, step)))
+    near_by = lax.ppermute(keep.astype(bf16), ZC, ahead(None, 1))
+    arrived = lax.ppermute(send, ZC, ahead(8, 9))
+    mine, other = pl.pallas_call(
+        end_kernel,
+        out_shape=(S((8, FEAT), f32), S((8, FEAT), f32)),
+        scratch_shapes=[pltpu.VMEM((2, 8, FEAT), f32)],
+        compiler_params=PARAMS,
+        name="end",
+    )(keep, arrived, near_by)
+    summed = mine + lax.ppermute(other, "core", SWAP)
 
     avg_grad = global_fragment - summed / N_REP
     new_momentum = outer_beta * outer_momentum + avg_grad
     new_global = global_fragment - outer_rate * (avg_grad + outer_beta * new_momentum)
-    key_out = along[0].astype(f32)
-    for piece in pieces:
-        key_out += piece.astype(f32)
+    key_out = jnp.sum(key_parts.astype(f32), axis=0)
     return (key_out.astype(bf16), gain_grad, new_global, new_momentum)
 
 

time: 145 us -> 131 us (0.903)
  the two profiles are of different devices: /device:TPU:8 before, /device:TPU:1 now
where the time goes in v6:
time: 131 us
  starting transfers between devices  77.6 us (59%)
  waiting for transfers between devices  37.5 us (29%)
  Pallas kernels  13.2 us (10%)
  other arithmetic  1.73 us (1%)
    ppermute x3, starting transfers between devices, per_device(): keep, send = fold(keep, lax.ppermute(send, ZC, ahead(step, step)))  29.8 us
    all_to_all x1, waiting for transfers between devices, per_device(): got = lax.all_to_all(packed, FSDP, 0, 0)  20.1 us
    ppermute x1, starting transfers between devices, per_device(): sibling_a = lax.ppermute(core_a, 'core', SWAP)  10.8 us
    ppermute x1, starting transfers between devices, per_device(): arrived = lax.ppermute(send, ZC, ahead(8, 9))  8.34 us
    all_to_all x1, starting transfers between devices, per_device(): got = lax.all_to_all(packed, FSDP, 0, 0)  7.62 us
    ppermute x1, starting transfers between devices, per_device(): near_by = lax.ppermute(keep.astype(bf16), ZC, ahead(None, 1))  6.82 us
    ppermute x3, waiting for transfers between devices, per_device(): keep, send = fold(keep, lax.ppermute(send, ZC, ahead(step, step)))  6.38 us
    ppermute x1, waiting for transfers between devices, per_device(): arrived = lax.ppermute(send, ZC, ahead(8, 9))  5.78 us
  transfers between devices with their start and end apart: 11, of which 7 were waited for; matrix products, arithmetic and copies ran while one was open for 0% of the time, Pallas kernels for 4%

profile of v6, /device:TPU:1, one launch (start us, length us, event | category | flops | bytes accessed | tf_op | source)
XLA Modules:
  0.0 130.9 jit_solution(3337720688268028625)
XLA Ops:
  0.6 3.1 %pack.1 = bf16[8,1056,128]{2,1,0:T(8,128)(2,1)} custom-call(bf16[128,1024]{1,0:T(8,128)(2,1)} %cot_hbm.1, bf16[576,1024]{1,0:T(8,128)(2,1)} %bitcast.6), custom_call_target="tpu_custom_call" | custom-call | tf_op jit(solution)/shard_map/pack/pallas_call | solution.py:175
  3.7 0.0 copy-start
  3.7 7.6 %all-to-all-start = ((bf16[8,1056,128]{2,1,0:T(8,128)(2,1)}), bf16[8,1056,128]{2,1,0:T(8,128)(2,1)S(1)}, u32[]{:S(2)}, u32[]{:S(2)}) async-start(bf16[8,1056,128]{2,1,0:T(8,128)(2,1)} %pack.1), calls=%async_computation | async-start | bytes 4325376 | tf_op jit(solution)/shard_map/all_to_all | solution.py:190
  11.4 0.0 copy-start.2
  11.4 0.0 copy-done
  11.4 1.5 %turn.1.w_ref = bf16[1024,576]{1,0:T(8,128)(2,1)} custom-call(bf16[576,1024]{1,0:T(8,128)(2,1)S(1)} %bitcast.4), custom_call_target="tpu_custom_call" | custom-call | flops 1000 | bytes 1000 | tf_op jit(solution)/shard_map/turn/pallas_call | solution.py:191
  12.9 20.1 %all-to-all-done.got_ref = bf16[8,1056,128]{2,1,0:T(8,128)(2,1)S(1)} async-done(((bf16[8,1056,128]{2,1,0:T(8,128)(2,1)}), bf16[8,1056,128]{2,1,0:T(8,128)(2,1)S(1)}, u32[]{:S(2)}, u32[]{:S(2)}) %all-to-all-start) | async-done | bytes 2162720 | tf_op jit(solution)/shard_map/all_to_all | solution.py:190
  32.9 0.0 copy-done.2
  32.9 5.2 %grad.1 = (bf16[16,16,576]{2,1,0:T(8,128)(2,1)S(1)}, bf16[16,16,576]{2,1,0:T(8,128)(2,1)S(1)}, f32[16,16,576]{2,1,0:T(8,128)S(1)}, f32[16,16,576]{2,1,0:T(8,128)...) custom-call(bf16[8,1056,128]{2,1,0:T(8,128)(2,1)S(1)} %all-to-all-done.got_ref, bf16[576,1024]{1,0:T(8,128)(2,1)} %bitcast.7, ...), custom_call_target="tpu_custom_call" | custom-call | tf_op jit(solution)/shard_map/grad/pallas_call | solution.py:202
  38.2 0.0 copy-start.1
  38.2 10.8 %collective-permute-start = (bf16[16,16,576]{2,1,0:T(8,128)(2,1)S(1)}, bf16[16,16,576]{2,1,0:T(8,128)(2,1)S(1)}, u32[]{:S(2)}, u32[]{:S(2)}) collective-permute-start(bf16[16,16,576]{2,1,0:T(8,128)(2,1)S(1)} %get-tuple-element.22), channel_id=1, source_target_pairs={{0,8},{8,0},{1,9},{9,1},{2,10},{10,2},{3,11},{11,3},{4,12},{12,4},... | collective-permute-start | bytes 884744 | tf_op jit(solution)/shard_map/ppermute | solution.py:222
  49.0 1.9 %collective-permute-start.1 = (bf16[16,16,576]{2,1,0:T(8,128)(2,1)S(1)}, bf16[16,16,576]{2,1,0:T(8,128)(2,1)S(1)}, u32[]{:S(2)}, u32[]{:S(2)}) collective-permute-start(bf16[16,16,576]{2,1,0:T(8,128)(2,1)S(1)} %get-tuple-element.24), channel_id=1, source_target_pairs={{0,8},{8,0},{1,9},{9,1},{2,10},{10,2},{3,11},{11,3},{4,12},{12,4},... | collective-permute-start | bytes 884744 | tf_op jit(solution)/shard_map/ppermute | solution.py:223
  51.0 0.0 collective-permute-done.sibling
  51.0 0.1 pair.1.after_ref
  51.0 5.0 %collective-permute-start.2 = (bf16[16,16,576]{2,1,0:T(8,128)(2,1)S(1)}, bf16[16,16,576]{2,1,0:T(8,128)(2,1)S(1)}, u32[]{:S(2)}, u32[]{:S(2)}) collective-permute-start(bf16[16,16,576]{2,1,0:T(8,128)(2,1)S(1)} %pair.1.after_ref), channel_id=1, source_target_pairs={{0,512},{512,0},{1,513},{513,1},{2,514},{514,2},{3,515},{515,3},{4... | collective-permute-start | bytes 884744 | tf_op jit(solution)/shard_map/ppermute | solution.py:225
  56.0 0.0 copy-done.1
  56.0 3.2 %keys.1.array = bf16[8,128,1024]{2,1,0:T(8,128)(2,1)} custom-call(bf16[576,1024]{1,0:T(8,128)(2,1)S(1)} %copy-done.1, bf16[576,1024]{1,0:T(8,128)(2,1)S(1)} %bitcast.5, bf16[16,16,576]{2,1,0:T(8,128)(2,1)S(1)} %pair.1.after_ref), custom_call_target="tpu_custom_call" | custom-call | tf_op jit(solution)/shard_map/keys/pallas_call | solution.py:226
  59.2 0.0 collective-permute-done.1.sibling
  59.2 4.4 %collective-permute-done.2.arrived = bf16[16,16,576]{2,1,0:T(8,128)(2,1)S(1)} collective-permute-done((bf16[16,16,576]{2,1,0:T(8,128)(2,1)S(1)}, bf16[16,16,576]{2,1,0:T(8,128)(2,1)S(1)}, u32[]{:S(2)}, u32[]{:S(2)}) %collective-permute-start.2) | collective-permute-done | bytes 294944 | tf_op jit(solution)/shard_map/ppermute | solution.py:225
  63.6 0.1 share.1
  63.8 0.0 copy-start.3
  63.8 0.0 copy-start.4
  63.8 3.8 %all-to-all-start.1 = ((bf16[8,128,1024]{2,1,0:T(8,128)(2,1)}), bf16[8,128,1024]{2,1,0:T(8,128)(2,1)S(1)}, u32[]{:S(2)}, u32[]{:S(2)}) async-start(bf16[8,128,1024]{2,1,0:T(8,128)(2,1)} %pass_on.1), calls=%async_computation.1 | async-start | bytes 4194304 | tf_op jit(solution)/shard_map/all_to_all | solution.py:250
  67.6 18.9 %collective-permute-start.3 = (bf16[8,16,576]{2,1,0:T(8,128)(2,1)S(1)}, bf16[8,16,576]{2,1,0:T(8,128)(2,1)S(1)}, u32[]{:S(2)}, u32[]{:S(2)}) collective-permute-start(bf16[8,16,576]{2,1,0:T(8,128)(2,1)S(1)} %get-tuple-element.25.after), channel_id=1, source_target_pairs={{0,16},{8,504},{16,32},{24,8},{32,48},{40,24},{48,64},{56,40},{64,... | collective-permute-start | bytes 442376 | tf_op jit(solution)/shard_map/ppermute | solution.py:252
  86.5 2.2 %collective-permute-done.3.arrived = bf16[8,16,576]{2,1,0:T(8,128)(2,1)S(1)} collective-permute-done((bf16[8,16,576]{2,1,0:T(8,128)(2,1)S(1)}, bf16[8,16,576]{2,1,0:T(8,128)(2,1)S(1)}, u32[]{:S(2)}, u32[]{:S(2)}) %collective-permute-start.3) | collective-permute-done | bytes 147488 | tf_op jit(solution)/shard_map/ppermute | solution.py:252
  88.8 4.6 %collective-permute-start.4 = (bf16[4,16,576]{2,1,0:T(8,128)(2,1)S(1)}, bf16[4,16,576]{2,1,0:T(8,128)(2,1)S(1)}, u32[]{:S(2)}, u32[]{:S(2)}) collective-permute-start(bf16[4,16,576]{2,1,0:T(8,128)(2,1)S(1)} %get-tuple-element.29), channel_id=1, source_target_pairs={{0,32},{8,488},{16,48},{24,504},{32,64},{40,8},{48,80},{56,24},{64... | collective-permute-start | bytes 221192 | tf_op jit(solution)/shard_map/ppermute | solution.py:252
  93.4 1.8 %collective-permute-done.4.arrived = bf16[4,16,576]{2,1,0:T(8,128)(2,1)S(1)} collective-permute-done((bf16[4,16,576]{2,1,0:T(8,128)(2,1)S(1)}, bf16[4,16,576]{2,1,0:T(8,128)(2,1)S(1)}, u32[]{:S(2)}, u32[]{:S(2)}) %collective-permute-start.4) | collective-permute-done | bytes 73760 | tf_op jit(solution)/shard_map/ppermute | solution.py:252
  95.2 6.3 %collective-permute-start.5 = (bf16[2,16,576]{2,1,0:T(8,128)(2,1)S(1)}, bf16[2,16,576]{2,1,0:T(8,128)(2,1)S(1)}, u32[]{:S(2)}, u32[]{:S(2)}) collective-permute-start(bf16[2,16,576]{2,1,0:T(8,128)(2,1)S(1)} %get-tuple-element.31), channel_id=1, source_target_pairs={{0,64},{8,456},{16,80},{24,472},{32,96},{40,488},{48,112},{56,504}... | collective-permute-start | bytes 110600 | tf_op jit(solution)/shard_map/ppermute | solution.py:252
  101.5 2.3 %collective-permute-done.5.arrived = bf16[2,16,576]{2,1,0:T(8,128)(2,1)S(1)} collective-permute-done((bf16[2,16,576]{2,1,0:T(8,128)(2,1)S(1)}, bf16[2,16,576]{2,1,0:T(8,128)(2,1)S(1)}, u32[]{:S(2)}, u32[]{:S(2)}) %collective-permute-start.5) | collective-permute-done | bytes 36896 | tf_op jit(solution)/shard_map/ppermute | solution.py:252
  103.9 6.8 %collective-permute-start.7 = (bf16[1,16,576]{2,1,0:T(8,128)(2,1)S(1)}, bf16[1,16,576]{2,1,0:T(8,128)(2,1)S(1)}, u32[]{:S(2)}, u32[]{:S(2)}) collective-permute-start(bf16[1,16,576]{2,1,0:T(8,128)(2,1)S(1)} %convert_element_type.2), channel_id=1, source_target_pairs={{8,504},{24,8},{40,24},{56,40},{72,56},{88,72},{104,88},{120,104},... | collective-permute-start | bytes 55304 | tf_op jit(solution)/shard_map/ppermute | solution.py:253
  110.7 8.3 %collective-permute-start.6 = (bf16[1,16,576]{2,1,0:T(8,128)(2,1)S(1)}, bf16[1,16,576]{2,1,0:T(8,128)(2,1)S(1)}, u32[]{:S(2)}, u32[]{:S(2)}) collective-permute-start(bf16[1,16,576]{2,1,0:T(8,128)(2,1)S(1)} %get-tuple-element.33), channel_id=1, source_target_pairs={{0,128},{8,376},{16,144},{24,392},{32,160},{40,408},{48,176},{56,4... | collective-permute-start | bytes 55304 | tf_op jit(solution)/shard_map/ppermute | solution.py:254
  119.1 0.0 collective-permute-done.7.near_by
  119.1 5.8 %collective-permute-done.6.arrived = bf16[1,16,576]{2,1,0:T(8,128)(2,1)S(1)} collective-permute-done((bf16[1,16,576]{2,1,0:T(8,128)(2,1)S(1)}, bf16[1,16,576]{2,1,0:T(8,128)(2,1)S(1)}, u32[]{:S(2)}, u32[]{:S(2)}) %collective-permute-start.6) | collective-permute-done | bytes 18464 | tf_op jit(solution)/shard_map/ppermute | solution.py:254
  124.9 3.4 %collective-permute-start.8 = (f32[8,576]{1,0:T(8,128)S(1)}, f32[8,576]{1,0:T(8,128)S(1)}, u32[]{:S(2)}, u32[]{:S(2)}) collective-permute-start(f32[8,576]{1,0:T(8,128)S(1)} %get-tuple-element.35), channel_id=1, source_target_pairs={{0,8},{8,0},{1,9},{9,1},{2,10},{10,2},{3,11},{11,3},{4,12},{12,4},... | collective-permute-start | bytes 55304 | tf_op jit(solution)/shard_map/ppermute | solution.py:262
  128.3 0.8 collective-permute-done.8
  129.1 0.0 copy-done.3
  129.1 0.0 copy-done.4
  129.2 0.6 multiply_subtract_fusion
  129.8 0.0 all-to-all-done.1
  129.8 1.1 reduce_sum.12
  (6 shorter events, 0.1 us)
Async XLA Ops:
  3.7 7.6 %copy-start = (bf16[1,1024,576]{1,2,0:T(8,128)(2,1)S(1)}, bf16[1,1024,576]{1,2,0:T(8,128)(2,1)}, u32[]{:S(2)}) copy-start(bf16[1,1024,576]{1,2,0:T(8,128)(2,1)} %param.8) | copy-start | bytes 3538948
  3.7 29.2 %all-to-all-start = ((bf16[8,1056,128]{2,1,0:T(8,128)(2,1)}), bf16[8,1056,128]{2,1,0:T(8,128)(2,1)S(1)}, u32[]{:S(2)}, u32[]{:S(2)}) async-start(bf16[8,1056,128]{2,1,0:T(8,128)(2,1)} %pack.1), calls=%async_computation | async-start | bytes 4325376 | tf_op jit(solution)/shard_map/all_to_all | solution.py:190
  11.4 21.6 %copy-start.2 = (bf16[1,576]{1,0:T(2,128)(2,1)S(1)}, bf16[1,576]{1,0:T(2,128)(2,1)}, u32[]{:S(2)}) copy-start(bf16[1,576]{1,0:T(2,128)(2,1)} %gain_ref.1) | copy-start | bytes 3460
  38.2 17.9 %copy-start.1 = (bf16[576,1024]{1,0:T(8,128)(2,1)S(1)}, bf16[576,1024]{1,0:T(8,128)(2,1)}, u32[]{:S(2)}) copy-start(bf16[576,1024]{1,0:T(8,128)(2,1)} %get-tuple-element.20.hid_ref) | copy-start | bytes 3538948
  38.2 12.8 %collective-permute-start = (bf16[16,16,576]{2,1,0:T(8,128)(2,1)S(1)}, bf16[16,16,576]{2,1,0:T(8,128)(2,1)S(1)}, u32[]{:S(2)}, u32[]{:S(2)}) collective-permute-start(bf16[16,16,576]{2,1,0:T(8,128)(2,1)S(1)} %get-tuple-element.22), channel_id=1, source_target_pairs={{0,8},{8,0},{1,9},{9,1},{2,10},{10,2},{3,11},{11,3},{4,12},{12,4},... | collective-permute-start | bytes 884744 | tf_op jit(solution)/shard_map/ppermute | solution.py:222
  49.0 10.2 %collective-permute-start.1 = (bf16[16,16,576]{2,1,0:T(8,128)(2,1)S(1)}, bf16[16,16,576]{2,1,0:T(8,128)(2,1)S(1)}, u32[]{:S(2)}, u32[]{:S(2)}) collective-permute-start(bf16[16,16,576]{2,1,0:T(8,128)(2,1)S(1)} %get-tuple-element.24), channel_id=1, source_target_pairs={{0,8},{8,0},{1,9},{9,1},{2,10},{10,2},{3,11},{11,3},{4,12},{12,4},... | collective-permute-start | bytes 884744 | tf_op jit(solution)/shard_map/ppermute | solution.py:223
  51.0 12.6 %collective-permute-start.2 = (bf16[16,16,576]{2,1,0:T(8,128)(2,1)S(1)}, bf16[16,16,576]{2,1,0:T(8,128)(2,1)S(1)}, u32[]{:S(2)}, u32[]{:S(2)}) collective-permute-start(bf16[16,16,576]{2,1,0:T(8,128)(2,1)S(1)} %pair.1.after_ref), channel_id=1, source_target_pairs={{0,512},{512,0},{1,513},{513,1},{2,514},{514,2},{3,515},{515,3},{4... | collective-permute-start | bytes 884744 | tf_op jit(solution)/shard_map/ppermute | solution.py:225
  63.8 65.4 %copy-start.3 = (f32[8,576]{1,0:T(8,128)S(1)}, f32[8,576]{1,0:T(8,128)}, u32[]{:S(2)}) copy-start(f32[8,576]{1,0:T(8,128)} %param.10) | copy-start | bytes 55300
  63.8 65.4 %copy-start.4 = (f32[8,576]{1,0:T(8,128)S(1)}, f32[8,576]{1,0:T(8,128)}, u32[]{:S(2)}) copy-start(f32[8,576]{1,0:T(8,128)} %param.11) | copy-start | bytes 55300
  63.8 66.0 %all-to-all-start.1 = ((bf16[8,128,1024]{2,1,0:T(8,128)(2,1)}), bf16[8,128,1024]{2,1,0:T(8,128)(2,1)S(1)}, u32[]{:S(2)}, u32[]{:S(2)}) async-start(bf16[8,128,1024]{2,1,0:T(8,128)(2,1)} %pass_on.1), calls=%async_computation.1 | async-start | bytes 4194304 | tf_op jit(solution)/shard_map/all_to_all | solution.py:250
  67.6 21.2 %collective-permute-start.3 = (bf16[8,16,576]{2,1,0:T(8,128)(2,1)S(1)}, bf16[8,16,576]{2,1,0:T(8,128)(2,1)S(1)}, u32[]{:S(2)}, u32[]{:S(2)}) collective-permute-start(bf16[8,16,576]{2,1,0:T(8,128)(2,1)S(1)} %get-tuple-element.25.after), channel_id=1, source_target_pairs={{0,16},{8,504},{16,32},{24,8},{32,48},{40,24},{48,64},{56,40},{64,... | collective-permute-start | bytes 442376 | tf_op jit(solution)/shard_map/ppermute | solution.py:252
  88.8 6.4 %collective-permute-start.4 = (bf16[4,16,576]{2,1,0:T(8,128)(2,1)S(1)}, bf16[4,16,576]{2,1,0:T(8,128)(2,1)S(1)}, u32[]{:S(2)}, u32[]{:S(2)}) collective-permute-start(bf16[4,16,576]{2,1,0:T(8,128)(2,1)S(1)} %get-tuple-element.29), channel_id=1, source_target_pairs={{0,32},{8,488},{16,48},{24,504},{32,64},{40,8},{48,80},{56,24},{64... | collective-permute-start | bytes 221192 | tf_op jit(solution)/shard_map/ppermute | solution.py:252
  95.2 8.7 %collective-permute-start.5 = (bf16[2,16,576]{2,1,0:T(8,128)(2,1)S(1)}, bf16[2,16,576]{2,1,0:T(8,128)(2,1)S(1)}, u32[]{:S(2)}, u32[]{:S(2)}) collective-permute-start(bf16[2,16,576]{2,1,0:T(8,128)(2,1)S(1)} %get-tuple-element.31), channel_id=1, source_target_pairs={{0,64},{8,456},{16,80},{24,472},{32,96},{40,488},{48,112},{56,504}... | collective-permute-start | bytes 110600 | tf_op jit(solution)/shard_map/ppermute | solution.py:252
  103.9 15.2 %collective-permute-start.7 = (bf16[1,16,576]{2,1,0:T(8,128)(2,1)S(1)}, bf16[1,16,576]{2,1,0:T(8,128)(2,1)S(1)}, u32[]{:S(2)}, u32[]{:S(2)}) collective-permute-start(bf16[1,16,576]{2,1,0:T(8,128)(2,1)S(1)} %convert_element_type.2), channel_id=1, source_target_pairs={{8,504},{24,8},{40,24},{56,40},{72,56},{88,72},{104,88},{120,104},... | collective-permute-start | bytes 55304 | tf_op jit(solution)/shard_map/ppermute | solution.py:253
  110.7 14.1 %collective-permute-start.6 = (bf16[1,16,576]{2,1,0:T(8,128)(2,1)S(1)}, bf16[1,16,576]{2,1,0:T(8,128)(2,1)S(1)}, u32[]{:S(2)}, u32[]{:S(2)}) collective-permute-start(bf16[1,16,576]{2,1,0:T(8,128)(2,1)S(1)} %get-tuple-element.33), channel_id=1, source_target_pairs={{0,128},{8,376},{16,144},{24,392},{32,160},{40,408},{48,176},{56,4... | collective-permute-start | bytes 55304 | tf_op jit(solution)/shard_map/ppermute | solution.py:254
  124.9 4.3 %collective-permute-start.8 = (f32[8,576]{1,0:T(8,128)S(1)}, f32[8,576]{1,0:T(8,128)S(1)}, u32[]{:S(2)}, u32[]{:S(2)}) collective-permute-start(f32[8,576]{1,0:T(8,128)S(1)} %get-tuple-element.35), channel_id=1, source_target_pairs={{0,8},{8,0},{1,9},{9,1},{2,10},{10,2},{3,11},{11,3},{4,12},{12,4},... | collective-permute-start | bytes 55304 | tf_op jit(solution)/shard_map/ppermute | solution.py:262

commit v7 on v6

--- a/solution.py
+++ b/solution.py
@@ -25,6 +25,7 @@
 
 
 HBM = pl.BlockSpec(memory_space=pltpu.HBM)
+LONG = 100 * 10**9
 CHEAP = pl.CostEstimate(flops=1000, bytes_accessed=1000, transcendentals=0)
 ANY = pl.BlockSpec(memory_space=pl.ANY)
 VMEM = pl.BlockSpec(memory_space=pltpu.VMEM)
@@ -43,13 +44,14 @@
     return pairs
 
 
-def pack_kernel(cot_hbm, tok_hbm, out_ref, cot, tok, buffer, sems, in_sems):
+def pack_kernel(cot_hbm, tok_hbm, out_ref, cot, tok, buffer, last, sems, tail_sems, in_sems):
     cot_copy = pltpu.make_async_copy(cot_hbm, cot, in_sems.at[0])
     tok_copy = pltpu.make_async_copy(tok_hbm, tok, in_sems.at[1])
     cot_copy.start()
     tok_copy.start()
     cot_copy.wait()
-    buffer[0:1024] = cot[...].astype(f32).T.astype(bf16)
+    buffer[...] = cot[...].astype(f32).T.astype(bf16)
+    copies = start_all([(buffer, out_ref.at[peer, pl.ds(0, 1024)]) for peer in range(8)], sems)
     tok_copy.wait()
     rows = []
     for j in range(8):
@@ -60,11 +62,8 @@
     middle = (square - high).astype(bf16).astype(f32)
     low = square - high - middle
     tail = jnp.concatenate([high, middle, low, jnp.zeros_like(low)], axis=0).astype(bf16)
-    buffer[1024:1056] = tail
-    copies = []
-    for peer in range(8):
-        copies.append(pltpu.make_async_copy(buffer, out_ref.at[peer], sems.at[peer]))
-        copies[-1].start()
+    last[...] = tail
+    copies += start_all([(last, out_ref.at[peer, pl.ds(1024, 32)]) for peer in range(8)], tail_sems)
     for copy in copies:
         copy.wait()
 
@@ -130,7 +129,7 @@
         send[i] = total[2 * i + 1].astype(bf16)
 
 
-def share_kernel(own, sibling, arrived, keep, send):
+def share_kernel(own, sibling, arrived, after, keep, send):
     halve(own[...] + sibling[...].astype(f32) + arrived[...].astype(f32), keep, send)
 
 
@@ -138,7 +137,7 @@
     halve(kept[...] + arrived[...].astype(f32), keep, send)
 
 
-def end_kernel(kept, arrived, near_by, mine, other, total):
+def end_kernel(kept, arrived, near_by, after, mine, other, total):
     core = lax.axis_index("core")
     held = kept[0] * (1 - core).astype(f32)
     both = held + arrived[0].astype(f32) + near_by[0].astype(f32)
@@ -147,12 +146,13 @@
     other[...] = total[1 - core]
 
 
-def fold(kept, arrived):
+def fold(kept, arrived, flops):
     n = kept.shape[0] // 2
     return pl.pallas_call(
         fold_kernel,
         out_shape=(S((n, 16, FEAT), f32), S((n, 16, FEAT), bf16)),
         compiler_params=PARAMS,
+        cost_estimate=pl.CostEstimate(flops=flops, bytes_accessed=1000, transcendentals=0),
         name="fold",
     )(kept, arrived)
 
@@ -167,6 +167,18 @@
 
 def pass_kernel(array, after, out):
     pass
+
+
+def pass_on(array, after):
+    return pl.pallas_call(
+        pass_kernel,
+        out_shape=pltpu.HBM(array.shape, array.dtype),
+        in_specs=[HBM, ANY],
+        out_specs=HBM,
+        input_output_aliases={0: 0},
+        compiler_params=PARAMS,
+        name="pass_on",
+    )(array, after)
 
 
 def per_device(tokens, norm_gain, key_weight, key_cotangent, global_fragment, outer_momentum):
@@ -180,7 +192,9 @@
         scratch_shapes=[
             pltpu.VMEM((128, 1024), bf16),
             pltpu.VMEM((FEAT, 1024), bf16),
-            pltpu.VMEM((1056, 128), bf16),
+            pltpu.VMEM((1024, 128), bf16),
+            pltpu.VMEM((32, 128), bf16),
+            pltpu.SemaphoreType.DMA((8,)),
             pltpu.SemaphoreType.DMA((8,)),
             pltpu.SemaphoreType.DMA((2,)),
         ],
@@ -220,7 +234,6 @@
     )(got, far(tok), far(weight), norm_gain)
 
     sibling_a = lax.ppermute(core_a, "core", SWAP)
-    sibling_b = lax.ppermute(core_b, "core", SWAP)
     pair = pl.pallas_call(pair_kernel, out_shape=quarter, compiler_params=PARAMS, name="pair")(own_a, sibling_a)
     arrived = lax.ppermute(pair, "yl", SWAP)
     keys = pl.pallas_call(
@@ -232,40 +245,44 @@
         name="keys",
     )(hid, weight_t, pair)
 
+    core_b = pl.pallas_call(
+        pass_kernel,
+        out_shape=quarter,
+        in_specs=[ANY, HBM],
+        out_specs=ANY,
+        input_output_aliases={0: 0},
+        compiler_params=PARAMS,
+        name="hold",
+    )(core_b, far(keys))
+    sibling_b = lax.ppermute(core_b, "core", SWAP)
     keep, send = pl.pallas_call(
         share_kernel,
         out_shape=(S((8, 16, FEAT), f32), S((8, 16, FEAT), bf16)),
+        in_specs=[VMEM, VMEM, VMEM, HBM],
         compiler_params=PARAMS,
         name="share",
-    )(own_b, sibling_b, arrived)
-    keys = pl.pallas_call(
-        pass_kernel,
-        out_shape=pltpu.HBM((8, 128, 1024), bf16),
-        in_specs=[HBM, ANY],
-        out_specs=HBM,
-        input_output_aliases={0: 0},
-        compiler_params=PARAMS,
-        name="pass_on",
-    )(keys, send)
+    )(own_b, sibling_b, arrived, far(keys))
+    keys = pass_on(keys, send)
     key_parts = lax.all_to_all(keys, FSDP, 0, 0)
-    for step in (1, 2, 4):
-        keep, send = fold(keep, lax.ppermute(send, ZC, ahead(step, step)))
+    key_out = jnp.sum(key_parts.astype(f32), axis=0).astype(bf16)
+    for step, flops in ((1, LONG), (2, 1000), (4, 1000)):
+        keep, send = fold(keep, lax.ppermute(send, ZC, ahead(step, step)), flops)
     near_by = lax.ppermute(keep.astype(bf16), ZC, ahead(None, 1))
     arrived = lax.ppermute(send, ZC, ahead(8, 9))
     mine, other = pl.pallas_call(
         end_kernel,
         out_shape=(S((8, FEAT), f32), S((8, FEAT), f32)),
+        in_specs=[VMEM, VMEM, VMEM, HBM],
         scratch_shapes=[pltpu.VMEM((2, 8, FEAT), f32)],
         compiler_params=PARAMS,
         name="end",
-    )(keep, arrived, near_by)
+    )(keep, arrived, near_by, far(key_out))
     summed = mine + lax.ppermute(other, "core", SWAP)
 
     avg_grad = global_fragment - summed / N_REP
     new_momentum = outer_beta * outer_momentum + avg_grad
     new_global = global_fragment - outer_rate * (avg_grad + outer_beta * new_momentum)
-    key_out = jnp.sum(key_parts.astype(f32), axis=0)
-    return (key_out.astype(bf16), gain_grad, new_global, new_momentum)
+    return (key_out, gain_grad, new_global, new_momentum)
 
 
 def solution(mesh):

time: 131 us -> 126 us (0.962)
  starting transfers between devices: 77.6 us -> 74.8 us
  waiting for transfers between devices: 37.5 us -> 34.9 us
    ppermute x1, waiting for transfers between devices: 4.45 us -> 2.04 us  [per_device(): arrived = lax.ppermute(pair, 'yl', SWAP)]
    ppermute x3, starting transfers between devices: 29.8 us -> 27.9 us  [per_device(): keep, send = fold(keep, lax.ppermute(send, ZC, ahead(step, step)), flops)]
    ppermute x1, starting transfers between devices: 6.82 us -> 5 us  [per_device(): near_by = lax.ppermute(keep.astype(bf16), ZC, ahead(None, 1))]
    ppermute x1, waiting for transfers between devices: 5.78 us -> 4.29 us  [per_device(): arrived = lax.ppermute(send, ZC, ahead(8, 9))]
  transfers between devices with their start and end apart: 11 -> 11, of which waited for: 7 -> 7; matrix products, arithmetic and copies ran while one was open for 0% -> 1% of each run, Pallas kernels for 4% -> 4%
where the time goes in v7:
time: 126 us; the launch traced here: 125 us
  starting transfers between devices  74.8 us (59%)
  waiting for transfers between devices  34.9 us (28%)
  Pallas kernels  12.7 us (10%)
  other arithmetic  1.73 us (1%)
    ppermute x3, starting transfers between devices, per_device(): keep, send = fold(keep, lax.ppermute(send, ZC, ahead(step, step)), flops)  27.9 us
    all_to_all x1, waiting for transfers between devices, per_device(): got = lax.all_to_all(packed, FSDP, 0, 0)  20.1 us
    ppermute x1, starting transfers between devices, per_device(): sibling_a = lax.ppermute(core_a, 'core', SWAP)  10.8 us
    ppermute x1, starting transfers between devices, per_device(): arrived = lax.ppermute(send, ZC, ahead(8, 9))  8.73 us
    all_to_all x1, starting transfers between devices, per_device(): got = lax.all_to_all(packed, FSDP, 0, 0)  7.62 us
    ppermute x3, waiting for transfers between devices, per_device(): keep, send = fold(keep, lax.ppermute(send, ZC, ahead(step, step)), flops)  6.42 us
    pallas_call x1, Pallas kernels, per_device(): pl.pallas_call(grad_kernel, out_shape=(quarter, quarter, quarter_wide, qu...  5.22 us
    ppermute x1, starting transfers between devices, per_device(): near_by = lax.ppermute(keep.astype(bf16), ZC, ahead(None, 1))  5 us
  transfers between devices with their start and end apart: 11, of which 7 were waited for; matrix products, arithmetic and copies ran while one was open for 1% of the time, Pallas kernels for 4%

profile of v7, /device:TPU:1, one launch (start us, length us, event | category | flops | bytes accessed | tf_op | source)
XLA Modules:
  0.0 125.0 jit_solution(2455186205429789657)
XLA Ops:
  0.6 2.6 %pack.1 = bf16[8,1056,128]{2,1,0:T(8,128)(2,1)} custom-call(bf16[128,1024]{1,0:T(8,128)(2,1)} %cot_hbm.1, bf16[576,1024]{1,0:T(8,128)(2,1)} %bitcast.6), custom_call_target="tpu_custom_call" | custom-call | tf_op jit(solution)/shard_map/pack/pallas_call | solution.py:187
  3.2 0.0 copy-start
  3.2 7.6 %all-to-all-start = ((bf16[8,1056,128]{2,1,0:T(8,128)(2,1)}), bf16[8,1056,128]{2,1,0:T(8,128)(2,1)S(1)}, u32[]{:S(2)}, u32[]{:S(2)}) async-start(bf16[8,1056,128]{2,1,0:T(8,128)(2,1)} %pack.1), calls=%async_computation | async-start | bytes 4325376 | tf_op jit(solution)/shard_map/all_to_all | solution.py:204
  10.9 0.0 copy-start.2
  10.9 0.0 copy-done
  10.9 1.5 %turn.1.w_ref = bf16[1024,576]{1,0:T(8,128)(2,1)} custom-call(bf16[576,1024]{1,0:T(8,128)(2,1)S(1)} %bitcast.4), custom_call_target="tpu_custom_call" | custom-call | flops 1000 | bytes 1000 | tf_op jit(solution)/shard_map/turn/pallas_call | solution.py:205
  12.4 20.1 %all-to-all-done.got_ref = bf16[8,1056,128]{2,1,0:T(8,128)(2,1)S(1)} async-done(((bf16[8,1056,128]{2,1,0:T(8,128)(2,1)}), bf16[8,1056,128]{2,1,0:T(8,128)(2,1)S(1)}, u32[]{:S(2)}, u32[]{:S(2)}) %all-to-all-start) | async-done | bytes 2162720 | tf_op jit(solution)/shard_map/all_to_all | solution.py:204
  32.5 0.0 copy-done.2
  32.5 5.2 %grad.1 = (bf16[16,16,576]{2,1,0:T(8,128)(2,1)S(1)}, bf16[16,16,576]{2,1,0:T(8,128)(2,1)S(1)}, f32[16,16,576]{2,1,0:T(8,128)S(1)}, f32[16,16,576]{2,1,0:T(8,128)...) custom-call(bf16[8,1056,128]{2,1,0:T(8,128)(2,1)S(1)} %all-to-all-done.got_ref, bf16[576,1024]{1,0:T(8,128)(2,1)} %bitcast.7, ...), custom_call_target="tpu_custom_call" | custom-call | tf_op jit(solution)/shard_map/grad/pallas_call | solution.py:216
  37.7 0.0 copy-start.1
  37.7 10.8 %collective-permute-start = (bf16[16,16,576]{2,1,0:T(8,128)(2,1)S(1)}, bf16[16,16,576]{2,1,0:T(8,128)(2,1)S(1)}, u32[]{:S(2)}, u32[]{:S(2)}) collective-permute-start(bf16[16,16,576]{2,1,0:T(8,128)(2,1)S(1)} %get-tuple-element.22), channel_id=1, source_target_pairs={{0,8},{8,0},{1,9},{9,1},{2,10},{10,2},{3,11},{11,3},{4,12},{12,4},... | collective-permute-start | bytes 884744 | tf_op jit(solution)/shard_map/ppermute | solution.py:236
  48.5 1.2 collective-permute-done.sibling
  49.8 0.1 pair.1.after_ref
  49.8 5.0 %collective-permute-start.2 = (bf16[16,16,576]{2,1,0:T(8,128)(2,1)S(1)}, bf16[16,16,576]{2,1,0:T(8,128)(2,1)S(1)}, u32[]{:S(2)}, u32[]{:S(2)}) collective-permute-start(bf16[16,16,576]{2,1,0:T(8,128)(2,1)S(1)} %pair.1.after_ref), channel_id=1, source_target_pairs={{0,512},{512,0},{1,513},{513,1},{2,514},{514,2},{3,515},{515,3},{4... | collective-permute-start | bytes 884744 | tf_op jit(solution)/shard_map/ppermute | solution.py:238
  54.8 0.0 copy-done.1
  54.8 3.2 %keys.1.after.array = bf16[8,128,1024]{2,1,0:T(8,128)(2,1)} custom-call(bf16[576,1024]{1,0:T(8,128)(2,1)S(1)} %copy-done.1, bf16[576,1024]{1,0:T(8,128)(2,1)S(1)} %bitcast.5, bf16[16,16,576]{2,1,0:T(8,128)(2,1)S(1)} %pair.1.after_ref), custom_call_target="tpu_custom_call" | custom-call | tf_op jit(solution)/shard_map/keys/pallas_call | solution.py:239
  58.0 2.5 %collective-permute-start.1 = (bf16[16,16,576]{2,1,0:T(8,128)(2,1)S(1)}, bf16[16,16,576]{2,1,0:T(8,128)(2,1)S(1)}, u32[]{:S(2)}, u32[]{:S(2)}) collective-permute-start(bf16[16,16,576]{2,1,0:T(8,128)(2,1)S(1)} %hold.1), channel_id=1, source_target_pairs={{0,8},{8,0},{1,9},{9,1},{2,10},{10,2},{3,11},{11,3},{4,12},{12,4},... | collective-permute-start | bytes 884744 | tf_op jit(solution)/shard_map/ppermute | solution.py:257
  60.6 2.0 %collective-permute-done.2.arrived = bf16[16,16,576]{2,1,0:T(8,128)(2,1)S(1)} collective-permute-done((bf16[16,16,576]{2,1,0:T(8,128)(2,1)S(1)}, bf16[16,16,576]{2,1,0:T(8,128)(2,1)S(1)}, u32[]{:S(2)}, u32[]{:S(2)}) %collective-permute-start.2) | collective-permute-done | bytes 294944 | tf_op jit(solution)/shard_map/ppermute | solution.py:238
  62.6 0.0 collective-permute-done.1.sibling
  62.6 0.1 share.1
  62.7 19.1 %collective-permute-start.3 = (bf16[8,16,576]{2,1,0:T(8,128)(2,1)S(1)}, bf16[8,16,576]{2,1,0:T(8,128)(2,1)S(1)}, u32[]{:S(2)}, u32[]{:S(2)}) collective-permute-start(bf16[8,16,576]{2,1,0:T(8,128)(2,1)S(1)} %get-tuple-element.25.after), channel_id=1, source_target_pairs={{0,16},{8,504},{16,32},{24,8},{32,48},{40,24},{48,64},{56,40},{64,... | collective-permute-start | bytes 442376 | tf_op jit(solution)/shard_map/ppermute | solution.py:269
  81.8 3.6 %all-to-all-start.1 = ((bf16[8,128,1024]{2,1,0:T(8,128)(2,1)}), bf16[8,128,1024]{2,1,0:T(8,128)(2,1)S(1)}, u32[]{:S(2)}, u32[]{:S(2)}) async-start(bf16[8,128,1024]{2,1,0:T(8,128)(2,1)} %pass_on.1), calls=%async_computation.1 | async-start | bytes 4194304 | tf_op jit(solution)/shard_map/all_to_all | solution.py:266
  85.5 0.0 collective-permute-done.3.arrived
  85.5 0.0 copy-start.3
  85.5 0.0 copy-start.4
  85.5 3.1 %collective-permute-start.4 = (bf16[4,16,576]{2,1,0:T(8,128)(2,1)S(1)}, bf16[4,16,576]{2,1,0:T(8,128)(2,1)S(1)}, u32[]{:S(2)}, u32[]{:S(2)}) collective-permute-start(bf16[4,16,576]{2,1,0:T(8,128)(2,1)S(1)} %get-tuple-element.29), channel_id=1, source_target_pairs={{0,32},{8,488},{16,48},{24,504},{32,64},{40,8},{48,80},{56,24},{64... | collective-permute-start | bytes 221192 | tf_op jit(solution)/shard_map/ppermute | solution.py:269
  88.7 3.0 %collective-permute-done.4.arrived = bf16[4,16,576]{2,1,0:T(8,128)(2,1)S(1)} collective-permute-done((bf16[4,16,576]{2,1,0:T(8,128)(2,1)S(1)}, bf16[4,16,576]{2,1,0:T(8,128)(2,1)S(1)}, u32[]{:S(2)}, u32[]{:S(2)}) %collective-permute-start.4) | collective-permute-done | bytes 73760 | tf_op jit(solution)/shard_map/ppermute | solution.py:269
  91.7 5.6 %collective-permute-start.5 = (bf16[2,16,576]{2,1,0:T(8,128)(2,1)S(1)}, bf16[2,16,576]{2,1,0:T(8,128)(2,1)S(1)}, u32[]{:S(2)}, u32[]{:S(2)}) collective-permute-start(bf16[2,16,576]{2,1,0:T(8,128)(2,1)S(1)} %get-tuple-element.31), channel_id=1, source_target_pairs={{0,64},{8,456},{16,80},{24,472},{32,96},{40,488},{48,112},{56,504}... | collective-permute-start | bytes 110600 | tf_op jit(solution)/shard_map/ppermute | solution.py:269
  97.3 3.5 %collective-permute-done.5.arrived = bf16[2,16,576]{2,1,0:T(8,128)(2,1)S(1)} collective-permute-done((bf16[2,16,576]{2,1,0:T(8,128)(2,1)S(1)}, bf16[2,16,576]{2,1,0:T(8,128)(2,1)S(1)}, u32[]{:S(2)}, u32[]{:S(2)}) %collective-permute-start.5) | collective-permute-done | bytes 36896 | tf_op jit(solution)/shard_map/ppermute | solution.py:269
  100.8 5.0 %collective-permute-start.7 = (bf16[1,16,576]{2,1,0:T(8,128)(2,1)S(1)}, bf16[1,16,576]{2,1,0:T(8,128)(2,1)S(1)}, u32[]{:S(2)}, u32[]{:S(2)}) collective-permute-start(bf16[1,16,576]{2,1,0:T(8,128)(2,1)S(1)} %convert_element_type.2), channel_id=1, source_target_pairs={{8,504},{24,8},{40,24},{56,40},{72,56},{88,72},{104,88},{120,104},... | collective-permute-start | bytes 55304 | tf_op jit(solution)/shard_map/ppermute | solution.py:270
  105.8 8.7 %collective-permute-start.6 = (bf16[1,16,576]{2,1,0:T(8,128)(2,1)S(1)}, bf16[1,16,576]{2,1,0:T(8,128)(2,1)S(1)}, u32[]{:S(2)}, u32[]{:S(2)}) collective-permute-start(bf16[1,16,576]{2,1,0:T(8,128)(2,1)S(1)} %get-tuple-element.33), channel_id=1, source_target_pairs={{0,128},{8,376},{16,144},{24,392},{32,160},{40,408},{48,176},{56,4... | collective-permute-start | bytes 55304 | tf_op jit(solution)/shard_map/ppermute | solution.py:271
  114.5 0.0 all-to-all-done.1
  114.6 1.1 reduce_sum.12.after
  115.7 0.0 collective-permute-done.7.near_by
  115.7 4.3 %collective-permute-done.6.arrived = bf16[1,16,576]{2,1,0:T(8,128)(2,1)S(1)} collective-permute-done((bf16[1,16,576]{2,1,0:T(8,128)(2,1)S(1)}, bf16[1,16,576]{2,1,0:T(8,128)(2,1)S(1)}, u32[]{:S(2)}, u32[]{:S(2)}) %collective-permute-start.6) | collective-permute-done | bytes 18464 | tf_op jit(solution)/shard_map/ppermute | solution.py:271
  120.0 3.5 %collective-permute-start.8 = (f32[8,576]{1,0:T(8,128)S(1)}, f32[8,576]{1,0:T(8,128)S(1)}, u32[]{:S(2)}, u32[]{:S(2)}) collective-permute-start(f32[8,576]{1,0:T(8,128)S(1)} %get-tuple-element.35), channel_id=1, source_target_pairs={{0,8},{8,0},{1,9},{9,1},{2,10},{10,2},{3,11},{11,3},{4,12},{12,4},... | collective-permute-start | bytes 55304 | tf_op jit(solution)/shard_map/ppermute | solution.py:280
  123.5 0.8 collective-permute-done.8
  124.3 0.0 copy-done.3
  124.3 0.0 copy-done.4
  124.3 0.6 multiply_subtract_fusion
  (7 shorter events, 0.1 us)
Async XLA Ops:
  3.2 7.6 %copy-start = (bf16[1,1024,576]{1,2,0:T(8,128)(2,1)S(1)}, bf16[1,1024,576]{1,2,0:T(8,128)(2,1)}, u32[]{:S(2)}) copy-start(bf16[1,1024,576]{1,2,0:T(8,128)(2,1)} %param.8) | copy-start | bytes 3538948
  3.2 29.2 %all-to-all-start = ((bf16[8,1056,128]{2,1,0:T(8,128)(2,1)}), bf16[8,1056,128]{2,1,0:T(8,128)(2,1)S(1)}, u32[]{:S(2)}, u32[]{:S(2)}) async-start(bf16[8,1056,128]{2,1,0:T(8,128)(2,1)} %pack.1), calls=%async_computation | async-start | bytes 4325376 | tf_op jit(solution)/shard_map/all_to_all | solution.py:204
  10.9 21.6 %copy-start.2 = (bf16[1,576]{1,0:T(2,128)(2,1)S(1)}, bf16[1,576]{1,0:T(2,128)(2,1)}, u32[]{:S(2)}) copy-start(bf16[1,576]{1,0:T(2,128)(2,1)} %gain_ref.1) | copy-start | bytes 3460
  37.7 17.1 %copy-start.1 = (bf16[576,1024]{1,0:T(8,128)(2,1)S(1)}, bf16[576,1024]{1,0:T(8,128)(2,1)}, u32[]{:S(2)}) copy-start(bf16[576,1024]{1,0:T(8,128)(2,1)} %get-tuple-element.20.hid_ref) | copy-start | bytes 3538948
  37.7 12.1 %collective-permute-start = (bf16[16,16,576]{2,1,0:T(8,128)(2,1)S(1)}, bf16[16,16,576]{2,1,0:T(8,128)(2,1)S(1)}, u32[]{:S(2)}, u32[]{:S(2)}) collective-permute-start(bf16[16,16,576]{2,1,0:T(8,128)(2,1)S(1)} %get-tuple-element.22), channel_id=1, source_target_pairs={{0,8},{8,0},{1,9},{9,1},{2,10},{10,2},{3,11},{11,3},{4,12},{12,4},... | collective-permute-start | bytes 884744 | tf_op jit(solution)/shard_map/ppermute | solution.py:236
  49.8 12.7 %collective-permute-start.2 = (bf16[16,16,576]{2,1,0:T(8,128)(2,1)S(1)}, bf16[16,16,576]{2,1,0:T(8,128)(2,1)S(1)}, u32[]{:S(2)}, u32[]{:S(2)}) collective-permute-start(bf16[16,16,576]{2,1,0:T(8,128)(2,1)S(1)} %pair.1.after_ref), channel_id=1, source_target_pairs={{0,512},{512,0},{1,513},{513,1},{2,514},{514,2},{3,515},{515,3},{4... | collective-permute-start | bytes 884744 | tf_op jit(solution)/shard_map/ppermute | solution.py:238
  58.0 4.6 %collective-permute-start.1 = (bf16[16,16,576]{2,1,0:T(8,128)(2,1)S(1)}, bf16[16,16,576]{2,1,0:T(8,128)(2,1)S(1)}, u32[]{:S(2)}, u32[]{:S(2)}) collective-permute-start(bf16[16,16,576]{2,1,0:T(8,128)(2,1)S(1)} %hold.1), channel_id=1, source_target_pairs={{0,8},{8,0},{1,9},{9,1},{2,10},{10,2},{3,11},{11,3},{4,12},{12,4},... | collective-permute-start | bytes 884744 | tf_op jit(solution)/shard_map/ppermute | solution.py:257
  62.7 22.8 %collective-permute-start.3 = (bf16[8,16,576]{2,1,0:T(8,128)(2,1)S(1)}, bf16[8,16,576]{2,1,0:T(8,128)(2,1)S(1)}, u32[]{:S(2)}, u32[]{:S(2)}) collective-permute-start(bf16[8,16,576]{2,1,0:T(8,128)(2,1)S(1)} %get-tuple-element.25.after), channel_id=1, source_target_pairs={{0,16},{8,504},{16,32},{24,8},{32,48},{40,24},{48,64},{56,40},{64,... | collective-permute-start | bytes 442376 | tf_op jit(solution)/shard_map/ppermute | solution.py:269
  81.8 32.7 %all-to-all-start.1 = ((bf16[8,128,1024]{2,1,0:T(8,128)(2,1)}), bf16[8,128,1024]{2,1,0:T(8,128)(2,1)S(1)}, u32[]{:S(2)}, u32[]{:S(2)}) async-start(bf16[8,128,1024]{2,1,0:T(8,128)(2,1)} %pass_on.1), calls=%async_computation.1 | async-start | bytes 4194304 | tf_op jit(solution)/shard_map/all_to_all | solution.py:266
  85.5 38.8 %copy-start.3 = (f32[8,576]{1,0:T(8,128)S(1)}, f32[8,576]{1,0:T(8,128)}, u32[]{:S(2)}) copy-start(f32[8,576]{1,0:T(8,128)} %param.10) | copy-start | bytes 55300
  85.5 38.8 %copy-start.4 = (f32[8,576]{1,0:T(8,128)S(1)}, f32[8,576]{1,0:T(8,128)}, u32[]{:S(2)}) copy-start(f32[8,576]{1,0:T(8,128)} %param.11) | copy-start | bytes 55300
  85.5 6.1 %collective-permute-start.4 = (bf16[4,16,576]{2,1,0:T(8,128)(2,1)S(1)}, bf16[4,16,576]{2,1,0:T(8,128)(2,1)S(1)}, u32[]{:S(2)}, u32[]{:S(2)}) collective-permute-start(bf16[4,16,576]{2,1,0:T(8,128)(2,1)S(1)} %get-tuple-element.29), channel_id=1, source_target_pairs={{0,32},{8,488},{16,48},{24,504},{32,64},{40,8},{48,80},{56,24},{64... | collective-permute-start | bytes 221192 | tf_op jit(solution)/shard_map/ppermute | solution.py:269
  91.7 9.1 %collective-permute-start.5 = (bf16[2,16,576]{2,1,0:T(8,128)(2,1)S(1)}, bf16[2,16,576]{2,1,0:T(8,128)(2,1)S(1)}, u32[]{:S(2)}, u32[]{:S(2)}) collective-permute-start(bf16[2,16,576]{2,1,0:T(8,128)(2,1)S(1)} %get-tuple-element.31), channel_id=1, source_target_pairs={{0,64},{8,456},{16,80},{24,472},{32,96},{40,488},{48,112},{56,504}... | collective-permute-start | bytes 110600 | tf_op jit(solution)/shard_map/ppermute | solution.py:269
  100.8 14.9 %collective-permute-start.7 = (bf16[1,16,576]{2,1,0:T(8,128)(2,1)S(1)}, bf16[1,16,576]{2,1,0:T(8,128)(2,1)S(1)}, u32[]{:S(2)}, u32[]{:S(2)}) collective-permute-start(bf16[1,16,576]{2,1,0:T(8,128)(2,1)S(1)} %convert_element_type.2), channel_id=1, source_target_pairs={{8,504},{24,8},{40,24},{56,40},{72,56},{88,72},{104,88},{120,104},... | collective-permute-start | bytes 55304 | tf_op jit(solution)/shard_map/ppermute | solution.py:270
  105.8 14.1 %collective-permute-start.6 = (bf16[1,16,576]{2,1,0:T(8,128)(2,1)S(1)}, bf16[1,16,576]{2,1,0:T(8,128)(2,1)S(1)}, u32[]{:S(2)}, u32[]{:S(2)}) collective-permute-start(bf16[1,16,576]{2,1,0:T(8,128)(2,1)S(1)} %get-tuple-element.33), channel_id=1, source_target_pairs={{0,128},{8,376},{16,144},{24,392},{32,160},{40,408},{48,176},{56,4... | collective-permute-start | bytes 55304 | tf_op jit(solution)/shard_map/ppermute | solution.py:271
  120.0 4.4 %collective-permute-start.8 = (f32[8,576]{1,0:T(8,128)S(1)}, f32[8,576]{1,0:T(8,128)S(1)}, u32[]{:S(2)}, u32[]{:S(2)}) collective-permute-start(f32[8,576]{1,0:T(8,128)S(1)} %get-tuple-element.35), channel_id=1, source_target_pairs={{0,8},{8,0},{1,9},{9,1},{2,10},{10,2},{3,11},{11,3},{4,12},{12,4},... | collective-permute-start | bytes 55304 | tf_op jit(solution)/shard_map/ppermute | solution.py:280

commit v8 on v7

--- a/solution.py
+++ b/solution.py
@@ -80,34 +80,38 @@
 
 
 def grad_kernel(
-    got_ref, tok_ref, w_ref, gain_ref,
+    got, tok_ref, w_ref, gain_ref,
     core_a_ref, core_b_ref, own_a_ref, own_b_ref, hid_hbm, gain_grad_ref,
-    got, tok, weight, hid, total, sems,
+    tok, weight, hid, total, sems,
 ):
     core = lax.axis_index("core")
     yl = lax.axis_index("yl")
-    copies = start_all([(got_ref, got), (tok_ref, tok), (w_ref, weight)], sems)
-    hid_copy = pltpu.make_async_copy(hid, hid_hbm, sems.at[3])
+    copies = start_all([(tok_ref, tok), (w_ref, weight)], sems)
+    hid_copy = pltpu.make_async_copy(hid, hid_hbm, sems.at[2])
     gain_row = gain_ref[...].astype(f32)
     gain = jnp.broadcast_to(gain_row, (8, FEAT)).T[:, 0:1]
-    copies[0].wait()
     square = jnp.zeros((8, 128), f32)
     for g in range(8):
         tail = got[g, 1024:1056].astype(f32)
         square += tail[0:8] + (tail[8:16] + tail[16:24])
     inv_rms = lax.rsqrt(square / D + rms_eps)
-    copies[1].wait()
+    copies[0].wait()
     for j in range(8):
         at = slice(j * 128, (j + 1) * 128)
         normed = tok[:, at].astype(f32) * inv_rms[j : j + 1]
         hid[:, at] = (normed * gain).astype(bf16)
     hid_copy.start()
-    cot = jnp.concatenate([got[g, 0:1024] for g in range(8)], axis=1)
-    grad = lax.dot_general(cot, hid[...], (((1,), (1,)), ((), ())), preferred_element_type=f32)
-    copies[2].wait()
-    w = weight[...].astype(f32)
-    gain_grad_ref[...] = jnp.sum(w * grad, axis=0, keepdims=True) / gain_row
-    total[...] = (w - inner_rate * grad).reshape(2, 32, 16, FEAT)
+    copies[1].wait()
+    gain_sum = jnp.zeros((1, FEAT), f32)
+    for m in range(4):
+        rows = slice(256 * m, 256 * (m + 1))
+        cot = jnp.concatenate([got[g, rows] for g in range(8)], axis=1)
+        grad = lax.dot_general(cot, hid[...], (((1,), (1,)), ((), ())), preferred_element_type=f32)
+        w = weight[rows].astype(f32)
+        gain_sum += jnp.sum(w * grad, axis=0, keepdims=True)
+        half = slice(m % 2 * 16, m % 2 * 16 + 16)
+        total[m // 2, half] = (w - inner_rate * grad).reshape(16, 16, FEAT)
+    gain_grad_ref[...] = gain_sum / gain_row
     z = lax.axis_index("z")
     for t in range(16):
         own = (z + (1 - 2 * core) * t - core + 64) % 32
@@ -219,15 +223,14 @@
             quarter, quarter, quarter_wide, quarter_wide,
             pltpu.HBM((FEAT, 1024), bf16), S((1, FEAT), f32),
         ),
-        in_specs=[ANY, HBM, HBM, VMEM],
+        in_specs=[VMEM, HBM, HBM, VMEM],
         out_specs=(VMEM, VMEM, VMEM, VMEM, HBM, VMEM),
         scratch_shapes=[
-            pltpu.VMEM((8, 1056, 128), bf16),
             pltpu.VMEM((FEAT, 1024), bf16),
             pltpu.VMEM((1024, FEAT), bf16),
             pltpu.VMEM((FEAT, 1024), bf16),
             pltpu.VMEM((2, 32, 16, FEAT), f32),
-            pltpu.SemaphoreType.DMA((4,)),
+            pltpu.SemaphoreType.DMA((3,)),
         ],
         compiler_params=PARAMS,
         name="grad",

time: 126 us -> 125 us (level)
  no operation moved by 1% of the time
where the time goes in v8:
time: 125 us; the launch traced here: 124 us
  starting transfers between devices  74.8 us (60%)
  waiting for transfers between devices  34.9 us (28%)
  Pallas kernels  11.8 us (9%)
  other arithmetic  1.73 us (1%)
    ppermute x3, starting transfers between devices, per_device(): keep, send = fold(keep, lax.ppermute(send, ZC, ahead(step, step)), flops)  27.9 us
    all_to_all x1, waiting for transfers between devices, per_device(): got = lax.all_to_all(packed, FSDP, 0, 0)  20.1 us
    ppermute x1, starting transfers between devices, per_device(): sibling_a = lax.ppermute(core_a, 'core', SWAP)  10.8 us
    ppermute x1, starting transfers between devices, per_device(): arrived = lax.ppermute(send, ZC, ahead(8, 9))  8.73 us
    all_to_all x1, starting transfers between devices, per_device(): got = lax.all_to_all(packed, FSDP, 0, 0)  7.62 us
    ppermute x3, waiting for transfers between devices, per_device(): keep, send = fold(keep, lax.ppermute(send, ZC, ahead(step, step)), flops)  6.43 us
    ppermute x1, starting transfers between devices, per_device(): near_by = lax.ppermute(keep.astype(bf16), ZC, ahead(None, 1))  5 us
    ppermute x1, starting transfers between devices, per_device(): arrived = lax.ppermute(pair, 'yl', SWAP)  4.97 us
  transfers between devices with their start and end apart: 11, of which 7 were waited for; matrix products, arithmetic and copies ran while one was open for 1% of the time, Pallas kernels for 4%

profile of v8, /device:TPU:1, one launch (start us, length us, event | category | flops | bytes accessed | tf_op | source)
XLA Modules:
  0.0 124.0 jit_solution(1539473728160279306)
XLA Ops:
  0.6 2.6 %pack.1 = bf16[8,1056,128]{2,1,0:T(8,128)(2,1)} custom-call(bf16[128,1024]{1,0:T(8,128)(2,1)} %cot_hbm.1, bf16[576,1024]{1,0:T(8,128)(2,1)} %bitcast.6), custom_call_target="tpu_custom_call" | custom-call | tf_op jit(solution)/shard_map/pack/pallas_call | solution.py:191
  3.2 0.0 copy-start
  3.2 7.6 %all-to-all-start = ((bf16[8,1056,128]{2,1,0:T(8,128)(2,1)}), bf16[8,1056,128]{2,1,0:T(8,128)(2,1)S(1)}, u32[]{:S(2)}, u32[]{:S(2)}) async-start(bf16[8,1056,128]{2,1,0:T(8,128)(2,1)} %pack.1), calls=%async_computation | async-start | bytes 4325376 | tf_op jit(solution)/shard_map/all_to_all | solution.py:208
  10.9 0.0 copy-start.2
  10.9 0.0 copy-done
  10.9 1.5 %turn.1.w_ref = bf16[1024,576]{1,0:T(8,128)(2,1)} custom-call(bf16[576,1024]{1,0:T(8,128)(2,1)S(1)} %bitcast.4), custom_call_target="tpu_custom_call" | custom-call | flops 1000 | bytes 1000 | tf_op jit(solution)/shard_map/turn/pallas_call | solution.py:209
  12.4 20.1 %all-to-all-done.got = bf16[8,1056,128]{2,1,0:T(8,128)(2,1)S(1)} async-done(((bf16[8,1056,128]{2,1,0:T(8,128)(2,1)}), bf16[8,1056,128]{2,1,0:T(8,128)(2,1)S(1)}, u32[]{:S(2)}, u32[]{:S(2)}) %all-to-all-start) | async-done | bytes 2162720 | tf_op jit(solution)/shard_map/all_to_all | solution.py:208
  32.5 0.0 copy-done.2
  32.5 4.3 %grad.1 = (bf16[16,16,576]{2,1,0:T(8,128)(2,1)S(1)}, bf16[16,16,576]{2,1,0:T(8,128)(2,1)S(1)}, f32[16,16,576]{2,1,0:T(8,128)S(1)}, f32[16,16,576]{2,1,0:T(8,128)...) custom-call(bf16[8,1056,128]{2,1,0:T(8,128)(2,1)S(1)} %all-to-all-done.got, bf16[576,1024]{1,0:T(8,128)(2,1)} %bitcast.7, ...), custom_call_target="tpu_custom_call" | custom-call | tf_op jit(solution)/shard_map/grad/pallas_call | solution.py:220
  36.8 0.0 copy-start.1
  36.8 10.8 %collective-permute-start = (bf16[16,16,576]{2,1,0:T(8,128)(2,1)S(1)}, bf16[16,16,576]{2,1,0:T(8,128)(2,1)S(1)}, u32[]{:S(2)}, u32[]{:S(2)}) collective-permute-start(bf16[16,16,576]{2,1,0:T(8,128)(2,1)S(1)} %get-tuple-element.22), channel_id=1, source_target_pairs={{0,8},{8,0},{1,9},{9,1},{2,10},{10,2},{3,11},{11,3},{4,12},{12,4},... | collective-permute-start | bytes 884744 | tf_op jit(solution)/shard_map/ppermute | solution.py:239
  47.6 1.2 collective-permute-done.sibling
  48.9 0.1 pair.1.after_ref
  48.9 5.0 %collective-permute-start.2 = (bf16[16,16,576]{2,1,0:T(8,128)(2,1)S(1)}, bf16[16,16,576]{2,1,0:T(8,128)(2,1)S(1)}, u32[]{:S(2)}, u32[]{:S(2)}) collective-permute-start(bf16[16,16,576]{2,1,0:T(8,128)(2,1)S(1)} %pair.1.after_ref), channel_id=1, source_target_pairs={{0,512},{512,0},{1,513},{513,1},{2,514},{514,2},{3,515},{515,3},{4... | collective-permute-start | bytes 884744 | tf_op jit(solution)/shard_map/ppermute | solution.py:241
  53.9 0.0 copy-done.1
  53.9 3.2 %keys.1.after.array = bf16[8,128,1024]{2,1,0:T(8,128)(2,1)} custom-call(bf16[576,1024]{1,0:T(8,128)(2,1)S(1)} %copy-done.1, bf16[576,1024]{1,0:T(8,128)(2,1)S(1)} %bitcast.5, bf16[16,16,576]{2,1,0:T(8,128)(2,1)S(1)} %pair.1.after_ref), custom_call_target="tpu_custom_call" | custom-call | tf_op jit(solution)/shard_map/keys/pallas_call | solution.py:242
  57.1 2.5 %collective-permute-start.1 = (bf16[16,16,576]{2,1,0:T(8,128)(2,1)S(1)}, bf16[16,16,576]{2,1,0:T(8,128)(2,1)S(1)}, u32[]{:S(2)}, u32[]{:S(2)}) collective-permute-start(bf16[16,16,576]{2,1,0:T(8,128)(2,1)S(1)} %hold.1), channel_id=1, source_target_pairs={{0,8},{8,0},{1,9},{9,1},{2,10},{10,2},{3,11},{11,3},{4,12},{12,4},... | collective-permute-start | bytes 884744 | tf_op jit(solution)/shard_map/ppermute | solution.py:260
  59.6 2.0 %collective-permute-done.2.arrived = bf16[16,16,576]{2,1,0:T(8,128)(2,1)S(1)} collective-permute-done((bf16[16,16,576]{2,1,0:T(8,128)(2,1)S(1)}, bf16[16,16,576]{2,1,0:T(8,128)(2,1)S(1)}, u32[]{:S(2)}, u32[]{:S(2)}) %collective-permute-start.2) | collective-permute-done | bytes 294944 | tf_op jit(solution)/shard_map/ppermute | solution.py:241
  61.7 0.0 collective-permute-done.1.sibling
  61.7 0.1 share.1
  61.8 19.1 %collective-permute-start.3 = (bf16[8,16,576]{2,1,0:T(8,128)(2,1)S(1)}, bf16[8,16,576]{2,1,0:T(8,128)(2,1)S(1)}, u32[]{:S(2)}, u32[]{:S(2)}) collective-permute-start(bf16[8,16,576]{2,1,0:T(8,128)(2,1)S(1)} %get-tuple-element.25.after), channel_id=1, source_target_pairs={{0,16},{8,504},{16,32},{24,8},{32,48},{40,24},{48,64},{56,40},{64,... | collective-permute-start | bytes 442376 | tf_op jit(solution)/shard_map/ppermute | solution.py:272
  80.9 3.6 %all-to-all-start.1 = ((bf16[8,128,1024]{2,1,0:T(8,128)(2,1)}), bf16[8,128,1024]{2,1,0:T(8,128)(2,1)S(1)}, u32[]{:S(2)}, u32[]{:S(2)}) async-start(bf16[8,128,1024]{2,1,0:T(8,128)(2,1)} %pass_on.1), calls=%async_computation.1 | async-start | bytes 4194304 | tf_op jit(solution)/shard_map/all_to_all | solution.py:269
  84.6 0.0 collective-permute-done.3.arrived
  84.6 0.0 copy-start.3
  84.6 0.0 copy-start.4
  84.6 3.1 %collective-permute-start.4 = (bf16[4,16,576]{2,1,0:T(8,128)(2,1)S(1)}, bf16[4,16,576]{2,1,0:T(8,128)(2,1)S(1)}, u32[]{:S(2)}, u32[]{:S(2)}) collective-permute-start(bf16[4,16,576]{2,1,0:T(8,128)(2,1)S(1)} %get-tuple-element.29), channel_id=1, source_target_pairs={{0,32},{8,488},{16,48},{24,504},{32,64},{40,8},{48,80},{56,24},{64... | collective-permute-start | bytes 221192 | tf_op jit(solution)/shard_map/ppermute | solution.py:272
  87.8 3.0 %collective-permute-done.4.arrived = bf16[4,16,576]{2,1,0:T(8,128)(2,1)S(1)} collective-permute-done((bf16[4,16,576]{2,1,0:T(8,128)(2,1)S(1)}, bf16[4,16,576]{2,1,0:T(8,128)(2,1)S(1)}, u32[]{:S(2)}, u32[]{:S(2)}) %collective-permute-start.4) | collective-permute-done | bytes 73760 | tf_op jit(solution)/shard_map/ppermute | solution.py:272
  90.8 5.6 %collective-permute-start.5 = (bf16[2,16,576]{2,1,0:T(8,128)(2,1)S(1)}, bf16[2,16,576]{2,1,0:T(8,128)(2,1)S(1)}, u32[]{:S(2)}, u32[]{:S(2)}) collective-permute-start(bf16[2,16,576]{2,1,0:T(8,128)(2,1)S(1)} %get-tuple-element.31), channel_id=1, source_target_pairs={{0,64},{8,456},{16,80},{24,472},{32,96},{40,488},{48,112},{56,504}... | collective-permute-start | bytes 110600 | tf_op jit(solution)/shard_map/ppermute | solution.py:272
  96.4 3.5 %collective-permute-done.5.arrived = bf16[2,16,576]{2,1,0:T(8,128)(2,1)S(1)} collective-permute-done((bf16[2,16,576]{2,1,0:T(8,128)(2,1)S(1)}, bf16[2,16,576]{2,1,0:T(8,128)(2,1)S(1)}, u32[]{:S(2)}, u32[]{:S(2)}) %collective-permute-start.5) | collective-permute-done | bytes 36896 | tf_op jit(solution)/shard_map/ppermute | solution.py:272
  99.9 5.0 %collective-permute-start.7 = (bf16[1,16,576]{2,1,0:T(8,128)(2,1)S(1)}, bf16[1,16,576]{2,1,0:T(8,128)(2,1)S(1)}, u32[]{:S(2)}, u32[]{:S(2)}) collective-permute-start(bf16[1,16,576]{2,1,0:T(8,128)(2,1)S(1)} %convert_element_type.2), channel_id=1, source_target_pairs={{8,504},{24,8},{40,24},{56,40},{72,56},{88,72},{104,88},{120,104},... | collective-permute-start | bytes 55304 | tf_op jit(solution)/shard_map/ppermute | solution.py:273
  104.9 8.7 %collective-permute-start.6 = (bf16[1,16,576]{2,1,0:T(8,128)(2,1)S(1)}, bf16[1,16,576]{2,1,0:T(8,128)(2,1)S(1)}, u32[]{:S(2)}, u32[]{:S(2)}) collective-permute-start(bf16[1,16,576]{2,1,0:T(8,128)(2,1)S(1)} %get-tuple-element.33), channel_id=1, source_target_pairs={{0,128},{8,376},{16,144},{24,392},{32,160},{40,408},{48,176},{56,4... | collective-permute-start | bytes 55304 | tf_op jit(solution)/shard_map/ppermute | solution.py:274
  113.6 0.0 all-to-all-done.1
  113.7 1.1 reduce_sum.12.after
  114.8 0.0 collective-permute-done.7.near_by
  114.8 4.3 %collective-permute-done.6.arrived = bf16[1,16,576]{2,1,0:T(8,128)(2,1)S(1)} collective-permute-done((bf16[1,16,576]{2,1,0:T(8,128)(2,1)S(1)}, bf16[1,16,576]{2,1,0:T(8,128)(2,1)S(1)}, u32[]{:S(2)}, u32[]{:S(2)}) %collective-permute-start.6) | collective-permute-done | bytes 18464 | tf_op jit(solution)/shard_map/ppermute | solution.py:274
  119.1 3.5 %collective-permute-start.8 = (f32[8,576]{1,0:T(8,128)S(1)}, f32[8,576]{1,0:T(8,128)S(1)}, u32[]{:S(2)}, u32[]{:S(2)}) collective-permute-start(f32[8,576]{1,0:T(8,128)S(1)} %get-tuple-element.35), channel_id=1, source_target_pairs={{0,8},{8,0},{1,9},{9,1},{2,10},{10,2},{3,11},{11,3},{4,12},{12,4},... | collective-permute-start | bytes 55304 | tf_op jit(solution)/shard_map/ppermute | solution.py:283
  122.6 0.8 collective-permute-done.8
  123.4 0.0 copy-done.3
  123.4 0.0 copy-done.4
  123.4 0.6 multiply_subtract_fusion
  (7 shorter events, 0.1 us)
Async XLA Ops:
  3.2 7.6 %copy-start = (bf16[1,1024,576]{1,2,0:T(8,128)(2,1)S(1)}, bf16[1,1024,576]{1,2,0:T(8,128)(2,1)}, u32[]{:S(2)}) copy-start(bf16[1,1024,576]{1,2,0:T(8,128)(2,1)} %param.8) | copy-start | bytes 3538948
  3.2 29.2 %all-to-all-start = ((bf16[8,1056,128]{2,1,0:T(8,128)(2,1)}), bf16[8,1056,128]{2,1,0:T(8,128)(2,1)S(1)}, u32[]{:S(2)}, u32[]{:S(2)}) async-start(bf16[8,1056,128]{2,1,0:T(8,128)(2,1)} %pack.1), calls=%async_computation | async-start | bytes 4325376 | tf_op jit(solution)/shard_map/all_to_all | solution.py:208
  10.9 21.6 %copy-start.2 = (bf16[1,576]{1,0:T(2,128)(2,1)S(1)}, bf16[1,576]{1,0:T(2,128)(2,1)}, u32[]{:S(2)}) copy-start(bf16[1,576]{1,0:T(2,128)(2,1)} %gain_ref.1) | copy-start | bytes 3460
  36.8 17.1 %copy-start.1 = (bf16[576,1024]{1,0:T(8,128)(2,1)S(1)}, bf16[576,1024]{1,0:T(8,128)(2,1)}, u32[]{:S(2)}) copy-start(bf16[576,1024]{1,0:T(8,128)(2,1)} %get-tuple-element.20.hid_ref) | copy-start | bytes 3538948
  36.8 12.1 %collective-permute-start = (bf16[16,16,576]{2,1,0:T(8,128)(2,1)S(1)}, bf16[16,16,576]{2,1,0:T(8,128)(2,1)S(1)}, u32[]{:S(2)}, u32[]{:S(2)}) collective-permute-start(bf16[16,16,576]{2,1,0:T(8,128)(2,1)S(1)} %get-tuple-element.22), channel_id=1, source_target_pairs={{0,8},{8,0},{1,9},{9,1},{2,10},{10,2},{3,11},{11,3},{4,12},{12,4},... | collective-permute-start | bytes 884744 | tf_op jit(solution)/shard_map/ppermute | solution.py:239
  48.9 12.7 %collective-permute-start.2 = (bf16[16,16,576]{2,1,0:T(8,128)(2,1)S(1)}, bf16[16,16,576]{2,1,0:T(8,128)(2,1)S(1)}, u32[]{:S(2)}, u32[]{:S(2)}) collective-permute-start(bf16[16,16,576]{2,1,0:T(8,128)(2,1)S(1)} %pair.1.after_ref), channel_id=1, source_target_pairs={{0,512},{512,0},{1,513},{513,1},{2,514},{514,2},{3,515},{515,3},{4... | collective-permute-start | bytes 884744 | tf_op jit(solution)/shard_map/ppermute | solution.py:241
  57.1 4.6 %collective-permute-start.1 = (bf16[16,16,576]{2,1,0:T(8,128)(2,1)S(1)}, bf16[16,16,576]{2,1,0:T(8,128)(2,1)S(1)}, u32[]{:S(2)}, u32[]{:S(2)}) collective-permute-start(bf16[16,16,576]{2,1,0:T(8,128)(2,1)S(1)} %hold.1), channel_id=1, source_target_pairs={{0,8},{8,0},{1,9},{9,1},{2,10},{10,2},{3,11},{11,3},{4,12},{12,4},... | collective-permute-start | bytes 884744 | tf_op jit(solution)/shard_map/ppermute | solution.py:260
  61.8 22.8 %collective-permute-start.3 = (bf16[8,16,576]{2,1,0:T(8,128)(2,1)S(1)}, bf16[8,16,576]{2,1,0:T(8,128)(2,1)S(1)}, u32[]{:S(2)}, u32[]{:S(2)}) collective-permute-start(bf16[8,16,576]{2,1,0:T(8,128)(2,1)S(1)} %get-tuple-element.25.after), channel_id=1, source_target_pairs={{0,16},{8,504},{16,32},{24,8},{32,48},{40,24},{48,64},{56,40},{64,... | collective-permute-start | bytes 442376 | tf_op jit(solution)/shard_map/ppermute | solution.py:272
  80.9 32.7 %all-to-all-start.1 = ((bf16[8,128,1024]{2,1,0:T(8,128)(2,1)}), bf16[8,128,1024]{2,1,0:T(8,128)(2,1)S(1)}, u32[]{:S(2)}, u32[]{:S(2)}) async-start(bf16[8,128,1024]{2,1,0:T(8,128)(2,1)} %pass_on.1), calls=%async_computation.1 | async-start | bytes 4194304 | tf_op jit(solution)/shard_map/all_to_all | solution.py:269
  84.6 38.8 %copy-start.3 = (f32[8,576]{1,0:T(8,128)S(1)}, f32[8,576]{1,0:T(8,128)}, u32[]{:S(2)}) copy-start(f32[8,576]{1,0:T(8,128)} %param.10) | copy-start | bytes 55300
  84.6 38.8 %copy-start.4 = (f32[8,576]{1,0:T(8,128)S(1)}, f32[8,576]{1,0:T(8,128)}, u32[]{:S(2)}) copy-start(f32[8,576]{1,0:T(8,128)} %param.11) | copy-start | bytes 55300
  84.6 6.1 %collective-permute-start.4 = (bf16[4,16,576]{2,1,0:T(8,128)(2,1)S(1)}, bf16[4,16,576]{2,1,0:T(8,128)(2,1)S(1)}, u32[]{:S(2)}, u32[]{:S(2)}) collective-permute-start(bf16[4,16,576]{2,1,0:T(8,128)(2,1)S(1)} %get-tuple-element.29), channel_id=1, source_target_pairs={{0,32},{8,488},{16,48},{24,504},{32,64},{40,8},{48,80},{56,24},{64... | collective-permute-start | bytes 221192 | tf_op jit(solution)/shard_map/ppermute | solution.py:272
  90.8 9.1 %collective-permute-start.5 = (bf16[2,16,576]{2,1,0:T(8,128)(2,1)S(1)}, bf16[2,16,576]{2,1,0:T(8,128)(2,1)S(1)}, u32[]{:S(2)}, u32[]{:S(2)}) collective-permute-start(bf16[2,16,576]{2,1,0:T(8,128)(2,1)S(1)} %get-tuple-element.31), channel_id=1, source_target_pairs={{0,64},{8,456},{16,80},{24,472},{32,96},{40,488},{48,112},{56,504}... | collective-permute-start | bytes 110600 | tf_op jit(solution)/shard_map/ppermute | solution.py:272
  99.9 14.9 %collective-permute-start.7 = (bf16[1,16,576]{2,1,0:T(8,128)(2,1)S(1)}, bf16[1,16,576]{2,1,0:T(8,128)(2,1)S(1)}, u32[]{:S(2)}, u32[]{:S(2)}) collective-permute-start(bf16[1,16,576]{2,1,0:T(8,128)(2,1)S(1)} %convert_element_type.2), channel_id=1, source_target_pairs={{8,504},{24,8},{40,24},{56,40},{72,56},{88,72},{104,88},{120,104},... | collective-permute-start | bytes 55304 | tf_op jit(solution)/shard_map/ppermute | solution.py:273
  104.9 14.1 %collective-permute-start.6 = (bf16[1,16,576]{2,1,0:T(8,128)(2,1)S(1)}, bf16[1,16,576]{2,1,0:T(8,128)(2,1)S(1)}, u32[]{:S(2)}, u32[]{:S(2)}) collective-permute-start(bf16[1,16,576]{2,1,0:T(8,128)(2,1)S(1)} %get-tuple-element.33), channel_id=1, source_target_pairs={{0,128},{8,376},{16,144},{24,392},{32,160},{40,408},{48,176},{56,4... | collective-permute-start | bytes 55304 | tf_op jit(solution)/shard_map/ppermute | solution.py:274
  119.1 4.3 %collective-permute-start.8 = (f32[8,576]{1,0:T(8,128)S(1)}, f32[8,576]{1,0:T(8,128)S(1)}, u32[]{:S(2)}, u32[]{:S(2)}) collective-permute-start(f32[8,576]{1,0:T(8,128)S(1)} %get-tuple-element.35), channel_id=1, source_target_pairs={{0,8},{8,0},{1,9},{9,1},{2,10},{10,2},{3,11},{11,3},{4,12},{12,4},... | collective-permute-start | bytes 55304 | tf_op jit(solution)/shard_map/ppermute | solution.py:283

commit v9 on v8

--- a/solution.py
+++ b/solution.py
@@ -101,12 +101,13 @@
         normed = tok[:, at].astype(f32) * inv_rms[j : j + 1]
         hid[:, at] = (normed * gain).astype(bf16)
     hid_copy.start()
-    copies[1].wait()
     gain_sum = jnp.zeros((1, FEAT), f32)
     for m in range(4):
         rows = slice(256 * m, 256 * (m + 1))
         cot = jnp.concatenate([got[g, rows] for g in range(8)], axis=1)
         grad = lax.dot_general(cot, hid[...], (((1,), (1,)), ((), ())), preferred_element_type=f32)
+        if m == 0:
+            copies[1].wait()
         w = weight[rows].astype(f32)
         gain_sum += jnp.sum(w * grad, axis=0, keepdims=True)
         half = slice(m % 2 * 16, m % 2 * 16 + 16)

time: 125 us -> 125 us (level)
  no operation moved by 1% of the time
where the time goes in v9:
time: 125 us; the launch traced here: 124 us
  starting transfers between devices  74.8 us (60%)
  waiting for transfers between devices  34.9 us (28%)
  Pallas kernels  12.2 us (10%)
  other arithmetic  1.73 us (1%)
    ppermute x3, starting transfers between devices, per_device(): keep, send = fold(keep, lax.ppermute(send, ZC, ahead(step, step)), flops)  27.9 us
    all_to_all x1, waiting for transfers between devices, per_device(): got = lax.all_to_all(packed, FSDP, 0, 0)  20.1 us
    ppermute x1, starting transfers between devices, per_device(): sibling_a = lax.ppermute(core_a, 'core', SWAP)  10.8 us
    ppermute x1, starting transfers between devices, per_device(): arrived = lax.ppermute(send, ZC, ahead(8, 9))  8.72 us
    all_to_all x1, starting transfers between devices, per_device(): got = lax.all_to_all(packed, FSDP, 0, 0)  7.62 us
    ppermute x3, waiting for transfers between devices, per_device(): keep, send = fold(keep, lax.ppermute(send, ZC, ahead(step, step)), flops)  6.43 us
    ppermute x1, starting transfers between devices, per_device(): near_by = lax.ppermute(keep.astype(bf16), ZC, ahead(None, 1))  5 us
    ppermute x1, starting transfers between devices, per_device(): arrived = lax.ppermute(pair, 'yl', SWAP)  4.98 us
  transfers between devices with their start and end apart: 11, of which 7 were waited for; matrix products, arithmetic and copies ran while one was open for 1% of the time, Pallas kernels for 4%

profile of v9, /device:TPU:1, one launch (start us, length us, event | category | flops | bytes accessed | tf_op | source)
XLA Modules:
  0.0 124.4 jit_solution(4099532970217533098)
XLA Ops:
  0.6 2.6 %pack.1 = bf16[8,1056,128]{2,1,0:T(8,128)(2,1)} custom-call(bf16[128,1024]{1,0:T(8,128)(2,1)} %cot_hbm.1, bf16[576,1024]{1,0:T(8,128)(2,1)} %bitcast.6), custom_call_target="tpu_custom_call" | custom-call | tf_op jit(solution)/shard_map/pack/pallas_call | solution.py:192
  3.2 0.0 copy-start
  3.2 7.6 %all-to-all-start = ((bf16[8,1056,128]{2,1,0:T(8,128)(2,1)}), bf16[8,1056,128]{2,1,0:T(8,128)(2,1)S(1)}, u32[]{:S(2)}, u32[]{:S(2)}) async-start(bf16[8,1056,128]{2,1,0:T(8,128)(2,1)} %pack.1), calls=%async_computation | async-start | bytes 4325376 | tf_op jit(solution)/shard_map/all_to_all | solution.py:209
  10.9 0.0 copy-start.2
  10.9 0.0 copy-done
  10.9 1.5 %turn.1.w_ref = bf16[1024,576]{1,0:T(8,128)(2,1)} custom-call(bf16[576,1024]{1,0:T(8,128)(2,1)S(1)} %bitcast.4), custom_call_target="tpu_custom_call" | custom-call | flops 1000 | bytes 1000 | tf_op jit(solution)/shard_map/turn/pallas_call | solution.py:210
  12.4 20.1 %all-to-all-done.got = bf16[8,1056,128]{2,1,0:T(8,128)(2,1)S(1)} async-done(((bf16[8,1056,128]{2,1,0:T(8,128)(2,1)}), bf16[8,1056,128]{2,1,0:T(8,128)(2,1)S(1)}, u32[]{:S(2)}, u32[]{:S(2)}) %all-to-all-start) | async-done | bytes 2162720 | tf_op jit(solution)/shard_map/all_to_all | solution.py:209
  32.5 0.0 copy-done.2
  32.5 4.7 %grad.1 = (bf16[16,16,576]{2,1,0:T(8,128)(2,1)S(1)}, bf16[16,16,576]{2,1,0:T(8,128)(2,1)S(1)}, f32[16,16,576]{2,1,0:T(8,128)S(1)}, f32[16,16,576]{2,1,0:T(8,128)...) custom-call(bf16[8,1056,128]{2,1,0:T(8,128)(2,1)S(1)} %all-to-all-done.got, bf16[576,1024]{1,0:T(8,128)(2,1)} %bitcast.7, ...), custom_call_target="tpu_custom_call" | custom-call | tf_op jit(solution)/shard_map/grad/pallas_call | solution.py:221
  37.2 0.0 copy-start.1
  37.2 10.8 %collective-permute-start = (bf16[16,16,576]{2,1,0:T(8,128)(2,1)S(1)}, bf16[16,16,576]{2,1,0:T(8,128)(2,1)S(1)}, u32[]{:S(2)}, u32[]{:S(2)}) collective-permute-start(bf16[16,16,576]{2,1,0:T(8,128)(2,1)S(1)} %get-tuple-element.22), channel_id=1, source_target_pairs={{0,8},{8,0},{1,9},{9,1},{2,10},{10,2},{3,11},{11,3},{4,12},{12,4},... | collective-permute-start | bytes 884744 | tf_op jit(solution)/shard_map/ppermute | solution.py:240
  48.0 1.2 collective-permute-done.sibling
  49.3 0.1 pair.1.after_ref
  49.3 5.0 %collective-permute-start.2 = (bf16[16,16,576]{2,1,0:T(8,128)(2,1)S(1)}, bf16[16,16,576]{2,1,0:T(8,128)(2,1)S(1)}, u32[]{:S(2)}, u32[]{:S(2)}) collective-permute-start(bf16[16,16,576]{2,1,0:T(8,128)(2,1)S(1)} %pair.1.after_ref), channel_id=1, source_target_pairs={{0,512},{512,0},{1,513},{513,1},{2,514},{514,2},{3,515},{515,3},{4... | collective-permute-start | bytes 884744 | tf_op jit(solution)/shard_map/ppermute | solution.py:242
  54.3 0.0 copy-done.1
  54.3 3.2 %keys.1.after.array = bf16[8,128,1024]{2,1,0:T(8,128)(2,1)} custom-call(bf16[576,1024]{1,0:T(8,128)(2,1)S(1)} %copy-done.1, bf16[576,1024]{1,0:T(8,128)(2,1)S(1)} %bitcast.5, bf16[16,16,576]{2,1,0:T(8,128)(2,1)S(1)} %pair.1.after_ref), custom_call_target="tpu_custom_call" | custom-call | tf_op jit(solution)/shard_map/keys/pallas_call | solution.py:243
  57.5 2.5 %collective-permute-start.1 = (bf16[16,16,576]{2,1,0:T(8,128)(2,1)S(1)}, bf16[16,16,576]{2,1,0:T(8,128)(2,1)S(1)}, u32[]{:S(2)}, u32[]{:S(2)}) collective-permute-start(bf16[16,16,576]{2,1,0:T(8,128)(2,1)S(1)} %hold.1), channel_id=1, source_target_pairs={{0,8},{8,0},{1,9},{9,1},{2,10},{10,2},{3,11},{11,3},{4,12},{12,4},... | collective-permute-start | bytes 884744 | tf_op jit(solution)/shard_map/ppermute | solution.py:261
  60.0 2.0 %collective-permute-done.2.arrived = bf16[16,16,576]{2,1,0:T(8,128)(2,1)S(1)} collective-permute-done((bf16[16,16,576]{2,1,0:T(8,128)(2,1)S(1)}, bf16[16,16,576]{2,1,0:T(8,128)(2,1)S(1)}, u32[]{:S(2)}, u32[]{:S(2)}) %collective-permute-start.2) | collective-permute-done | bytes 294944 | tf_op jit(solution)/shard_map/ppermute | solution.py:242
  62.1 0.0 collective-permute-done.1.sibling
  62.1 0.1 share.1
  62.2 19.1 %collective-permute-start.3 = (bf16[8,16,576]{2,1,0:T(8,128)(2,1)S(1)}, bf16[8,16,576]{2,1,0:T(8,128)(2,1)S(1)}, u32[]{:S(2)}, u32[]{:S(2)}) collective-permute-start(bf16[8,16,576]{2,1,0:T(8,128)(2,1)S(1)} %get-tuple-element.25.after), channel_id=1, source_target_pairs={{0,16},{8,504},{16,32},{24,8},{32,48},{40,24},{48,64},{56,40},{64,... | collective-permute-start | bytes 442376 | tf_op jit(solution)/shard_map/ppermute | solution.py:273
  81.3 3.6 %all-to-all-start.1 = ((bf16[8,128,1024]{2,1,0:T(8,128)(2,1)}), bf16[8,128,1024]{2,1,0:T(8,128)(2,1)S(1)}, u32[]{:S(2)}, u32[]{:S(2)}) async-start(bf16[8,128,1024]{2,1,0:T(8,128)(2,1)} %pass_on.1), calls=%async_computation.1 | async-start | bytes 4194304 | tf_op jit(solution)/shard_map/all_to_all | solution.py:270
  84.9 0.0 collective-permute-done.3.arrived
  85.0 0.0 copy-start.3
  85.0 0.0 copy-start.4
  85.0 3.1 %collective-permute-start.4 = (bf16[4,16,576]{2,1,0:T(8,128)(2,1)S(1)}, bf16[4,16,576]{2,1,0:T(8,128)(2,1)S(1)}, u32[]{:S(2)}, u32[]{:S(2)}) collective-permute-start(bf16[4,16,576]{2,1,0:T(8,128)(2,1)S(1)} %get-tuple-element.29), channel_id=1, source_target_pairs={{0,32},{8,488},{16,48},{24,504},{32,64},{40,8},{48,80},{56,24},{64... | collective-permute-start | bytes 221192 | tf_op jit(solution)/shard_map/ppermute | solution.py:273
  88.2 3.0 %collective-permute-done.4.arrived = bf16[4,16,576]{2,1,0:T(8,128)(2,1)S(1)} collective-permute-done((bf16[4,16,576]{2,1,0:T(8,128)(2,1)S(1)}, bf16[4,16,576]{2,1,0:T(8,128)(2,1)S(1)}, u32[]{:S(2)}, u32[]{:S(2)}) %collective-permute-start.4) | collective-permute-done | bytes 73760 | tf_op jit(solution)/shard_map/ppermute | solution.py:273
  91.2 5.6 %collective-permute-start.5 = (bf16[2,16,576]{2,1,0:T(8,128)(2,1)S(1)}, bf16[2,16,576]{2,1,0:T(8,128)(2,1)S(1)}, u32[]{:S(2)}, u32[]{:S(2)}) collective-permute-start(bf16[2,16,576]{2,1,0:T(8,128)(2,1)S(1)} %get-tuple-element.31), channel_id=1, source_target_pairs={{0,64},{8,456},{16,80},{24,472},{32,96},{40,488},{48,112},{56,504}... | collective-permute-start | bytes 110600 | tf_op jit(solution)/shard_map/ppermute | solution.py:273
  96.8 3.5 %collective-permute-done.5.arrived = bf16[2,16,576]{2,1,0:T(8,128)(2,1)S(1)} collective-permute-done((bf16[2,16,576]{2,1,0:T(8,128)(2,1)S(1)}, bf16[2,16,576]{2,1,0:T(8,128)(2,1)S(1)}, u32[]{:S(2)}, u32[]{:S(2)}) %collective-permute-start.5) | collective-permute-done | bytes 36896 | tf_op jit(solution)/shard_map/ppermute | solution.py:273
  100.3 5.0 %collective-permute-start.7 = (bf16[1,16,576]{2,1,0:T(8,128)(2,1)S(1)}, bf16[1,16,576]{2,1,0:T(8,128)(2,1)S(1)}, u32[]{:S(2)}, u32[]{:S(2)}) collective-permute-start(bf16[1,16,576]{2,1,0:T(8,128)(2,1)S(1)} %convert_element_type.2), channel_id=1, source_target_pairs={{8,504},{24,8},{40,24},{56,40},{72,56},{88,72},{104,88},{120,104},... | collective-permute-start | bytes 55304 | tf_op jit(solution)/shard_map/ppermute | solution.py:274
  105.3 8.7 %collective-permute-start.6 = (bf16[1,16,576]{2,1,0:T(8,128)(2,1)S(1)}, bf16[1,16,576]{2,1,0:T(8,128)(2,1)S(1)}, u32[]{:S(2)}, u32[]{:S(2)}) collective-permute-start(bf16[1,16,576]{2,1,0:T(8,128)(2,1)S(1)} %get-tuple-element.33), channel_id=1, source_target_pairs={{0,128},{8,376},{16,144},{24,392},{32,160},{40,408},{48,176},{56,4... | collective-permute-start | bytes 55304 | tf_op jit(solution)/shard_map/ppermute | solution.py:275
  114.0 0.0 all-to-all-done.1
  114.0 1.1 reduce_sum.12.after
  115.1 0.0 collective-permute-done.7.near_by
  115.1 4.3 %collective-permute-done.6.arrived = bf16[1,16,576]{2,1,0:T(8,128)(2,1)S(1)} collective-permute-done((bf16[1,16,576]{2,1,0:T(8,128)(2,1)S(1)}, bf16[1,16,576]{2,1,0:T(8,128)(2,1)S(1)}, u32[]{:S(2)}, u32[]{:S(2)}) %collective-permute-start.6) | collective-permute-done | bytes 18464 | tf_op jit(solution)/shard_map/ppermute | solution.py:275
  119.5 3.5 %collective-permute-start.8 = (f32[8,576]{1,0:T(8,128)S(1)}, f32[8,576]{1,0:T(8,128)S(1)}, u32[]{:S(2)}, u32[]{:S(2)}) collective-permute-start(f32[8,576]{1,0:T(8,128)S(1)} %get-tuple-element.35), channel_id=1, source_target_pairs={{0,8},{8,0},{1,9},{9,1},{2,10},{10,2},{3,11},{11,3},{4,12},{12,4},... | collective-permute-start | bytes 55304 | tf_op jit(solution)/shard_map/ppermute | solution.py:284
  123.0 0.8 collective-permute-done.8
  123.8 0.0 copy-done.3
  123.8 0.0 copy-done.4
  123.8 0.6 multiply_subtract_fusion
  (7 shorter events, 0.1 us)
Async XLA Ops:
  3.2 7.6 %copy-start = (bf16[1,1024,576]{1,2,0:T(8,128)(2,1)S(1)}, bf16[1,1024,576]{1,2,0:T(8,128)(2,1)}, u32[]{:S(2)}) copy-start(bf16[1,1024,576]{1,2,0:T(8,128)(2,1)} %param.8) | copy-start | bytes 3538948
  3.2 29.2 %all-to-all-start = ((bf16[8,1056,128]{2,1,0:T(8,128)(2,1)}), bf16[8,1056,128]{2,1,0:T(8,128)(2,1)S(1)}, u32[]{:S(2)}, u32[]{:S(2)}) async-start(bf16[8,1056,128]{2,1,0:T(8,128)(2,1)} %pack.1), calls=%async_computation | async-start | bytes 4325376 | tf_op jit(solution)/shard_map/all_to_all | solution.py:209
  10.9 21.6 %copy-start.2 = (bf16[1,576]{1,0:T(2,128)(2,1)S(1)}, bf16[1,576]{1,0:T(2,128)(2,1)}, u32[]{:S(2)}) copy-start(bf16[1,576]{1,0:T(2,128)(2,1)} %gain_ref.1) | copy-start | bytes 3460
  37.2 17.1 %copy-start.1 = (bf16[576,1024]{1,0:T(8,128)(2,1)S(1)}, bf16[576,1024]{1,0:T(8,128)(2,1)}, u32[]{:S(2)}) copy-start(bf16[576,1024]{1,0:T(8,128)(2,1)} %get-tuple-element.20.hid_ref) | copy-start | bytes 3538948
  37.2 12.1 %collective-permute-start = (bf16[16,16,576]{2,1,0:T(8,128)(2,1)S(1)}, bf16[16,16,576]{2,1,0:T(8,128)(2,1)S(1)}, u32[]{:S(2)}, u32[]{:S(2)}) collective-permute-start(bf16[16,16,576]{2,1,0:T(8,128)(2,1)S(1)} %get-tuple-element.22), channel_id=1, source_target_pairs={{0,8},{8,0},{1,9},{9,1},{2,10},{10,2},{3,11},{11,3},{4,12},{12,4},... | collective-permute-start | bytes 884744 | tf_op jit(solution)/shard_map/ppermute | solution.py:240
  49.3 12.7 %collective-permute-start.2 = (bf16[16,16,576]{2,1,0:T(8,128)(2,1)S(1)}, bf16[16,16,576]{2,1,0:T(8,128)(2,1)S(1)}, u32[]{:S(2)}, u32[]{:S(2)}) collective-permute-start(bf16[16,16,576]{2,1,0:T(8,128)(2,1)S(1)} %pair.1.after_ref), channel_id=1, source_target_pairs={{0,512},{512,0},{1,513},{513,1},{2,514},{514,2},{3,515},{515,3},{4... | collective-permute-start | bytes 884744 | tf_op jit(solution)/shard_map/ppermute | solution.py:242
  57.5 4.6 %collective-permute-start.1 = (bf16[16,16,576]{2,1,0:T(8,128)(2,1)S(1)}, bf16[16,16,576]{2,1,0:T(8,128)(2,1)S(1)}, u32[]{:S(2)}, u32[]{:S(2)}) collective-permute-start(bf16[16,16,576]{2,1,0:T(8,128)(2,1)S(1)} %hold.1), channel_id=1, source_target_pairs={{0,8},{8,0},{1,9},{9,1},{2,10},{10,2},{3,11},{11,3},{4,12},{12,4},... | collective-permute-start | bytes 884744 | tf_op jit(solution)/shard_map/ppermute | solution.py:261
  62.2 22.8 %collective-permute-start.3 = (bf16[8,16,576]{2,1,0:T(8,128)(2,1)S(1)}, bf16[8,16,576]{2,1,0:T(8,128)(2,1)S(1)}, u32[]{:S(2)}, u32[]{:S(2)}) collective-permute-start(bf16[8,16,576]{2,1,0:T(8,128)(2,1)S(1)} %get-tuple-element.25.after), channel_id=1, source_target_pairs={{0,16},{8,504},{16,32},{24,8},{32,48},{40,24},{48,64},{56,40},{64,... | collective-permute-start | bytes 442376 | tf_op jit(solution)/shard_map/ppermute | solution.py:273
  81.3 32.7 %all-to-all-start.1 = ((bf16[8,128,1024]{2,1,0:T(8,128)(2,1)}), bf16[8,128,1024]{2,1,0:T(8,128)(2,1)S(1)}, u32[]{:S(2)}, u32[]{:S(2)}) async-start(bf16[8,128,1024]{2,1,0:T(8,128)(2,1)} %pass_on.1), calls=%async_computation.1 | async-start | bytes 4194304 | tf_op jit(solution)/shard_map/all_to_all | solution.py:270
  85.0 38.8 %copy-start.3 = (f32[8,576]{1,0:T(8,128)S(1)}, f32[8,576]{1,0:T(8,128)}, u32[]{:S(2)}) copy-start(f32[8,576]{1,0:T(8,128)} %param.10) | copy-start | bytes 55300
  85.0 38.8 %copy-start.4 = (f32[8,576]{1,0:T(8,128)S(1)}, f32[8,576]{1,0:T(8,128)}, u32[]{:S(2)}) copy-start(f32[8,576]{1,0:T(8,128)} %param.11) | copy-start | bytes 55300
  85.0 6.1 %collective-permute-start.4 = (bf16[4,16,576]{2,1,0:T(8,128)(2,1)S(1)}, bf16[4,16,576]{2,1,0:T(8,128)(2,1)S(1)}, u32[]{:S(2)}, u32[]{:S(2)}) collective-permute-start(bf16[4,16,576]{2,1,0:T(8,128)(2,1)S(1)} %get-tuple-element.29), channel_id=1, source_target_pairs={{0,32},{8,488},{16,48},{24,504},{32,64},{40,8},{48,80},{56,24},{64... | collective-permute-start | bytes 221192 | tf_op jit(solution)/shard_map/ppermute | solution.py:273
  91.2 9.1 %collective-permute-start.5 = (bf16[2,16,576]{2,1,0:T(8,128)(2,1)S(1)}, bf16[2,16,576]{2,1,0:T(8,128)(2,1)S(1)}, u32[]{:S(2)}, u32[]{:S(2)}) collective-permute-start(bf16[2,16,576]{2,1,0:T(8,128)(2,1)S(1)} %get-tuple-element.31), channel_id=1, source_target_pairs={{0,64},{8,456},{16,80},{24,472},{32,96},{40,488},{48,112},{56,504}... | collective-permute-start | bytes 110600 | tf_op jit(solution)/shard_map/ppermute | solution.py:273
  100.3 14.9 %collective-permute-start.7 = (bf16[1,16,576]{2,1,0:T(8,128)(2,1)S(1)}, bf16[1,16,576]{2,1,0:T(8,128)(2,1)S(1)}, u32[]{:S(2)}, u32[]{:S(2)}) collective-permute-start(bf16[1,16,576]{2,1,0:T(8,128)(2,1)S(1)} %convert_element_type.2), channel_id=1, source_target_pairs={{8,504},{24,8},{40,24},{56,40},{72,56},{88,72},{104,88},{120,104},... | collective-permute-start | bytes 55304 | tf_op jit(solution)/shard_map/ppermute | solution.py:274
  105.3 14.1 %collective-permute-start.6 = (bf16[1,16,576]{2,1,0:T(8,128)(2,1)S(1)}, bf16[1,16,576]{2,1,0:T(8,128)(2,1)S(1)}, u32[]{:S(2)}, u32[]{:S(2)}) collective-permute-start(bf16[1,16,576]{2,1,0:T(8,128)(2,1)S(1)} %get-tuple-element.33), channel_id=1, source_target_pairs={{0,128},{8,376},{16,144},{24,392},{32,160},{40,408},{48,176},{56,4... | collective-permute-start | bytes 55304 | tf_op jit(solution)/shard_map/ppermute | solution.py:275
  119.5 4.3 %collective-permute-start.8 = (f32[8,576]{1,0:T(8,128)S(1)}, f32[8,576]{1,0:T(8,128)S(1)}, u32[]{:S(2)}, u32[]{:S(2)}) collective-permute-start(f32[8,576]{1,0:T(8,128)S(1)} %get-tuple-element.35), channel_id=1, source_target_pairs={{0,8},{8,0},{1,9},{9,1},{2,10},{10,2},{3,11},{11,3},{4,12},{12,4},... | collective-permute-start | bytes 55304 | tf_op jit(solution)/shard_map/ppermute | solution.py:284
